TPU v7x, 512 devices: a whole 4x8x8 slice. The times are simulated.
512 devices in a mesh: dp: 8 (over y_lo, x), resp: 32 (over y_hi, z), tensor: 2 (over core).
Axes of the slice: x: 4, y: 8 (y_hi: 4, y_lo: 2; y = y_hi * 2 + y_lo), z: 8, core: 2. Of those that a mesh axis runs over, the one named last changes fastest.
Arguments:
- query_raw: bfloat16 [8, 32, 128, 4096], P('dp', 'resp', None, 'tensor'), may hold values from -6 to 6
- response_key_input: bfloat16 [8, 32, 128, 512], P('dp', 'resp', None, 'tensor'), may hold values from -6 to 6
- response_value_input: bfloat16 [8, 32, 128, 512], P('dp', 'resp', None, 'tensor'), may hold values from -6 to 6
- prompt_key_input: bfloat16 [8, 256, 512], P('dp', 'resp', 'tensor'), may hold values from -6 to 6
- prompt_value_input: bfloat16 [8, 256, 512], P('dp', 'resp', 'tensor'), may hold values from -6 to 6
- query_gain: float32 [128], replicated, may hold values from 0.1 to 1.9
- key_gain: float32 [128], replicated, may hold values from 0.1 to 1.9
- grad_out: bfloat16 [8, 32, 128, 4096], P('dp', 'resp', None, 'tensor'), may hold values from -12 to 12
- rewards: float32 [8, 32], P('dp', 'resp'), may hold values from -12 to 12
- resp_len: int32 [8, 32], P('dp', 'resp'), may hold values from 1 to 128, as said below
- prompt_len: int32 [8], P('dp'), may hold values from 64 to 256, as said below
Outputs:
- grad_query: bfloat16 [8, 32, 128, 4096], P('dp', 'resp', None, 'tensor')
- grad_key: bfloat16 [8, 32, 128, 512], P('dp', 'resp', None, 'tensor')
- grad_value: bfloat16 [8, 32, 128, 512], P('dp', 'resp', None, 'tensor')
- grad_prefix_key: float32 [8, 256, 512], P('dp', 'resp', 'tensor')
- grad_prefix_value: float32 [8, 256, 512], P('dp', 'resp', 'tensor')
- grad_query_gain: float32 [128], replicated
- grad_key_gain: float32 [128], replicated
Inputs may be any that keep to these rules, and one draw needn't show every extreme that they name: `resp_len`: each response has 1 to 128 valid tokens, and in every draw some response has exactly 128. `prompt_len`: each prompt has 64 to 256 valid tokens, and in every draw some prompt has exactly 256.
All inputs are finite; a program needn't handle non-finite values.
Results may differ from a plain program's by a relative error of at most 0.0078.
Values may be sent and summed in bfloat16 or wider, within the bound.
No kernel may reach another device: no remote copies, remote signals or barrier semaphores. Data moves between devices by JAX's collectives and lax.ppermute only.
A program may use at most 64 MiB of HBM per device.

v0:
```python
import jax
import jax.numpy as jnp
from jax import lax
from jax.sharding import PartitionSpec as P

EPSILON = 1e-06
THETA = 1000000.0


def rotate(vectors):
    half_width = vectors.shape[-1] // 2
    return jnp.concatenate([-vectors[..., half_width:], vectors[..., :half_width]], axis=-1)


def rotate_back(vectors):
    half_width = vectors.shape[-1] // 2
    return jnp.concatenate([vectors[..., half_width:], -vectors[..., :half_width]], axis=-1)


def tables(positions, head_dimension):
    half_width = head_dimension // 2
    inv_freq = THETA ** (-(jnp.arange(half_width, dtype=jnp.float32) * 2.0) / head_dimension)
    angles = positions.astype(jnp.float32)[:, None] * inv_freq[None, :]
    angles = jnp.concatenate([angles, angles], axis=1)
    return (jnp.cos(angles)[:, None, :], jnp.sin(angles)[:, None, :])


def norm_rope(raw_rows, gain_vec, positions, head_dimension):
    row_count = raw_rows.shape[0]
    raw_f32 = raw_rows.astype(jnp.float32).reshape(row_count, -1, head_dimension)
    inverse = lax.rsqrt(jnp.mean(raw_f32 * raw_f32, axis=-1, keepdims=True) + EPSILON)
    unit_vec = raw_f32 * inverse
    normed = unit_vec * gain_vec
    cos_table, sin_table = tables(positions, head_dimension)
    rotated = normed * cos_table + rotate(normed) * sin_table
    return (rotated.astype(jnp.bfloat16), unit_vec, inverse, cos_table, sin_table)


def norm_rope_back(grad_in, unit_vec, inverse, gain_vec, cos_table, sin_table):
    normed_grad = grad_in * cos_table + rotate_back(grad_in * sin_table)
    gain_term = jnp.sum(normed_grad * unit_vec, axis=(0, 1))
    unit_grad = normed_grad * gain_vec
    raw_grad = inverse * (
        unit_grad - unit_vec * jnp.mean(unit_grad * unit_vec, axis=-1, keepdims=True)
    )
    return (raw_grad, gain_term)


def kv_group(
    query_matrix, joined_keys, value_matrix, output_gradient, starting_position, prefix, length
):
    row_count, head_dimension = query_matrix.shape
    block_rows = min(512, row_count)
    block_count = row_count // block_rows
    score_scale = head_dimension ** (-0.5)
    column_ids = jnp.arange(joined_keys.shape[0], dtype=jnp.int32)
    query_blocks = query_matrix.reshape(block_count, block_rows, head_dimension)
    grad_blocks = output_gradient.reshape(block_count, block_rows, head_dimension)
    first_rows = jnp.arange(block_count, dtype=jnp.int32) * block_rows
    contract_rows = (((0,), (0,)), ((), ()))
    contract_last = (((1,), (1,)), ((), ()))

    def one_block(accum, inputs):
        query_rows, grad_rows, first_row = inputs
        token_numbers = (first_row + jnp.arange(block_rows, dtype=jnp.int32)) % length
        allowed = jnp.where(
            column_ids[None, :] < prefix,
            column_ids[None, :] < starting_position,
            column_ids[None, :] - prefix <= token_numbers[:, None],
        )
        score = (
            lax.dot_general(
                query_rows, joined_keys, contract_last, preferred_element_type=jnp.float32
            )
            * score_scale
        )
        expo_score = jnp.where(allowed, jnp.exp(score), 0.0)
        prob_f32 = expo_score / jnp.sum(expo_score, axis=1, keepdims=True)
        prob_low = prob_f32.astype(jnp.bfloat16)
        dprob_f32 = lax.dot_general(
            grad_rows, value_matrix, contract_last, preferred_element_type=jnp.float32
        )
        delta_row = jnp.sum(prob_f32 * dprob_f32, axis=1, keepdims=True)
        dscore = (prob_f32 * (dprob_f32 - delta_row) * score_scale).astype(jnp.bfloat16)
        query_gradient_out = jnp.dot(dscore, joined_keys, preferred_element_type=jnp.float32)
        saved = ()
        key_gradient_full = accum[0] + lax.dot_general(
            dscore, query_rows, contract_rows, preferred_element_type=jnp.float32
        )
        value_gradient_out = accum[1] + lax.dot_general(
            prob_low, grad_rows, contract_rows, preferred_element_type=jnp.float32
        )
        return ((key_gradient_full, value_gradient_out), (query_gradient_out, saved))

    acc_rows = joined_keys.shape[0]
    zero_acc = jnp.zeros((acc_rows, head_dimension), jnp.float32)
    (key_gradient_full, value_gradient_out), (query_gradient_out, saved) = lax.scan(
        one_block, (zero_acc, zero_acc), (query_blocks, grad_blocks, first_rows)
    )
    query_gradient_out = query_gradient_out.reshape(row_count, head_dimension)
    return (
        query_gradient_out,
        key_gradient_full[prefix:],
        value_gradient_out[prefix:],
        (key_gradient_full[:prefix], value_gradient_out[:prefix]),
    )


def local(
    query_raw,
    response_key_input,
    response_value_input,
    prompt_key_input,
    prompt_value_input,
    query_gain,
    key_gain,
    grad_out,
    rewards,
    resp_len,
    prompt_len,
):
    length = query_raw.shape[2]
    head_dimension = query_gain.shape[0]
    query_heads = query_raw.shape[3] // head_dimension
    kv_heads = response_key_input.shape[3] // head_dimension
    kv_cols = kv_heads * head_dimension
    responses_per_group = query_heads // kv_heads
    responses = lax.axis_size("resp")
    reward_sum = lax.psum(rewards, "resp")
    advantage = rewards[0, 0] - reward_sum[0, 0] / responses
    starting_position = prompt_len[0]
    token_numbers = jnp.arange(length, dtype=jnp.int32)
    positions = starting_position + token_numbers
    gathered_key, gathered_value = (
        lax.all_gather(prompt_key_input, "resp", axis=1, tiled=True),
        lax.all_gather(prompt_value_input, "resp", axis=1, tiled=True),
    )
    prefix = gathered_key.shape[1]
    pre_rot = norm_rope(
        gathered_key[0], key_gain, jnp.arange(prefix, dtype=jnp.int32), head_dimension
    )[0]
    rotated_query_rows, query_unit, query_inv, query_cos, query_sin = norm_rope(
        query_raw[0, 0], query_gain, positions, head_dimension
    )
    key_rot, key_unit, key_inv, key_cos, key_sin = norm_rope(
        response_key_input[0, 0], key_gain, positions, head_dimension
    )
    valid_rows = (token_numbers < resp_len[0, 0])[:, None]
    output_gradient = jnp.where(
        valid_rows, grad_out[0, 0].astype(jnp.float32) * advantage, 0.0
    ).astype(jnp.bfloat16)
    joined_keys = jnp.concatenate([pre_rot, key_rot], axis=0).transpose(1, 0, 2)
    value_matrix = jnp.concatenate(
        [
            gathered_value[0].reshape(prefix, kv_heads, head_dimension),
            response_value_input[0, 0].reshape(length, kv_heads, head_dimension),
        ],
        axis=0,
    ).transpose(1, 0, 2)
    query_matrix = (
        rotated_query_rows.reshape(length, kv_heads, responses_per_group, head_dimension)
        .transpose(1, 2, 0, 3)
        .reshape(kv_heads, responses_per_group * length, head_dimension)
    )
    incoming_gradients = (
        output_gradient.reshape(length, kv_heads, responses_per_group, head_dimension)
        .transpose(1, 2, 0, 3)
        .reshape(kv_heads, responses_per_group * length, head_dimension)
    )
    query_gradient_out, dkey_local, dvalue_local, pre_parts = lax.map(
        lambda operands: kv_group(
            operands[0], operands[1], operands[2], operands[3], starting_position, prefix, length
        ),
        (query_matrix, joined_keys, value_matrix, incoming_gradients),
    )
    dquery_rot = (
        query_gradient_out.reshape(kv_heads, responses_per_group, length, head_dimension)
        .transpose(2, 0, 1, 3)
        .reshape(length, query_heads, head_dimension)
    )
    grad_query_rows, query_contribution = norm_rope_back(
        dquery_rot, query_unit, query_inv, query_gain, query_cos, query_sin
    )
    grad_key_rows, key_contribution = norm_rope_back(
        dkey_local.transpose(1, 0, 2), key_unit, key_inv, key_gain, key_cos, key_sin
    )
    grad_value_rows = dvalue_local.transpose(1, 0, 2).reshape(length, kv_cols)
    own_rows = prefix // responses
    dkey_pre, prompt_value_gradient = pre_parts
    dkey_owned, dvalue_owned = (
        lax.psum_scatter(
            dkey_pre.transpose(1, 0, 2).reshape(prefix, kv_cols),
            "resp",
            scatter_dimension=0,
            tiled=True,
        ),
        lax.psum_scatter(
            prompt_value_gradient.transpose(1, 0, 2).reshape(prefix, kv_cols),
            "resp",
            scatter_dimension=0,
            tiled=True,
        ),
    )
    own_positions = lax.axis_index("resp") * own_rows + jnp.arange(own_rows, dtype=jnp.int32)
    owned_rot, owned_unit, owned_inv, owned_cos, owned_sin = norm_rope(
        prompt_key_input[0], key_gain, own_positions, head_dimension
    )
    prompt_key_gradient, prompt_contribution = norm_rope_back(
        dkey_owned.reshape(own_rows, kv_heads, head_dimension),
        owned_unit,
        owned_inv,
        key_gain,
        owned_cos,
        owned_sin,
    )
    query_total, key_total = lax.psum(
        (query_contribution, key_contribution + prompt_contribution), ("dp", "resp", "tensor")
    )
    replicas = lax.axis_size("dp") * responses
    return (
        grad_query_rows.reshape(1, 1, length, query_heads * head_dimension).astype(jnp.bfloat16),
        grad_key_rows.reshape(1, 1, length, kv_cols).astype(jnp.bfloat16),
        grad_value_rows.reshape(1, 1, length, kv_cols).astype(jnp.bfloat16),
        prompt_key_gradient.reshape(1, own_rows, kv_cols),
        dvalue_owned.reshape(1, own_rows, kv_cols),
        query_total / replicas,
        key_total / replicas,
    )


def solution(mesh):
    return jax.shard_map(
        local,
        mesh=mesh,
        in_specs=(
            P("dp", "resp", None, "tensor"),
            P("dp", "resp", None, "tensor"),
            P("dp", "resp", None, "tensor"),
            P("dp", "resp", "tensor"),
            P("dp", "resp", "tensor"),
            P(),
            P(),
            P("dp", "resp", None, "tensor"),
            P("dp", "resp"),
            P("dp", "resp"),
            P("dp"),
        ),
        out_specs=(
            P("dp", "resp", None, "tensor"),
            P("dp", "resp", None, "tensor"),
            P("dp", "resp", None, "tensor"),
            P("dp", "resp", "tensor"),
            P("dp", "resp", "tensor"),
            P(),
            P(),
        ),
        check_vma=False,
    )
```

profile of v0, /device:TPU:1, one launch (start us, length us, event | category | flops | bytes accessed | tf_op | source)
XLA Modules:
  0.0 755.7 jit_solution(6067830529273465979)
XLA Ops:
  7.2 77.1 %psum.21 = f32[1,1]{1,0:T(1,128)} all-reduce(f32[1,1]{1,0:T(1,128)} %param.23), channel_id=1, replica_groups=mesh['dp'=8,'resp'=32,'tensor'=2] {'resp'}, use_global_device_ids=true, to_apply=%region_3.0 | all-reduce | flops 1 | bytes 8 | tf_op jit(solution)/shard_map/psum | solution.py:129
  85.0 1.0 copy.101
  86.8 0.7 slice_negate_fusion.4
  88.8 62.0 %all_gather.6 = bf16[1,256,256]{2,1,0:T(8,128)(2,1)S(1)} all-gather(bf16[1,8,256]{2,1,0:T(8,128)(2,1)S(1)} %copy-done.35), channel_id=1, replica_groups=mesh['dp'=8,'resp'=32,'tensor'=2] {'resp'}, dimensions={1}, use_global_device_ids=true | all-gather | bytes 135168 | tf_op jit(solution)/shard_map/all_gather | solution.py:135
  151.6 0.7 slice_negate_fusion.2
  152.4 1.2 fusion.44
  153.6 64.1 %all_gather.7 = bf16[1,256,256]{2,1,0:T(8,128)(2,1)S(1)} all-gather(bf16[1,8,256]{2,1,0:T(8,128)(2,1)S(1)} %copy-done.50), channel_id=1, replica_groups=mesh['dp'=8,'resp'=32,'tensor'=2] {'resp'}, dimensions={1}, use_global_device_ids=true | all-gather | bytes 135168 | tf_op jit(solution)/shard_map/all_gather | solution.py:136
  217.6 0.8 copy.102
  218.5 0.7 copy.103
  221.5 0.7 copy.97
  222.4 0.7 copy-done.46
  223.1 1.4 fusion.28
  224.5 0.9 copy.98
  227.9 1.0 fusion.27
  229.7 0.8 copy-done.27
  230.5 0.8 maximum_bitcast_fusion
  231.3 33.8 %while.52 = (s32[]{:T(128)}, f32[2,1024,128]{2,1,0:T(8,128)}, f32[2,128,128]{1,2,0:T(8,128)}, bf16[2,128,128]{2,1,0:T(8,128)(2,1)}, f32[2,256,128]{2,1,0:T(8,128...) while((s32[]{:T(128)}, f32[2,1024,128]{2,1,0:T(8,128)}, ...), condition=%wide.region_9.10_spmd, body=%wide.region_4.9_spmd.sunk | while | flops 254810240 | bytes 16113049 | solution.py:170
  231.3 1.0 constant_dynamic-slice_fusion.8
  232.3 1.0 constant_dynamic-slice_fusion.10
  233.3 0.9 constant_dynamic-slice_fusion.9
  234.3 0.9 constant_dynamic-slice_fusion.11
  235.4 9.5 %while.53 = (s32[]{:T(128)}, f32[384,128]{1,0:T(8,128)S(1)}, f32[384,128]{1,0:T(8,128)S(1)}, f32[2,512,128]{2,1,0:T(8,128)S(1)}, s32[]{:T(128)}, /*index=5*/s32[...) while((s32[]{:T(128)}, f32[384,128]{1,0:T(8,128)S(1)}, ...), condition=%wide.region_8.8_spmd.clone.clone, body=%wide.region_5.7_spmd.clone.clone.sunk | while | flops 254810240 | bytes 10672148 | solution.py:97
  236.1 0.7 add_select_fusion.2
  236.7 0.7 iota_compare_fusion.4
  238.9 1.2 convolution_add_fusion.5
  240.8 0.7 add_select_fusion.2
  243.6 1.3 convolution_add_fusion.5
  244.9 0.7 bitcast_dynamic-update-slice_fusion.9
  245.7 0.8 copy-done.24
  246.6 0.8 copy-done.38
  247.4 0.9 bitcast_dynamic-update-slice_fusion.7
  248.3 1.0 constant_dynamic-slice_fusion.8
  249.2 1.0 constant_dynamic-slice_fusion.10
  250.2 0.9 constant_dynamic-slice_fusion.9
  251.3 0.9 constant_dynamic-slice_fusion.11
  252.3 9.5 %while.53 = (s32[]{:T(128)}, f32[384,128]{1,0:T(8,128)S(1)}, f32[384,128]{1,0:T(8,128)S(1)}, f32[2,512,128]{2,1,0:T(8,128)S(1)}, s32[]{:T(128)}, /*index=5*/s32[...) while((s32[]{:T(128)}, f32[384,128]{1,0:T(8,128)S(1)}, ...), condition=%wide.region_8.8_spmd.clone.clone, body=%wide.region_5.7_spmd.clone.clone.sunk | while | flops 254810240 | bytes 10672148 | solution.py:97
  253.0 0.7 add_select_fusion.2
  255.8 1.2 convolution_add_fusion.5
  257.7 0.7 add_select_fusion.2
  260.5 1.3 convolution_add_fusion.5
  261.8 0.7 bitcast_dynamic-update-slice_fusion.9
  262.7 0.8 copy-done.24
  263.5 0.8 copy-done.38
  264.3 0.8 bitcast_dynamic-update-slice_fusion.7
  265.2 1.8 copy_bitcast_fusion.2
  267.2 1.7 copy_bitcast_fusion.1
  269.0 0.7 copy-done.20
  270.4 1.6 copy.146
  272.9 2.5 fusion.66
  275.6 0.7 copy.116
  276.4 1.9 pad_maximum_fusion
  278.3 1.1 concatenate.85
  279.4 2.8 multiply_reduce_fusion.1
  282.9 1.1 copy-done.3
  284.0 1.2 reshape.489
  285.2 1.1 mul.528
  286.7 1.2 mul.487
  287.9 0.7 convert_element_type.177
  288.6 3.4 fusion.23
  292.0 229.9 %reduce-scatter.3.cloned.1.call-done = f32[8,256]{1,0:T(8,128)} async-done(((f32[256,256]{1,0:T(8,128)}), f32[8,256]{1,0:T(8,128)}) %reduce-scatter.3.cloned.1.call-update) | async-done | bytes 8208 | tf_op jit(solution)/shard_map/reduce_scatter | solution.py:191
  521.8 0.7 bitcast_multiply_fusion.4
  523.3 101.4 %all-reduce = (f32[128]{0:T(128)S(1)}, f32[128]{0:T(128)S(1)}) all-reduce(f32[128]{0:T(128)S(1)} %get-tuple-element.458, f32[128]{0:T(128)S(1)} %add.190), channel_id=1, replica_groups=mesh['dp'=8,'resp'=32,'tensor'=2] {'dp','resp','tensor'}, use_global_device_ids=true, to_apply=%region_17.18 | all-reduce | flops 256 | bytes 2048 | tf_op jit(solution)/shard_map/psum | solution.py:216
  625.9 0.7 bitcast_multiply_fusion.1
  626.6 122.3 %reduce-scatter.5.cloned.1.call-done = f32[8,256]{1,0:T(8,128)} async-done(((f32[256,256]{1,0:T(8,128)}), f32[8,256]{1,0:T(8,128)}) %reduce-scatter.5.cloned.1.call-update) | async-done | bytes 8208 | tf_op jit(solution)/shard_map/reduce_scatter | solution.py:197
  (243 shorter events, 22.9 us)
Async XLA Ops:
  7.2 514.7 %reduce-scatter.3.cloned.1.call-start = ((), (), s32[]{:S(2)}) async-start(), calls=%async_computation.2 | async-start | bytes 270336 | tf_op jit(solution)/shard_map/reduce_scatter | solution.py:191
  7.2 145.1 %copy-start.48 = (f32[64]{0:T(128)}, f32[64]{0:T(128)S(1)}, u32[]{:S(2)}) copy-start(f32[64]{0:T(128)S(1)} %multiply_power_fusion) | copy-start | bytes 772
  86.0 141.1 %copy-start.7 = (bf16[1,1,128,256]{2,3,1,0:T(8,128)(2,1)}, bf16[1,1,128,256]{2,3,1,0:T(8,128)(2,1)S(1)}, u32[]{:S(2)}) copy-start(bf16[1,1,128,256]{2,3,1,0:T(8,128)(2,1)S(1)} %copy.101) | copy-start | bytes 196612
  88.1 0.7 copy-start.35
  88.8 132.5 %copy-start.17 = (f32[128,128]{0,1:T(8,128)}, f32[128,128]{0,1:T(8,128)S(1)}, u32[]{:S(2)}) copy-start(f32[128,128]{0,1:T(8,128)S(1)} %get-tuple-element.531) | copy-start | bytes 196612
  88.8 132.6 %copy-start.14 = (f32[128,128]{0,1:T(8,128)}, f32[128,128]{0,1:T(8,128)S(1)}, u32[]{:S(2)}) copy-start(f32[128,128]{0,1:T(8,128)S(1)} %get-tuple-element.532) | copy-start | bytes 196612
  151.6 2.0 copy-start.50
  152.3 66.9 %copy-start.9 = (bf16[1,1,128,2048]{3,2,1,0:T(8,128)(2,1)S(1)}, bf16[1,1,128,2048]{3,2,1,0:T(8,128)(2,1)}, u32[]{:S(2)}) copy-start(bf16[1,1,128,2048]{3,2,1,0:T(8,128)(2,1)} %param.15) | copy-start | bytes 1572868
  217.6 0.8 copy-start.37
  219.9 0.8 copy-start.45
  221.5 0.9 copy-start.12
  222.4 2.1 copy-start.10
  224.5 1.6 copy-start.23
  226.3 0.9 copy-start.15
  226.3 0.9 copy-start.18
  226.3 0.9 copy-start.33
  226.3 0.9 copy-start.34
  227.1 0.7 copy-start.42
  227.9 1.1 copy-start.28
  227.9 1.1 copy-start.29
  227.9 1.0 copy-start.30
  227.9 1.1 copy-start.31
  228.9 0.7 copy-start.44
  229.6 0.9 copy-start.27
  229.6 0.9 copy-start.32
  235.4 2.4 copy-start.1
  235.4 2.4 copy-start.5
  238.9 1.3 copy-start.2
  238.9 1.3 copy-start.6
  240.2 2.4 copy-start.1
  240.2 2.4 copy-start.5
  243.6 1.3 copy-start.2
  243.6 1.3 copy-start.6
  245.6 0.9 copy-start.24
  246.5 0.8 copy-start.38
  246.6 1.7 copy-start.25
  247.4 0.9 copy-start.39
  252.3 2.4 copy-start.1
  252.4 2.4 copy-start.5
  255.8 1.3 copy-start.2
  255.8 1.3 copy-start.6
  257.1 2.4 copy-start.1
  257.1 2.4 copy-start.5
  260.5 1.3 copy-start.2
  260.5 1.3 copy-start.6
  262.5 0.9 copy-start.24
  263.4 0.8 copy-start.38
  263.5 1.7 copy-start.25
  264.3 0.9 copy-start.39
  265.2 3.8 copy-start
  267.0 481.9 %reduce-scatter.5.cloned.1.call-start = ((), (), s32[]{:S(2)}) async-start(), calls=%async_computation.3 | async-start | bytes 270336 | tf_op jit(solution)/shard_map/reduce_scatter | solution.py:197
  268.9 0.8 copy-start.20
  270.3 1.7 copy-start.47
  270.3 2.5 copy-start.16
  270.3 2.5 copy-start.26
  272.9 2.5 copy-start.8
  272.9 2.5 copy-start.19
  278.3 1.1 copy-start.11
  278.3 1.1 copy-start.13
  282.7 1.2 copy-start.3
  285.2 1.1 copy-start.22
  286.7 1.2 copy-start.40
  286.7 1.9 copy-start.4
  522.5 0.7 copy-start.36
  (5 other events, 3.2 us)
Sparse Core Ops, SparseCore 0:
  267.1 254.7 reduce-scatter.2
  527.4 221.4 reduce-scatter.4
where the time goes:
time: 761 us; the launch traced here: 756 us
  waiting for transfers between devices  352 us (46%)
  blocking collectives  305 us (40%)
  local copies, waits for them, and re-layouts  42.4 us (6%)
  other arithmetic  28.4 us (4%)
  between operations  17.3 us (2%)
  matrix products  10 us (1%)
    reduce_scatter x1, waiting for transfers between devices, local(): lax.psum_scatter(dkey_pre.transpose(1, 0, 2).reshape(prefix, kv_cols), 'r...  230 us
    reduce_scatter x1, waiting for transfers between devices, local(): lax.psum_scatter(prompt_value_gradient.transpose(1, 0, 2).reshape(prefix,...  122 us
    psum x1, blocking collectives, local(): lax.psum((query_contribution, key_contribution + prompt_contribution), ('...  101 us
    psum x1, blocking collectives, local(): reward_sum = lax.psum(rewards, 'resp')  77.1 us
    all_gather x1, blocking collectives, local(): lax.all_gather(prompt_value_input, 'resp', axis=1, tiled=True)  64.1 us
    all_gather x1, blocking collectives, local(): lax.all_gather(prompt_key_input, 'resp', axis=1, tiled=True)  62 us
  transfers between devices with their start and end apart: 2, of which 2 were waited for; matrix products, arithmetic and copies ran while one was open for 3% of the time, Pallas kernels for 0%

commit v1 on v0

--- a/solution.py
+++ b/solution.py
@@ -104,6 +104,15 @@
         value_gradient_out[prefix:],
         (key_gradient_full[:prefix], value_gradient_out[:prefix]),
     )
+
+
+def split_terms(value, terms):
+    found = []
+    for _ in range(terms):
+        term = lax.reduce_precision(value, 8, 7)
+        found.append(term.astype(jnp.bfloat16))
+        value = value - term
+    return jnp.stack(found)
 
 
 def local(
@@ -126,19 +135,25 @@
     kv_cols = kv_heads * head_dimension
     responses_per_group = query_heads // kv_heads
     responses = lax.axis_size("resp")
-    reward_sum = lax.psum(rewards, "resp")
-    advantage = rewards[0, 0] - reward_sum[0, 0] / responses
+    own_rows = prompt_key_input.shape[1]
+    kv_width = 2 * kv_cols
+    reward_cols = jnp.broadcast_to(split_terms(rewards[0, 0], 3), (own_rows, 3))
+    reward_cols = jnp.pad(reward_cols, ((0, 0), (0, head_dimension - 3)))
+    outgoing = jnp.concatenate([prompt_key_input[0], prompt_value_input[0], reward_cols], axis=1)
+    arrived = lax.all_to_all(
+        jnp.broadcast_to(outgoing[None], (responses,) + outgoing.shape), "resp", 0, 0
+    )
+    reward_all = jnp.sum(arrived[:, 0, kv_width : kv_width + 3].astype(jnp.float32), axis=1)
+    advantage = rewards[0, 0] - jnp.sum(reward_all) / responses
     starting_position = prompt_len[0]
     token_numbers = jnp.arange(length, dtype=jnp.int32)
     positions = starting_position + token_numbers
-    gathered_key, gathered_value = (
-        lax.all_gather(prompt_key_input, "resp", axis=1, tiled=True),
-        lax.all_gather(prompt_value_input, "resp", axis=1, tiled=True),
-    )
+    joined = arrived.reshape(1, responses * own_rows, kv_width + head_dimension)
+    gathered_key, gathered_value = joined[:, :, :kv_cols], joined[:, :, kv_cols:kv_width]
     prefix = gathered_key.shape[1]
-    pre_rot = norm_rope(
+    pre_rot, pre_unit, pre_inv, pre_cos, pre_sin = norm_rope(
         gathered_key[0], key_gain, jnp.arange(prefix, dtype=jnp.int32), head_dimension
-    )[0]
+    )
     rotated_query_rows, query_unit, query_inv, query_cos, query_sin = norm_rope(
         query_raw[0, 0], query_gain, positions, head_dimension
     )
@@ -185,36 +200,45 @@
         dkey_local.transpose(1, 0, 2), key_unit, key_inv, key_gain, key_cos, key_sin
     )
     grad_value_rows = dvalue_local.transpose(1, 0, 2).reshape(length, kv_cols)
-    own_rows = prefix // responses
     dkey_pre, prompt_value_gradient = pre_parts
-    dkey_owned, dvalue_owned = (
-        lax.psum_scatter(
-            dkey_pre.transpose(1, 0, 2).reshape(prefix, kv_cols),
-            "resp",
-            scatter_dimension=0,
-            tiled=True,
-        ),
-        lax.psum_scatter(
-            prompt_value_gradient.transpose(1, 0, 2).reshape(prefix, kv_cols),
-            "resp",
-            scatter_dimension=0,
-            tiled=True,
-        ),
+    dkey_pre = dkey_pre.transpose(1, 0, 2)
+    prompt_contribution = norm_rope_back(dkey_pre, pre_unit, pre_inv, key_gain, pre_cos, pre_sin)[1]
+    gain_terms = jnp.concatenate(
+        [split_terms(query_contribution, 2), split_terms(key_contribution + prompt_contribution, 2)]
+    )
+    gain_rows = jnp.pad(gain_terms, ((0, own_rows - 4), (0, 0)))
+    blocks = jnp.concatenate(
+        [
+            dkey_pre.reshape(responses, own_rows, kv_cols).astype(jnp.bfloat16),
+            prompt_value_gradient.transpose(1, 0, 2)
+            .reshape(responses, own_rows, kv_cols)
+            .astype(jnp.bfloat16),
+            jnp.broadcast_to(gain_rows[None], (responses,) + gain_rows.shape),
+        ],
+        axis=2,
+    )
+    owned = jnp.sum(lax.all_to_all(blocks, "resp", 0, 0).astype(jnp.float32), axis=0)
+    dkey_owned, dvalue_owned = owned[:, :kv_cols], owned[:, kv_cols:kv_width]
+    gain_sums = owned[:4, kv_width:]
+    gain_sums = jnp.stack([gain_sums[0] + gain_sums[1], gain_sums[2] + gain_sums[3]])
+    others = lax.axis_size("dp") * lax.axis_size("tensor")
+    totals = jnp.sum(
+        lax.all_to_all(
+            jnp.broadcast_to(gain_sums[None], (others,) + gain_sums.shape), ("dp", "tensor"), 0, 0
+        ),
+        axis=0,
     )
     own_positions = lax.axis_index("resp") * own_rows + jnp.arange(own_rows, dtype=jnp.int32)
     owned_rot, owned_unit, owned_inv, owned_cos, owned_sin = norm_rope(
         prompt_key_input[0], key_gain, own_positions, head_dimension
     )
-    prompt_key_gradient, prompt_contribution = norm_rope_back(
+    prompt_key_gradient, _ = norm_rope_back(
         dkey_owned.reshape(own_rows, kv_heads, head_dimension),
         owned_unit,
         owned_inv,
         key_gain,
         owned_cos,
         owned_sin,
-    )
-    query_total, key_total = lax.psum(
-        (query_contribution, key_contribution + prompt_contribution), ("dp", "resp", "tensor")
     )
     replicas = lax.axis_size("dp") * responses
     return (
@@ -223,8 +247,8 @@
         grad_value_rows.reshape(1, 1, length, kv_cols).astype(jnp.bfloat16),
         prompt_key_gradient.reshape(1, own_rows, kv_cols),
         dvalue_owned.reshape(1, own_rows, kv_cols),
-        query_total / replicas,
-        key_total / replicas,
+        totals[0] / replicas,
+        totals[1] / replicas,
     )
 
 

time: 761 us -> 144 us (0.19)
  waiting for transfers between devices: 352 us -> 4.64 us
  blocking collectives: 305 us -> 0 us
  starting transfers between devices: 0.26 us -> 36.5 us
  between operations: 17.3 us -> 8.01 us
    reduce_scatter x2 -> x0, waiting for transfers between devices: 352 us -> none  [the longest x1 230 us: local(): lax.psum_scatter(dkey_pre.transpose(1, 0, 2).reshape(prefix, kv_cols), 'r...]
    psum x2 -> x0, blocking collectives: 178 us -> none  [the longest x1 101 us: local(): lax.psum((query_contribution, key_contribution + prompt_contribution), ('...]
    all_gather x2 -> x0, blocking collectives: 126 us -> none  [the longest x1 64.1 us: local(): lax.all_gather(prompt_value_input, 'resp', axis=1, tiled=True)]
    all_to_all x0 -> x3, starting transfers between devices: none -> 36.5 us  [the longest x1 16.8 us: local(): lax.all_to_all(jnp.broadcast_to(outgoing[None], (responses,) + outgoing.s...]
  transfers between devices with their start and end apart: 2 -> 3, of which waited for: 2 -> 2; matrix products, arithmetic and copies ran while one was open for 3% -> 17% of each run, Pallas kernels for 0% -> 0%
where the time goes in v1:
time: 144 us; the launch traced here: 142 us
  local copies, waits for them, and re-layouts  47.7 us (33%)
  starting transfers between devices  36.5 us (25%)
  other arithmetic  31.9 us (22%)
  matrix products  12.9 us (9%)
  between operations  8.01 us (6%)
  waiting for transfers between devices  4.64 us (3%)
    all_to_all x1, starting transfers between devices, local(): lax.all_to_all(jnp.broadcast_to(outgoing[None], (responses,) + outgoing.s...  16.8 us
    all_to_all x1, starting transfers between devices, local(): lax.all_to_all(blocks, 'resp', 0, 0).astype(jnp.float32)  12 us
    unnamed x107, local copies, waits for them, and re-layouts  10.9 us
    while x72, local copies, waits for them, and re-layouts  9.25 us
    dot_general x4, matrix products, one_block(): lax.dot_general(prob_low, grad_rows, contract_rows, preferred_element_typ...  7.87 us
    all_to_all x1, starting transfers between devices, local(): lax.all_to_all(jnp.broadcast_to(gain_sums[None], (others,) + gain_sums.sh...  7.75 us
    dynamic_update_slice x12, local copies, waits for them, and re-layouts, local(): lax.map(lambda operands: kv_group(operands[0], operands[1], operands[2],...  6.88 us
    convert_element_type x1, other arithmetic, local(): grad_query_rows.reshape(1, 1, length, query_heads * head_dimension)  3.37 us
  transfers between devices with their start and end apart: 3, of which 2 were waited for; matrix products, arithmetic and copies ran while one was open for 17% of the time, Pallas kernels for 0%

profile of v1, /device:TPU:1, one launch (start us, length us, event | category | flops | bytes accessed | tf_op | source)
XLA Modules:
  0.0 142.2 jit_solution(14053645666384049086)
XLA Ops:
  5.4 0.7 select_maximum_fusion
  6.2 0.8 broadcast_in_dim.143
  7.0 16.8 %all-to-all-start = ((bf16[32,8,640]{2,1,0:T(8,128)(2,1)}), bf16[32,8,640]{2,1,0:T(8,128)(2,1)}, u32[]{:S(2)}, u32[]{:S(2)}) async-start(bf16[32,8,640]{2,1,0:T(8,128)(2,1)} %broadcast_in_dim.143), calls=%async_computation | async-start | bytes 655360 | tf_op jit(solution)/shard_map/all_to_all | solution.py:143
  24.0 1.2 fusion.44
  26.9 0.7 copy.156
  33.2 0.7 fusion.64
  34.6 1.1 mul.543
  36.1 1.2 mul.502
  38.0 0.8 copy-done.20
  38.8 0.7 fusion.46
  39.5 1.0 fusion.77
  40.8 0.8 copy.155
  41.6 1.5 %fusion.49 = f32[]{:T(128)} fusion(bf16[32,8,640]{2,1,0:T(8,128)(2,1)} %all-to-all-done), kind=kLoop, calls=%fused_computation.114 | loop fusion | flops 191 | bytes 196 | tf_op jit(solution)/shard_map/reduce_sum | solution.py:147
  43.6 1.2 multiply_bitcast_fusion
  45.8 0.7 copy-done.12
  46.7 0.8 copy-done.36
  47.5 0.8 maximum_bitcast_fusion
  48.3 40.4 %while.52 = (s32[]{:T(128)}, f32[2,1024,128]{2,1,0:T(8,128)}, f32[2,128,128]{1,2,0:T(8,128)}, bf16[2,128,128]{2,1,0:T(8,128)(2,1)}, f32[2,256,128]{2,1,0:T(8,128...) while((s32[]{:T(128)}, f32[2,1024,128]{2,1,0:T(8,128)}, ...), condition=%wide.region_9.10_spmd, body=%wide.region_4.9_spmd.sunk | while | flops 254810240 | bytes 24632956 | solution.py:185
  48.3 0.8 copy-done.5
  49.2 1.0 constant_dynamic-slice_fusion.7
  50.5 13.1 %while.53 = (s32[]{:T(128)}, f32[384,128]{1,0:T(8,128)S(1)}, f32[384,128]{1,0:T(8,128)}, f32[2,512,128]{2,1,0:T(8,128)S(1)}, s32[]{:T(128)}, /*index=5*/s32[2]{0...) while((s32[]{:T(128)}, f32[384,128]{1,0:T(8,128)S(1)}, ...), condition=%wide.region_8.8_spmd.clone.clone, body=%wide.region_5.7_spmd.clone.clone.sunk | while | flops 254810240 | bytes 9885780 | solution.py:97
  51.6 0.7 add_select_fusion.2
  54.4 1.9 %convolution_add_fusion.5 = f32[384,128]{1,0:T(8,128)} fusion(f32[384,128]{1,0:T(8,128)} %get-tuple-element.776, bf16[2,512,128]{2,1,0:T(8,128)(2,1)} %copy-done.3, s32[]{:T(128)} %get-tuple-element.774, pred[]{:T(512)S(6)} %compare.39, f32[512,384]{0,1:T(8,128)S(1)} %get-tuple-element.758, f32[512]{0:T(512)S(1)} %get-tuple-element.759), kind=kOutput, calls=%fused_computation.6.clone.1 | convolution fusion | flops 50823168 | bytes 1313281 | tf_op jit(solution)/shard_map/while/body/eval_jaxpr/while/body/eval_jaxpr/dot_general | solution.py:90
  58.1 0.7 add_select_fusion.2
  60.9 2.0 %convolution_add_fusion.5 = f32[384,128]{1,0:T(8,128)} fusion(f32[384,128]{1,0:T(8,128)} %get-tuple-element.776, bf16[2,512,128]{2,1,0:T(8,128)(2,1)} %copy-done.3, s32[]{:T(128)} %get-tuple-element.774, pred[]{:T(512)S(6)} %compare.39, f32[512,384]{0,1:T(8,128)S(1)} %get-tuple-element.758, f32[512]{0:T(512)S(1)} %get-tuple-element.759), kind=kOutput, calls=%fused_computation.6.clone.1 | convolution fusion | flops 50823168 | bytes 1313281 | tf_op jit(solution)/shard_map/while/body/eval_jaxpr/while/body/eval_jaxpr/dot_general | solution.py:90
  64.3 0.8 copy-done.32
  65.2 1.0 bitcast_dynamic-update-slice_fusion.11
  66.1 0.9 bitcast_dynamic-update-slice_fusion.9
  67.1 0.8 bitcast_dynamic-update-slice_fusion.8
  68.5 0.8 copy-done.5
  69.4 1.0 constant_dynamic-slice_fusion.7
  70.7 13.0 %while.53 = (s32[]{:T(128)}, f32[384,128]{1,0:T(8,128)S(1)}, f32[384,128]{1,0:T(8,128)}, f32[2,512,128]{2,1,0:T(8,128)S(1)}, s32[]{:T(128)}, /*index=5*/s32[2]{0...) while((s32[]{:T(128)}, f32[384,128]{1,0:T(8,128)S(1)}, ...), condition=%wide.region_8.8_spmd.clone.clone, body=%wide.region_5.7_spmd.clone.clone.sunk | while | flops 254810240 | bytes 9885780 | solution.py:97
  71.8 0.7 add_select_fusion.2
  74.6 1.9 %convolution_add_fusion.5 = f32[384,128]{1,0:T(8,128)} fusion(f32[384,128]{1,0:T(8,128)} %get-tuple-element.776, bf16[2,512,128]{2,1,0:T(8,128)(2,1)} %copy-done.3, s32[]{:T(128)} %get-tuple-element.774, pred[]{:T(512)S(6)} %compare.39, f32[512,384]{0,1:T(8,128)S(1)} %get-tuple-element.758, f32[512]{0:T(512)S(1)} %get-tuple-element.759), kind=kOutput, calls=%fused_computation.6.clone.1 | convolution fusion | flops 50823168 | bytes 1313281 | tf_op jit(solution)/shard_map/while/body/eval_jaxpr/while/body/eval_jaxpr/dot_general | solution.py:90
  81.1 2.0 %convolution_add_fusion.5 = f32[384,128]{1,0:T(8,128)} fusion(f32[384,128]{1,0:T(8,128)} %get-tuple-element.776, bf16[2,512,128]{2,1,0:T(8,128)(2,1)} %copy-done.3, s32[]{:T(128)} %get-tuple-element.774, pred[]{:T(512)S(6)} %compare.39, f32[512,384]{0,1:T(8,128)S(1)} %get-tuple-element.758, f32[512]{0:T(512)S(1)} %get-tuple-element.759), kind=kOutput, calls=%fused_computation.6.clone.1 | convolution fusion | flops 50823168 | bytes 1313281 | tf_op jit(solution)/shard_map/while/body/eval_jaxpr/while/body/eval_jaxpr/dot_general | solution.py:90
  83.7 0.7 bitcast_dynamic-update-slice_fusion.10
  84.5 0.8 copy-done.32
  85.3 1.0 bitcast_dynamic-update-slice_fusion.11
  86.3 0.9 bitcast_dynamic-update-slice_fusion.9
  87.2 0.8 bitcast_dynamic-update-slice_fusion.8
  88.6 1.1 copy.169
  89.9 0.7 fusion.78
  91.0 0.7 fusion.79
  92.5 1.4 fusion.76
  94.6 2.1 %multiply_reduce_fusion.1 = (f32[128]{0:T(128)S(1)}, f32[128,2,8]{2,1,0:T(2,128)}) fusion(f32[128,2,8,128]{3,2,1,0:T(8,128)S(1)} %bitcast.230, f32[128,2,8]{2,1,0:T(2,128)S(1)} %copy-done.17, f32[128]{0:T(128)S(1)} %copy-done.59, f32[128,2,8,64]{3,2,1,0:T(8,128)S(1)} %get-tuple-element.552, f32[128,2,8,64]{3,2,1,0:T(8,128)S(1)} %get-tuple-element.553, ...), kind=kLoop, calls=%fused_computation.61 | loop fusion | flops 2357120 | bytes 3228672 | tf_op jit(solution)/shard_map/reduce_sum | solution.py:41
  96.9 0.8 copy-done.43
  97.7 0.8 copy.168
  98.5 1.0 convert_element_type.261
  100.7 0.8 pad_maximum_fusion.1
  101.5 12.0 %all-to-all-start.1 = ((bf16[32,8,640]{2,1,0:T(8,128)(2,1)}), bf16[32,8,640]{2,1,0:T(8,128)(2,1)}, u32[]{:S(2)}, u32[]{:S(2)}) async-start(bf16[32,8,640]{2,1,0:T(8,128)(2,1)} %pad_maximum_fusion.1), calls=%async_computation.1 | async-start | bytes 655360 | tf_op jit(solution)/shard_map/all_to_all | solution.py:220
  113.7 1.6 %pad_maximum_fusion = f32[128,16,128]{2,1,0:T(8,128)S(1)} fusion(f32[128,16,64]{2,1,0:T(8,128)} %get-tuple-element.554, f32[128,16,64]{2,1,0:T(8,128)S(1)} %get-tuple-element.551), kind=kLoop, calls=%fused_computation.56 | loop fusion | flops 262144 | bytes 2097152 | tf_op jit(solution)/shard_map/concatenate | solution.py:17
  115.8 0.7 copy.172
  116.6 1.1 concatenate.98
  118.2 1.1 mul.556
  119.3 1.2 reshape.547
  120.5 0.7 convert_element_type.253
  121.4 3.4 %fusion.23 = bf16[1,1,128,2048]{3,2,1,0:T(8,128)(2,1)} fusion(f32[1,1,128,2048]{3,2,1,0:T(8,128)S(1)} %copy-done.10, f32[1,1,128,2048]{3,2,1,0:T(8,128)} %mul.556, bf16[1,1,128,2048]{3,2,1,0:T(8,128)(2,1)} %param.15, f32[1,1,128,2048]{3,2,1,0:T(8,128)} %concatenate.98, f32[1,1,128,2048]{3,2,1,0:T(8,128)} %reshape.547, f32[1,1,128,2048]{3,2,1,0:T(8,128)S(1)} %copy-done.9, ...), kind=kLoop, calls=%fused_computation.48 | loop fusion | flops 2359296 | bytes 6299648 | tf_op jit(solution)/shard_map/convert_element_type | solution.py:245
  124.8 1.7 %all-to-all-done.1 = bf16[32,8,640]{2,1,0:T(8,128)(2,1)} async-done(((bf16[32,8,640]{2,1,0:T(8,128)(2,1)}), bf16[32,8,640]{2,1,0:T(8,128)(2,1)}, u32[]{:S(2)}, u32[]{:S(2)}) %all-to-all-start.1) | async-done | bytes 327712 | tf_op jit(solution)/shard_map/all_to_all | solution.py:220
  126.5 1.0 convert_reduce_fusion
  128.1 7.8 %all-to-all-start.2 = ((f32[16,2,128]{2,1,0:T(2,128)}), f32[16,2,128]{2,1,0:T(2,128)S(1)}, u32[]{:S(2)}, u32[]{:S(2)}) async-start(f32[16,2,128]{2,1,0:T(2,128)} %broadcast_in_dim.146), calls=%async_computation.2 | async-start | bytes 32768 | tf_op jit(solution)/shard_map/all_to_all | solution.py:226
  136.0 0.7 copy-done.57
  136.8 0.7 copy-done.61
  137.5 0.7 bitcast_multiply_fusion.1
  138.7 2.9 %all-to-all-done.2 = f32[16,2,128]{2,1,0:T(2,128)S(1)} async-done(((f32[16,2,128]{2,1,0:T(2,128)}), f32[16,2,128]{2,1,0:T(2,128)S(1)}, u32[]{:S(2)}, u32[]{:S(2)}) %all-to-all-start.2) | async-done | bytes 16416 | tf_op jit(solution)/shard_map/all_to_all | solution.py:226
  (297 shorter events, 34.9 us)
Async XLA Ops:
  6.9 18.2 %copy-start.44 = (bf16[1,1,128,256]{3,2,1,0:T(8,128)(2,1)S(1)}, bf16[1,1,128,256]{3,2,1,0:T(8,128)(2,1)}, u32[]{:S(2)}) copy-start(bf16[1,1,128,256]{3,2,1,0:T(8,128)(2,1)} %param.16) | copy-start | bytes 196612
  7.0 32.6 %all-to-all-start = ((bf16[32,8,640]{2,1,0:T(8,128)(2,1)}), bf16[32,8,640]{2,1,0:T(8,128)(2,1)}, u32[]{:S(2)}, u32[]{:S(2)}) async-start(bf16[32,8,640]{2,1,0:T(8,128)(2,1)} %broadcast_in_dim.143), calls=%async_computation | async-start | bytes 655360 | tf_op jit(solution)/shard_map/all_to_all | solution.py:143
  23.7 3.9 %copy-start.11 = (bf16[1,1,128,2048]{3,2,1,0:T(8,128)(2,1)S(1)}, bf16[1,1,128,2048]{3,2,1,0:T(8,128)(2,1)}, u32[]{:S(2)}) copy-start(bf16[1,1,128,2048]{3,2,1,0:T(8,128)(2,1)} %param.15) | copy-start | bytes 1572868
  25.3 12.6 %copy-start.51 = (f32[128,2]{0,1:T(2,128)}, f32[128,2]{0,1:T(2,128)S(1)}, u32[]{:S(2)}) copy-start(f32[128,2]{0,1:T(2,128)S(1)} %add_rsqrt_fusion.3) | copy-start | bytes 3076
  26.9 3.4 %copy-start.22 = (f32[128,128]{0,1:T(8,128)}, f32[128,128]{0,1:T(8,128)S(1)}, u32[]{:S(2)}) copy-start(f32[128,128]{0,1:T(8,128)S(1)} %get-tuple-element.569) | copy-start | bytes 196612
  26.9 3.5 %copy-start.19 = (f32[128,128]{0,1:T(8,128)}, f32[128,128]{0,1:T(8,128)S(1)}, u32[]{:S(2)}) copy-start(f32[128,128]{0,1:T(8,128)S(1)} %get-tuple-element.570) | copy-start | bytes 196612
  29.0 1.0 copy-start.27
  30.7 1.1 copy-start.16
  34.6 1.2 copy-start.28
  36.1 1.2 copy-start.53
  37.9 0.9 copy-start.23
  40.7 5.1 %copy-start.1 = (f32[1,256,256]{1,2,0:T(8,128)}, f32[1,256,256]{1,2,0:T(8,128)S(1)}, u32[]{:S(2)}) copy-start(f32[1,256,256]{1,2,0:T(8,128)S(1)} %copy.153) | copy-start | bytes 786436
  45.6 0.9 copy-start.12
  45.6 1.0 copy-start.14
  46.5 0.9 copy-start.36
  46.5 0.9 copy-start.37
  46.5 0.9 copy-start.38
  48.3 1.0 copy-start.7
  50.5 2.8 %copy-start.3 = (bf16[2,512,128]{2,1,0:T(8,128)(2,1)}, bf16[2,512,128]{2,1,0:T(8,128)(2,1)S(1)}, u32[]{:S(2)}) copy-start(bf16[2,512,128]{2,1,0:T(8,128)(2,1)S(1)} %get-tuple-element.794) | copy-start | bytes 786436 | tf_op jit(solution)/shard_map/while/body/eval_jaxpr/while
  54.4 1.9 %copy-start.4 = (bf16[2,512,128]{2,1,0:T(8,128)(2,1)S(1)}, bf16[2,512,128]{2,1,0:T(8,128)(2,1)}, u32[]{:S(2)}) copy-start(bf16[2,512,128]{2,1,0:T(8,128)(2,1)} %copy-done.3) | copy-start | bytes 786436 | tf_op jit(solution)/shard_map/while/body/eval_jaxpr/while
  57.0 2.8 %copy-start.3 = (bf16[2,512,128]{2,1,0:T(8,128)(2,1)}, bf16[2,512,128]{2,1,0:T(8,128)(2,1)S(1)}, u32[]{:S(2)}) copy-start(bf16[2,512,128]{2,1,0:T(8,128)(2,1)S(1)} %get-tuple-element.794) | copy-start | bytes 786436 | tf_op jit(solution)/shard_map/while/body/eval_jaxpr/while
  60.9 2.0 %copy-start.4 = (bf16[2,512,128]{2,1,0:T(8,128)(2,1)S(1)}, bf16[2,512,128]{2,1,0:T(8,128)(2,1)}, u32[]{:S(2)}) copy-start(bf16[2,512,128]{2,1,0:T(8,128)(2,1)} %copy-done.3) | copy-start | bytes 786436 | tf_op jit(solution)/shard_map/while/body/eval_jaxpr/while
  64.2 0.9 copy-start.32
  64.2 1.0 copy-start.41
  65.1 2.8 %copy-start.33 = (f32[2,128,128]{1,2,0:T(8,128)}, f32[2,128,128]{1,2,0:T(8,128)S(1)}, u32[]{:S(2)}) copy-start(f32[2,128,128]{1,2,0:T(8,128)S(1)} %constant_dynamic-update-slice_fusion.2) | copy-start | bytes 393220 | tf_op jit(solution)/shard_map/while
  65.2 1.0 copy-start.46
  66.1 1.8 %copy-start.42 = (bf16[2,256,128]{2,1,0:T(8,128)(2,1)}, bf16[2,256,128]{2,1,0:T(8,128)(2,1)S(1)}, u32[]{:S(2)}) copy-start(bf16[2,256,128]{2,1,0:T(8,128)(2,1)S(1)} %bitcast_dynamic-update-slice_fusion.11) | copy-start | bytes 393220 | tf_op jit(solution)/shard_map/while
  67.0 0.9 copy-start.47
  67.0 1.3 copy-start.6
  67.0 1.4 copy-start.8
  68.5 1.0 copy-start.7
  70.7 2.8 %copy-start.3 = (bf16[2,512,128]{2,1,0:T(8,128)(2,1)}, bf16[2,512,128]{2,1,0:T(8,128)(2,1)S(1)}, u32[]{:S(2)}) copy-start(bf16[2,512,128]{2,1,0:T(8,128)(2,1)S(1)} %get-tuple-element.794) | copy-start | bytes 786436 | tf_op jit(solution)/shard_map/while/body/eval_jaxpr/while
  74.6 1.9 %copy-start.4 = (bf16[2,512,128]{2,1,0:T(8,128)(2,1)S(1)}, bf16[2,512,128]{2,1,0:T(8,128)(2,1)}, u32[]{:S(2)}) copy-start(bf16[2,512,128]{2,1,0:T(8,128)(2,1)} %copy-done.3) | copy-start | bytes 786436 | tf_op jit(solution)/shard_map/while/body/eval_jaxpr/while
  77.2 2.8 %copy-start.3 = (bf16[2,512,128]{2,1,0:T(8,128)(2,1)}, bf16[2,512,128]{2,1,0:T(8,128)(2,1)S(1)}, u32[]{:S(2)}) copy-start(bf16[2,512,128]{2,1,0:T(8,128)(2,1)S(1)} %get-tuple-element.794) | copy-start | bytes 786436 | tf_op jit(solution)/shard_map/while/body/eval_jaxpr/while
  81.1 2.0 %copy-start.4 = (bf16[2,512,128]{2,1,0:T(8,128)(2,1)S(1)}, bf16[2,512,128]{2,1,0:T(8,128)(2,1)}, u32[]{:S(2)}) copy-start(bf16[2,512,128]{2,1,0:T(8,128)(2,1)} %copy-done.3) | copy-start | bytes 786436 | tf_op jit(solution)/shard_map/while/body/eval_jaxpr/while
  84.4 0.9 copy-start.32
  84.4 1.0 copy-start.41
  85.3 2.8 %copy-start.33 = (f32[2,128,128]{1,2,0:T(8,128)}, f32[2,128,128]{1,2,0:T(8,128)S(1)}, u32[]{:S(2)}) copy-start(f32[2,128,128]{1,2,0:T(8,128)S(1)} %constant_dynamic-update-slice_fusion.2) | copy-start | bytes 393220 | tf_op jit(solution)/shard_map/while
  85.3 1.0 copy-start.46
  86.3 1.8 %copy-start.42 = (bf16[2,256,128]{2,1,0:T(8,128)(2,1)}, bf16[2,256,128]{2,1,0:T(8,128)(2,1)S(1)}, u32[]{:S(2)}) copy-start(bf16[2,256,128]{2,1,0:T(8,128)(2,1)S(1)} %bitcast_dynamic-update-slice_fusion.11) | copy-start | bytes 393220 | tf_op jit(solution)/shard_map/while
  87.2 1.3 copy-start.6
  87.2 1.4 copy-start.8
  88.6 1.2 copy-start.18
  88.6 1.2 copy-start.15
  89.8 1.9 %copy-start = (f32[2,1024,128]{2,1,0:T(8,128)S(1)}, f32[2,1024,128]{2,1,0:T(8,128)}, u32[]{:S(2)}) copy-start(f32[2,1024,128]{2,1,0:T(8,128)} %get-tuple-element.319) | copy-start | bytes 3145732
  89.9 1.0 copy-start.21
  89.9 1.1 copy-start.34
  91.0 0.9 copy-start.26
  92.5 1.4 copy-start.17
  96.8 0.9 copy-start.43
  96.8 2.7 %copy-start.31 = (f32[256,2,64]{0,2,1:T(8,128)S(1)}, f32[256,2,64]{0,2,1:T(8,128)}, u32[]{:S(2)}) copy-start(f32[256,2,64]{0,2,1:T(8,128)} %get-tuple-element.560) | copy-start | bytes 393220
  97.7 1.8 %copy-start.2 = (f32[1,256,256]{1,2,0:T(8,128)S(1)}, f32[1,256,256]{1,2,0:T(8,128)}, u32[]{:S(2)}) copy-start(f32[1,256,256]{1,2,0:T(8,128)} %copy-done.1) | copy-start | bytes 786436
  98.5 1.1 copy-start.13
  98.5 1.1 copy-start.30
  99.6 0.9 copy-start.35
  99.6 0.9 copy-start.39
  99.6 0.9 copy-start.40
  101.5 12.0 %copy-start.29 = (f32[128,2,8]{2,1,0:T(2,128)S(1)}, f32[128,2,8]{2,1,0:T(2,128)}, u32[]{:S(2)}) copy-start(f32[128,2,8]{2,1,0:T(2,128)} %get-tuple-element.495) | copy-start | bytes 24580
  101.5 25.0 %all-to-all-start.1 = ((bf16[32,8,640]{2,1,0:T(8,128)(2,1)}), bf16[32,8,640]{2,1,0:T(8,128)(2,1)}, u32[]{:S(2)}, u32[]{:S(2)}) async-start(bf16[32,8,640]{2,1,0:T(8,128)(2,1)} %pad_maximum_fusion.1), calls=%async_computation.1 | async-start | bytes 655360 | tf_op jit(solution)/shard_map/all_to_all | solution.py:220
  118.1 2.3 %copy-start.48 = (bf16[2,128,128]{2,1,0:T(8,128)(2,1)S(1)}, bf16[2,128,128]{2,1,0:T(8,128)(2,1)}, u32[]{:S(2)}) copy-start(bf16[2,128,128]{2,1,0:T(8,128)(2,1)} %get-tuple-element.321) | copy-start | bytes 196612
  119.3 1.9 %copy-start.9 = (f32[1,1,128,2048]{3,2,1,0:T(8,128)S(1)}, f32[1,1,128,2048]{3,2,1,0:T(8,128)}, u32[]{:S(2)}) copy-start(f32[1,1,128,2048]{3,2,1,0:T(8,128)} %mul.543) | copy-start | bytes 3145732
  119.3 1.9 %copy-start.10 = (f32[1,1,128,2048]{3,2,1,0:T(8,128)S(1)}, f32[1,1,128,2048]{3,2,1,0:T(8,128)}, u32[]{:S(2)}) copy-start(f32[1,1,128,2048]{3,2,1,0:T(8,128)} %mul.502) | copy-start | bytes 3145732
  121.4 14.5 %copy-start.56 = (f32[8,128]{1,0:T(8,128)S(1)}, f32[8,128]{1,0:T(8,128)}, u32[]{:S(2)}) copy-start(f32[8,128]{1,0:T(8,128)} %get-tuple-element.577) | copy-start | bytes 12292
  128.1 13.5 %all-to-all-start.2 = ((f32[16,2,128]{2,1,0:T(2,128)}), f32[16,2,128]{2,1,0:T(2,128)S(1)}, u32[]{:S(2)}, u32[]{:S(2)}) async-start(f32[16,2,128]{2,1,0:T(2,128)} %broadcast_in_dim.146), calls=%async_computation.2 | async-start | bytes 32768 | tf_op jit(solution)/shard_map/all_to_all | solution.py:226
  (26 other events, 18.2 us)

commit v2 on v0

v2 whole, which is shorter than its diff:
```python
import functools
import math

import jax
import jax.numpy as jnp
import numpy as np
from jax import lax
from jax.experimental import pallas as pl
from jax.experimental.pallas import tpu as pltpu
from jax.sharding import PartitionSpec as P

EPSILON = 1e-06
THETA = 1000000.0
LOG2_E = math.log2(math.e)
F32, BF16 = jnp.float32, jnp.bfloat16
SMEM = pl.BlockSpec(memory_space=pltpu.SMEM)
VMEM = pl.BlockSpec(memory_space=pltpu.VMEM)
CONTRACT_LAST = (((1,), (1,)), ((), ()))
CONTRACT_FIRST = (((0,), (0,)), ((), ()))
HEADS_AT_ONCE = 2


def rope_tables(positions, width):
    half = width // 2
    inv_freq = (THETA ** (-(np.arange(half) * 2.0) / width)).astype(np.float32)
    angles = (np.arange(positions, dtype=np.float32)[:, None] * inv_freq).astype(np.float64)
    cos, sin = np.cos(angles), np.sin(angles)
    return (
        np.concatenate([cos, cos], axis=1).astype(np.float32),
        np.concatenate([-sin, sin], axis=1).astype(np.float32),
    )


def half_turn(rows):
    return pltpu.roll(rows, rows.shape[1] // 2, 1)


def unit_rows(raw):
    raw = raw.astype(F32)
    inverse = lax.rsqrt(jnp.mean(raw * raw, axis=1, keepdims=True) + EPSILON)
    return raw * inverse, inverse


def rotated(unit, gain, cos, sin):
    normed = unit * gain
    return (normed * cos + half_turn(normed) * sin).astype(BF16)


def norm_rope_back(grad, unit, inverse, gain, cos, sin):
    normed_grad = grad * cos - half_turn(grad) * sin
    term = normed_grad * unit
    mean = jnp.mean(term * gain, axis=1, keepdims=True)
    return inverse * (normed_grad * gain - unit * mean), term


def fold(rows):
    return jnp.sum(rows.reshape(-1, 8, rows.shape[1]), axis=0)


def split_terms(value, terms):
    found = []
    for _ in range(terms):
        found.append(value.astype(BF16).astype(F32))
        value = value - found[-1]
    return found


def send_prompt(reward_ref, key_ref, value_ref, out_ref):
    own, width = key_ref.shape
    lane = lax.broadcasted_iota(jnp.int32, (own, 128), 1)
    reward = jnp.full((own, 128), reward_ref[0, 0], F32)
    first, second, third = split_terms(reward, 3)
    tail = jnp.where(
        lane == 0, first, jnp.where(lane == 1, second, jnp.where(lane == 2, third, 0.0))
    )
    slot = jnp.concatenate([key_ref[...].astype(F32), value_ref[...].astype(F32), tail], axis=1)
    slots = jnp.concatenate([slot, slot], axis=0).astype(BF16)
    for i in range(out_ref.shape[0] // (2 * own)):
        out_ref[2 * own * i : 2 * own * (i + 1), :] = slots


def prepare(prompt_len_ref, query_ref, key_ref, query_gain_ref, key_gain_ref, cos_ref, sin_ref,
            query_out, key_out):
    length, width = query_ref.shape[0], query_gain_ref.shape[1]
    start = prompt_len_ref[0]
    cos, sin = cos_ref[pl.ds(start, length), :], sin_ref[pl.ds(start, length), :]
    for source, gain_ref, out in (
        (key_ref, key_gain_ref, key_out),
        (query_ref, query_gain_ref, query_out),
    ):
        gain = gain_ref[...]

        def one(h, _, source=source, gain=gain, out=out):
            raw = source[:, pl.ds(pl.multiple_of(h * width, width), width)]
            rows = rotated(unit_rows(raw)[0], gain, cos, sin)
            out[pl.ds(pl.multiple_of(h * length, length), length), :] = rows
            return 0

        heads = source.shape[1] // width
        lax.fori_loop(0, heads, one, 0, unroll=2)


def attend(
    reward_ref, resp_len_ref, prompt_len_ref,
    arrived_ref, query_ref, key_ref, raw_query_ref, raw_key_ref, value_ref, grad_ref,
    query_gain_ref, key_gain_ref, cos_ref, sin_ref,
    query_out, key_out, value_out, blocks_out,
    keys, values, key_sum, value_sum, query_terms, key_terms, *, responses,
):
    length, width = grad_ref.shape[0], query_gain_ref.shape[1]
    prefix = arrived_ref.shape[0]
    kv_heads = raw_key_ref.shape[1] // width
    kv_cols = kv_heads * width
    group = grad_ref.shape[1] // kv_cols
    own = prefix // responses
    scale = width**-0.5
    start = prompt_len_ref[0]
    query_gain, key_gain = query_gain_ref[...], key_gain_ref[...]
    cos, sin = cos_ref[pl.ds(start, length), :], sin_ref[pl.ds(start, length), :]
    pre_cos, pre_sin = cos_ref[:prefix, :], sin_ref[:prefix, :]

    reward_sum = jnp.sum(arrived_ref[:, 2 * kv_cols :].astype(F32)) / own
    advantage = reward_ref[0, 0] - reward_sum / responses
    token = lax.broadcasted_iota(jnp.int32, (length, width), 0)
    factor = jnp.where(token < resp_len_ref[0, 0], advantage, 0.0)
    query_terms[...] = jnp.zeros_like(query_terms)
    key_terms[...] = jnp.zeros_like(key_terms)

    def one_kv_head(c, _):
        own_cols = pl.ds(pl.multiple_of(c * width, width), width)
        value_cols = pl.ds(pl.multiple_of(kv_cols + c * width, width), width)
        pre_unit, pre_inverse = unit_rows(arrived_ref[:, own_cols])
        keys[:prefix, :] = rotated(pre_unit, key_gain, pre_cos, pre_sin)
        keys[prefix:, :] = key_ref[pl.ds(pl.multiple_of(c * length, length), length), :]
        values[:prefix, :] = arrived_ref[:, value_cols]
        values[prefix:, :] = value_ref[:, own_cols]
        key_sum[...] = jnp.zeros_like(key_sum)
        value_sum[...] = jnp.zeros_like(value_sum)

        def some_heads(p, _):
            first = c * group + p * HEADS_AT_ONCE
            count = HEADS_AT_ONCE * length
            query_rows = query_ref[pl.ds(pl.multiple_of(first * length, length), count), :]
            heads = [
                pl.ds(pl.multiple_of((first + i) * width, width), width)
                for i in range(HEADS_AT_ONCE)
            ]
            grad_rows = jnp.concatenate(
                [(grad_ref[:, cols].astype(F32) * factor).astype(BF16) for cols in heads], axis=0
            )
            score = lax.dot_general(
                keys[...], query_rows, CONTRACT_LAST, preferred_element_type=F32
            )
            expo = jnp.exp2(score * (scale * LOG2_E))
            row = lax.broadcasted_iota(jnp.int32, (prefix, count), 0)
            resp_row = lax.broadcasted_iota(jnp.int32, (length, count), 0)
            query_token = lax.broadcasted_iota(jnp.int32, (length, count), 1) % length
            expo = jnp.concatenate(
                [
                    jnp.where(row < start, expo[:prefix], 0.0),
                    jnp.where(resp_row <= query_token, expo[prefix:], 0.0),
                ],
                axis=0,
            )
            prob = expo * (1.0 / jnp.sum(expo, axis=0, keepdims=True))
            dprob = lax.dot_general(
                values[...], grad_rows, CONTRACT_LAST, preferred_element_type=F32
            )
            delta = jnp.sum(prob * dprob, axis=0, keepdims=True)
            dscore = (prob * (dprob - delta) * scale).astype(BF16)
            key_sum[...] += jnp.dot(dscore, query_rows, preferred_element_type=F32)
            value_sum[...] += jnp.dot(prob.astype(BF16), grad_rows, preferred_element_type=F32)
            query_grad = lax.dot_general(
                dscore, keys[...], CONTRACT_FIRST, preferred_element_type=F32
            )
            for i, cols in enumerate(heads):
                unit, inverse = unit_rows(raw_query_ref[:, cols])
                raw_grad, term = norm_rope_back(
                    query_grad[i * length : (i + 1) * length], unit, inverse, query_gain, cos, sin
                )
                query_out[:, cols] = raw_grad.astype(BF16)
                query_terms[...] += fold(term)
            return 0

        lax.fori_loop(0, group // HEADS_AT_ONCE, some_heads, 0)
        raw_grad, term = norm_rope_back(
            key_sum[:prefix, :], pre_unit, pre_inverse, key_gain, pre_cos, pre_sin
        )
        blocks_out[:, own_cols] = raw_grad.astype(BF16)
        blocks_out[:, value_cols] = value_sum[:prefix, :].astype(BF16)
        key_terms[...] += fold(term)
        unit, inverse = unit_rows(raw_key_ref[:, own_cols])
        raw_grad, term = norm_rope_back(key_sum[prefix:, :], unit, inverse, key_gain, cos, sin)
        key_out[:, own_cols] = raw_grad.astype(BF16)
        value_out[:, own_cols] = value_sum[prefix:, :].astype(BF16)
        key_terms[...] += fold(term)
        return 0

    lax.fori_loop(0, kv_heads, one_kv_head, 0)
    slot_row = lax.broadcasted_iota(jnp.int32, (own, width), 0)
    gains = jnp.zeros((own, width), F32)
    for i, terms in enumerate((query_terms, key_terms)):
        high, low = split_terms(jnp.sum(terms[...], axis=0, keepdims=True), 2)
        gains = jnp.where(slot_row == 2 * i, high, jnp.where(slot_row == 2 * i + 1, low, gains))
    pair = jnp.concatenate([gains, gains], axis=0).astype(BF16)
    for i in range(responses // 2):
        blocks_out[2 * own * i : 2 * own * (i + 1), 2 * kv_cols :] = pair


def add_blocks(arrived_ref, key_out, value_out, gains_out):
    kv_cols = key_out.shape[1]
    own = key_out.shape[0]
    total = jnp.zeros((2 * own, arrived_ref.shape[1]), F32)
    for i in range(arrived_ref.shape[0] // (2 * own)):
        total += arrived_ref[2 * own * i : 2 * own * (i + 1), :].astype(F32)
    total = total[:own] + total[own:]
    key_out[...] = total[:, :kv_cols]
    value_out[...] = total[:, kv_cols : 2 * kv_cols]
    gains = total[:, 2 * kv_cols :]
    row = lax.broadcasted_iota(jnp.int32, gains.shape, 0)
    query = jnp.sum(jnp.where(row < 2, gains, 0.0), axis=0, keepdims=True)
    key = jnp.sum(jnp.where(row < 2, 0.0, gains), axis=0, keepdims=True)
    row = lax.broadcasted_iota(jnp.int32, gains_out.shape, 0)
    gains_out[...] = jnp.where(row % 2 == 0, query, key)


def local(
    query_raw, response_key_input, response_value_input, prompt_key_input, prompt_value_input,
    query_gain, key_gain, grad_out, rewards, resp_len, prompt_len,
):
    length = query_raw.shape[2]
    width = query_gain.shape[0]
    kv_cols = response_key_input.shape[3]
    kv_heads = kv_cols // width
    query_heads = query_raw.shape[3] // width
    responses = lax.axis_size("resp")
    own = prompt_key_input.shape[1]
    prefix = own * responses
    slot_cols = 2 * kv_cols + width
    cos, sin = (jnp.asarray(t) for t in rope_tables(prefix + length, width))
    gains = (query_gain.reshape(1, width), key_gain.reshape(1, width))
    query, key = query_raw[0, 0], response_key_input[0, 0]
    shape = jax.ShapeDtypeStruct

    slots = pl.pallas_call(
        send_prompt,
        out_shape=shape((prefix, slot_cols), BF16),
        in_specs=[SMEM, VMEM, VMEM],
        out_specs=VMEM,
        name="send_prompt",
    )(rewards, prompt_key_input[0], prompt_value_input[0])
    arrived = lax.all_to_all(slots.reshape(responses, own, slot_cols), "resp", 0, 0)
    rotated_query, rotated_key = pl.pallas_call(
        prepare,
        out_shape=(shape((query_heads * length, width), BF16), shape((kv_heads * length, width), BF16)),
        in_specs=[SMEM] + [VMEM] * 6,
        out_specs=(VMEM, VMEM),
        name="prepare",
        cost_estimate=pl.CostEstimate(flops=20_000_000, bytes_accessed=2_000_000, transcendentals=0),
    )(prompt_len, query, key, *gains, cos, sin)
    grad_query, grad_key, grad_value, blocks = pl.pallas_call(
        functools.partial(attend, responses=responses),
        out_shape=(
            shape(query.shape, BF16),
            shape(key.shape, BF16),
            shape(key.shape, BF16),
            shape((prefix, slot_cols), BF16),
        ),
        in_specs=[SMEM] * 3 + [VMEM] * 11,
        out_specs=(VMEM,) * 4,
        scratch_shapes=[
            pltpu.VMEM((prefix + length, width), BF16),
            pltpu.VMEM((prefix + length, width), BF16),
            pltpu.VMEM((prefix + length, width), F32),
            pltpu.VMEM((prefix + length, width), F32),
            pltpu.VMEM((8, width), F32),
            pltpu.VMEM((8, width), F32),
        ],
        compiler_params=pltpu.CompilerParams(vmem_limit_bytes=32 * 2**20),
        name="attend",
    )(
        rewards, resp_len, prompt_len,
        arrived.reshape(prefix, slot_cols), rotated_query, rotated_key, query, key,
        response_value_input[0, 0], grad_out[0, 0], *gains, cos, sin,
    )
    summed = lax.all_to_all(blocks.reshape(responses, own, slot_cols), "resp", 0, 0)
    others = lax.axis_size("dp") * lax.axis_size("tensor")
    prefix_key, prefix_value, gain_slots = pl.pallas_call(
        add_blocks,
        out_shape=(
            shape((own, kv_cols), F32),
            shape((own, kv_cols), F32),
            shape((others * 2, width), F32),
        ),
        in_specs=[VMEM],
        out_specs=(VMEM,) * 3,
        name="add_blocks",
    )(summed.reshape(prefix, slot_cols))
    gain_slots = lax.all_to_all(
        gain_slots.reshape(others, 2, width), ("dp", "tensor"), 0, 0
    )
    totals = jnp.sum(gain_slots, axis=0) / (lax.axis_size("dp") * responses)
    return (
        grad_query[None, None],
        grad_key[None, None],
        grad_value[None, None],
        prefix_key[None],
        prefix_value[None],
        totals[0],
        totals[1],
    )


def solution(mesh):
    token_spec = P("dp", "resp", None, "tensor")
    prompt_spec = P("dp", "resp", "tensor")
    return jax.shard_map(
        local,
        mesh=mesh,
        in_specs=(token_spec,) * 3 + (prompt_spec,) * 2 + (P(), P(), token_spec)
        + (P("dp", "resp"), P("dp", "resp"), P("dp")),
        out_specs=(token_spec,) * 3 + (prompt_spec,) * 2 + (P(), P()),
        check_vma=False,
    )
```

time: 761 us -> 79.8 us (0.10)
  waiting for transfers between devices: 352 us -> 8.06 us
  blocking collectives: 305 us -> 33.4 us
  local copies, waits for them, and re-layouts: 42.4 us -> 3.06 us
  other arithmetic: 28.4 us -> 0.03 us
  starting transfers between devices: 0.26 us -> 16.6 us
  Pallas kernels: 0 us -> 15.4 us
  between operations: 17.3 us -> 2.72 us
  matrix products: 10 us -> 0 us
    reduce_scatter x2 -> x0, waiting for transfers between devices: 352 us -> none  [the longest x1 230 us: local(): lax.psum_scatter(dkey_pre.transpose(1, 0, 2).reshape(prefix, kv_cols), 'r...]
    psum x2 -> x0, blocking collectives: 178 us -> none  [the longest x1 101 us: local(): lax.psum((query_contribution, key_contribution + prompt_contribution), ('...]
    all_gather x2 -> x0, blocking collectives: 126 us -> none  [the longest x1 64.1 us: local(): lax.all_gather(prompt_value_input, 'resp', axis=1, tiled=True)]
    all_to_all x0 -> x2, blocking collectives: none -> 33.4 us  [the longest x1 20.7 us: local(): lax.all_to_all(blocks.reshape(responses, own, slot_cols), 'resp', 0, 0)]
    all_to_all x0 -> x1, starting transfers between devices: none -> 16.6 us  [local(): lax.all_to_all(slots.reshape(responses, own, slot_cols), 'resp', 0, 0)]
    pallas_call x0 -> x4, Pallas kernels: none -> 15.4 us  [the longest x1 8.47 us: local(): pl.pallas_call(functools.partial(attend, responses=responses), out_shape=...]
    dynamic_slice x16 -> x0, local copies, waits for them, and re-layouts: 10.4 us -> none  [the longest x12 8.01 us: local(): lax.map(lambda operands: kv_group(operands[0], operands[1], operands[2],...]
    dot_general x20 -> x0, matrix products: 10 us -> none  [the longest x4 4.98 us: one_block(): lax.dot_general(prob_low, grad_rows, contract_rows, preferred_element_typ...]
  transfers between devices with their start and end apart: 2 -> 1, of which waited for: 2 -> 1; matrix products, arithmetic and copies ran while one was open for 3% -> 0% of each run, Pallas kernels for 0% -> 5%
where the time goes in v2:
time: 79.8 us; the launch traced here: 79.3 us
  blocking collectives  33.4 us (42%)
  starting transfers between devices  16.6 us (21%)
  Pallas kernels  15.4 us (19%)
  waiting for transfers between devices  8.06 us (10%)
  local copies, waits for them, and re-layouts  3.06 us (4%)
  between operations  2.72 us (3%)
    all_to_all x1, blocking collectives, local(): lax.all_to_all(blocks.reshape(responses, own, slot_cols), 'resp', 0, 0)  20.7 us
    all_to_all x1, starting transfers between devices, local(): lax.all_to_all(slots.reshape(responses, own, slot_cols), 'resp', 0, 0)  16.6 us
    all_to_all x1, blocking collectives, local(): lax.all_to_all(gain_slots.reshape(others, 2, width), ('dp', 'tensor'), 0, 0)  12.7 us
    pallas_call x1, Pallas kernels, local(): pl.pallas_call(functools.partial(attend, responses=responses), out_shape=...  8.47 us
    all_to_all x1, waiting for transfers between devices, local(): lax.all_to_all(slots.reshape(responses, own, slot_cols), 'resp', 0, 0)  8.06 us
    pallas_call x1, Pallas kernels, local(): pl.pallas_call(prepare, out_shape=(shape((query_heads * length, width), B...  3.82 us
    unnamed x20, local copies, waits for them, and re-layouts  2.54 us
    pallas_call x1, Pallas kernels, local(): pl.pallas_call(add_blocks, out_shape=(shape((own, kv_cols), F32), shape((...  1.64 us
  transfers between devices with their start and end apart: 1, of which 1 were waited for; matrix products, arithmetic and copies ran while one was open for 0% of the time, Pallas kernels for 5%

profile of v2, /device:TPU:1, one launch (start us, length us, event | category | flops | bytes accessed | tf_op | source)
XLA Modules:
  0.0 79.3 jit_solution(12984500878152056957)
XLA Ops:
  1.3 1.4 %send_prompt.1 = bf16[256,640]{1,0:T(8,128)(2,1)} custom-call(f32[1,1]{1,0:T(1,128)S(6)} %copy.20.reward_ref, bf16[8,256]{1,0:T(8,128)(2,1)} %bitcast.37, bf16[8,256]{1,0:T(8,128)(2,1)} %bitcast.38), custom_call_target="tpu_custom_call" | custom-call | tf_op jit(solution)/shard_map/send_prompt/pallas_call | solution.py:245
  2.7 0.0 copy-start.3
  2.7 0.0 copy-start.6
  2.7 16.6 %all-to-all-start = ((bf16[32,8,640]{2,1,0:T(8,128)(2,1)}), bf16[32,8,640]{2,1,0:T(8,128)(2,1)S(1)}, u32[]{:S(2)}, u32[]{:S(2)}) async-start(bf16[32,8,640]{2,1,0:T(8,128)(2,1)} %bitcast.34), calls=%async_computation | async-start | bytes 655360 | tf_op jit(solution)/shard_map/all_to_all | solution.py:252
  19.4 0.0 copy-start
  20.8 0.0 copy-start.1
  20.8 0.0 copy-start.2
  20.8 0.0 copy-start.5
  20.8 3.8 %prepare.1 = (bf16[2048,128]{1,0:T(8,128)(2,1)}, bf16[256,128]{1,0:T(8,128)(2,1)}) custom-call(s32[1]{0:T(128)S(6)} %copy.22.prompt_len_ref, bf16[128,2048]{1,0:T(8,128)(2,1)} %bitcast.22, bf16[128,256]{1,0:T(8,128)(2,1)} %bitcast.27, f32[1,128]{1,0:T(1,128)} %bitcast.30, f32[1,128]{1,0:T(1,128)} %bitcast.32, f32[384,128]{1,0:T(8,128)} %constant.9.clone.cos_ref, ...), custom_call_target="tpu_custom_call" | custom-call | flops 20000000 | bytes 2000000 | tf_op jit(solution)/shard_map/prepare/pallas_call | solution.py:253
  24.6 8.1 %all-to-all-done = bf16[32,8,640]{2,1,0:T(8,128)(2,1)S(1)} async-done(((bf16[32,8,640]{2,1,0:T(8,128)(2,1)}), bf16[32,8,640]{2,1,0:T(8,128)(2,1)S(1)}, u32[]{:S(2)}, u32[]{:S(2)}) %all-to-all-start) | async-done | bytes 327712 | tf_op jit(solution)/shard_map/all_to_all | solution.py:252
  32.7 0.0 copy-start.8
  32.7 0.0 copy-start.9
  32.7 0.0 copy-done.3
  32.7 0.0 copy-done.6
  32.7 0.0 copy-done
  32.7 0.0 copy-done.1
  32.7 0.0 copy-done.2
  32.7 0.0 copy-done.5
  32.7 0.6 copy-done.8
  33.3 0.0 copy-done.9
  33.3 0.0 copy-start.4
  33.3 1.0 %copy-done.4 = bf16[2048,128]{1,0:T(8,128)(2,1)S(1)} copy-done((bf16[2048,128]{1,0:T(8,128)(2,1)S(1)}, bf16[2048,128]{1,0:T(8,128)(2,1)}, u32[]{:S(2)}) %copy-start.4) | copy-done | bytes 524312
  34.4 0.0 copy-start.7
  34.4 0.8 %copy-done.7 = bf16[256,128]{1,0:T(8,128)(2,1)S(1)} copy-done((bf16[256,128]{1,0:T(8,128)(2,1)S(1)}, bf16[256,128]{1,0:T(8,128)(2,1)}, u32[]{:S(2)}) %copy-start.7) | copy-done | bytes 65560
  35.2 8.5 %attend.1 = (bf16[128,2048]{1,0:T(8,128)(2,1)}, bf16[128,256]{1,0:T(8,128)(2,1)}, bf16[128,256]{1,0:T(8,128)(2,1)}, bf16[256,640]{1,0:T(8,128)(2,1)S(1)}) custom-call(f32[1,1]{1,0:T(1,128)S(6)} %copy.20.reward_ref, s32[1,1]{1,0:T(1,128)S(6)} %copy.21.resp_len_ref, s32[1]{0:T(128)S(6)} %copy.22.prompt_len_ref, bf16[256,640]{1,0:T(8,128)(2,1)S(1)} %bitcast.24, ...), custom_call_target="tpu_custom_call" | custom-call | tf_op jit(solution)/shard_map/attend/pallas_call | solution.py:261
  43.7 20.7 %all_to_all.15 = bf16[32,8,640]{2,1,0:T(8,128)(2,1)} all-to-all(bf16[32,8,640]{2,1,0:T(8,128)(2,1)S(1)} %bitcast.26), channel_id=1, replica_groups=mesh['dp'=8,'resp'=32,'tensor'=2] {'resp'}, dimensions={0} | all-to-all | bytes 655360 | tf_op jit(solution)/shard_map/all_to_all | solution.py:286
  64.4 1.6 %add_blocks.1 = (f32[8,256]{1,0:T(8,128)}, f32[8,256]{1,0:T(8,128)}, f32[32,128]{1,0:T(8,128)}) custom-call(bf16[256,640]{1,0:T(8,128)(2,1)} %bitcast.35), custom_call_target="tpu_custom_call" | custom-call | tf_op jit(solution)/shard_map/add_blocks/pallas_call | solution.py:288
  66.0 12.7 %all_to_all.16 = f32[16,2,128]{2,1,0:T(2,128)S(1)} all-to-all(f32[16,2,128]{2,1,0:T(2,128)} %bitcast.36), channel_id=1, replica_groups=mesh['dp'=8,'resp'=32,'tensor'=2] {'dp','tensor'}, dimensions={0} | all-to-all | bytes 32768 | tf_op jit(solution)/shard_map/all_to_all | solution.py:299
  78.8 0.5 slice_bitcast_fusion
  (2 shorter events, 0.0 us)
Async XLA Ops:
  2.7 29.9 %copy-start.3 = (bf16[1,1,128,2048]{3,2,1,0:T(8,128)(2,1)S(1)}, bf16[1,1,128,2048]{3,2,1,0:T(8,128)(2,1)}, u32[]{:S(2)}) copy-start(bf16[1,1,128,2048]{3,2,1,0:T(8,128)(2,1)} %param.20) | copy-start | bytes 1572868
  2.7 29.9 %copy-start.6 = (bf16[1,1,128,256]{3,2,1,0:T(8,128)(2,1)S(1)}, bf16[1,1,128,256]{3,2,1,0:T(8,128)(2,1)}, u32[]{:S(2)}) copy-start(bf16[1,1,128,256]{3,2,1,0:T(8,128)(2,1)} %param.15) | copy-start | bytes 196612
  2.7 29.9 %all-to-all-start = ((bf16[32,8,640]{2,1,0:T(8,128)(2,1)}), bf16[32,8,640]{2,1,0:T(8,128)(2,1)S(1)}, u32[]{:S(2)}, u32[]{:S(2)}) async-start(bf16[32,8,640]{2,1,0:T(8,128)(2,1)} %bitcast.34), calls=%async_computation | async-start | bytes 655360 | tf_op jit(solution)/shard_map/all_to_all | solution.py:252
  19.4 13.3 %copy-start = (bf16[1,1,128,2048]{3,2,1,0:T(8,128)(2,1)S(1)}, bf16[1,1,128,2048]{3,2,1,0:T(8,128)(2,1)}, u32[]{:S(2)}) copy-start(bf16[1,1,128,2048]{3,2,1,0:T(8,128)(2,1)} %param.13) | copy-start | bytes 1572868
  20.8 11.9 %copy-start.1 = (f32[384,128]{1,0:T(8,128)S(1)}, f32[384,128]{1,0:T(8,128)}, u32[]{:S(2)}) copy-start(f32[384,128]{1,0:T(8,128)} %constant.10.clone.sin_ref) | copy-start | bytes 589828
  20.8 11.9 %copy-start.2 = (f32[384,128]{1,0:T(8,128)S(1)}, f32[384,128]{1,0:T(8,128)}, u32[]{:S(2)}) copy-start(f32[384,128]{1,0:T(8,128)} %constant.9.clone.cos_ref) | copy-start | bytes 589828
  20.8 11.9 %copy-start.5 = (bf16[1,1,128,256]{3,2,1,0:T(8,128)(2,1)S(1)}, bf16[1,1,128,256]{3,2,1,0:T(8,128)(2,1)}, u32[]{:S(2)}) copy-start(bf16[1,1,128,256]{3,2,1,0:T(8,128)(2,1)} %param.14) | copy-start | bytes 196612
  32.7 0.7 copy-start.8
  32.7 0.7 copy-start.9
  33.3 1.0 %copy-start.4 = (bf16[2048,128]{1,0:T(8,128)(2,1)S(1)}, bf16[2048,128]{1,0:T(8,128)(2,1)}, u32[]{:S(2)}) copy-start(bf16[2048,128]{1,0:T(8,128)(2,1)} %get-tuple-element.16.query_ref) | copy-start | bytes 1572868
  34.4 0.8 %copy-start.7 = (bf16[256,128]{1,0:T(8,128)(2,1)S(1)}, bf16[256,128]{1,0:T(8,128)(2,1)}, u32[]{:S(2)}) copy-start(bf16[256,128]{1,0:T(8,128)(2,1)} %get-tuple-element.17.key_ref) | copy-start | bytes 196612

commit v3 on v2

v3 whole, which is shorter than its diff:
```python
import functools
import math

import jax
import jax.numpy as jnp
import numpy as np
from jax import lax
from jax.experimental import pallas as pl
from jax.experimental.pallas import tpu as pltpu
from jax.sharding import PartitionSpec as P

EPSILON = 1e-06
THETA = 1000000.0
LOG2_E = math.log2(math.e)
F32, BF16 = jnp.float32, jnp.bfloat16
SMEM = pl.BlockSpec(memory_space=pltpu.SMEM)
VMEM = pl.BlockSpec(memory_space=pltpu.VMEM)
CONTRACT_LAST = (((1,), (1,)), ((), ()))
CONTRACT_FIRST = (((0,), (0,)), ((), ()))
HEADS_AT_ONCE = 4
STEP = 16
UNROLL = 1
UNROLL_KV = 1


def rope_tables(positions, width):
    half = width // 2
    inv_freq = (THETA ** (-(np.arange(half) * 2.0) / width)).astype(np.float32)
    rows = [np.arange(STEP), np.arange(0, positions, STEP)]
    angles = [r[:, None].astype(np.float64) * inv_freq for r in rows]
    sign = np.repeat([-1.0, 1.0], half)
    found = []
    for angle in angles:
        angle = np.concatenate([angle, angle], axis=1)
        found += [np.cos(angle), np.sin(angle) * sign]
    return np.concatenate(found, axis=0).astype(np.float32)


def add_angles(one, other):
    return one[0] * other[0] - one[1] * other[1], one[1] * other[0] + one[0] * other[1]


def rope_at(table_ref, start, count):
    steps = (table_ref.shape[0] - 2 * STEP) // 2
    low = (table_ref[:STEP, :], table_ref[STEP : 2 * STEP, :])

    def high(m):
        first = 2 * STEP + m
        return table_ref[pl.ds(first, 1), :], table_ref[pl.ds(first + steps, 1), :]

    if not isinstance(start, int):
        within = start % STEP
        row = (table_ref[pl.ds(within, 1), :], table_ref[pl.ds(STEP + within, 1), :])
        low = add_angles(low, add_angles(high(start // STEP), row))
    blocks = [add_angles(low, high(m)) for m in range(count // STEP)]
    return tuple(jnp.concatenate([block[i] for block in blocks], axis=0) for i in range(2))


def half_turn(rows):
    return pltpu.roll(rows, rows.shape[1] // 2, 1)


def unit_rows(raw):
    raw = raw.astype(F32)
    inverse = lax.rsqrt(jnp.mean(raw * raw, axis=1, keepdims=True) + EPSILON)
    return raw * inverse, inverse


def rotated(unit, gain, cos, sin):
    normed = unit * gain
    return (normed * cos + half_turn(normed) * sin).astype(BF16)


def norm_rope_back(grad, unit, inverse, gain, cos, sin):
    normed_grad = grad * cos - half_turn(grad) * sin
    term = normed_grad * unit
    mean = jnp.mean(term * gain, axis=1, keepdims=True)
    return inverse * (normed_grad * gain - unit * mean), term


def fold(rows):
    return jnp.sum(rows.reshape(-1, 8, rows.shape[1]), axis=0)


def split_terms(value, terms):
    found = []
    for _ in range(terms):
        found.append(value.astype(BF16).astype(F32))
        value = value - found[-1]
    return found


def send_prompt(key_ref, value_ref, out_ref):
    own = key_ref.shape[0]
    slot = jnp.concatenate([key_ref[...], value_ref[...]], axis=1).astype(F32)
    slots = jnp.concatenate([slot, slot], axis=0).astype(BF16)
    for i in range(out_ref.shape[0] // (2 * own)):
        out_ref[2 * own * i : 2 * own * (i + 1), :] = slots


def head_slices(first, width):
    return [
        pl.ds(pl.multiple_of((first + i) * width, width), width) for i in range(HEADS_AT_ONCE)
    ]


def prepare(
    prompt_len_ref, query_ref, key_ref, query_gain_ref, key_gain_ref, table_ref,
    query_out, key_out, shared_out,
):
    length, width = query_ref.shape[0], query_gain_ref.shape[1]
    cos, sin = rope_at(table_ref, prompt_len_ref[0], length)
    shared_out[: table_ref.shape[0], :] = table_ref[...]
    shared_out[table_ref.shape[0] :, :] = jnp.concatenate(
        [query_gain_ref[...], key_gain_ref[...], jnp.zeros((6, width), F32)], axis=0
    )
    for source, gain_ref, out in (
        (key_ref, key_gain_ref, key_out),
        (query_ref, query_gain_ref, query_out),
    ):
        gain = gain_ref[...]

        def one(h, _, source=source, gain=gain, out=out):
            raw = source[:, pl.ds(pl.multiple_of(h * width, width), width)]
            rows = rotated(unit_rows(raw)[0], gain, cos, sin)
            out[pl.ds(pl.multiple_of(h * length, length), length), :] = rows
            return 0

        lax.fori_loop(0, source.shape[1] // width, one, 0, unroll=2)


def attend(
    reward_ref, resp_len_ref, prompt_len_ref,
    arrived_ref, query_ref, key_ref, shared_ref, raw_query_ref, raw_key_ref, value_ref, grad_ref,
    query_hbm, key_hbm, value_hbm, blocks_out,
    keys, values, key_sum, value_sum, query_terms, key_terms, query_out, key_out, value_out, sems,
    *, responses,
):
    length, width = grad_ref.shape[0], shared_ref.shape[1]
    prefix = arrived_ref.shape[0]
    kv_heads = raw_key_ref.shape[1] // width
    kv_cols = kv_heads * width
    group = grad_ref.shape[1] // kv_cols
    own = prefix // responses
    count = HEADS_AT_ONCE * length
    scale = width**-0.5
    start = prompt_len_ref[0]
    table_ref = shared_ref.at[: shared_ref.shape[0] - 8]
    query_gain, key_gain = (shared_ref[pl.ds(shared_ref.shape[0] - 8 + i, 1), :] for i in range(2))
    cos, sin = rope_at(table_ref, start, length)
    pre_cos, pre_sin = rope_at(table_ref, 0, prefix)

    valid = lax.broadcasted_iota(jnp.int32, (1, count), 1) % length < resp_len_ref[0, 0]
    visible = lax.broadcasted_iota(jnp.int32, (prefix, count), 0) < start
    causal = lax.broadcasted_iota(jnp.int32, (length, count), 0) <= (
        lax.broadcasted_iota(jnp.int32, (length, count), 1) % length
    )
    query_terms[...] = jnp.zeros_like(query_terms)
    key_terms[...] = jnp.zeros_like(key_terms)

    def query_copy(first):
        cols = pl.ds(pl.multiple_of(first * width, width), HEADS_AT_ONCE * width)
        return pltpu.make_async_copy(
            query_out.at[:, cols], query_hbm.at[:, cols], sems.at[first // HEADS_AT_ONCE]
        )

    def one_kv_head(c, _):
        own_cols = pl.ds(pl.multiple_of(c * width, width), width)
        value_cols = pl.ds(pl.multiple_of(kv_cols + c * width, width), width)
        pre_unit, pre_inverse = unit_rows(arrived_ref[:, own_cols])
        keys[:prefix, :] = rotated(pre_unit, key_gain, pre_cos, pre_sin)
        keys[prefix:, :] = key_ref[pl.ds(pl.multiple_of(c * length, length), length), :]
        values[:prefix, :] = arrived_ref[:, value_cols]
        values[prefix:, :] = value_ref[:, own_cols]
        key_sum[...] = jnp.zeros_like(key_sum)
        value_sum[...] = jnp.zeros_like(value_sum)

        def some_heads(p, _):
            first = c * group + p * HEADS_AT_ONCE
            span = pl.ds(pl.multiple_of(first * length, count), count)
            query_rows = query_ref[span, :]
            heads = head_slices(first, width)
            grad_rows = jnp.concatenate([grad_ref[:, cols] for cols in heads], axis=0)
            score = lax.dot_general(
                keys[...], query_rows, CONTRACT_LAST, preferred_element_type=F32
            )
            expo = jnp.exp2(score * (scale * LOG2_E))
            expo = jnp.concatenate(
                [
                    jnp.where(visible, expo[:prefix], 0.0),
                    jnp.where(causal, expo[prefix:], 0.0),
                ],
                axis=0,
            )
            dprob = lax.dot_general(
                values[...], grad_rows, CONTRACT_LAST, preferred_element_type=F32
            )
            inverse_sum = 1.0 / jnp.sum(expo, axis=0, keepdims=True)
            delta = jnp.sum(expo * dprob, axis=0, keepdims=True) * inverse_sum
            weight = jnp.where(valid, inverse_sum, 0.0)
            dscore = (expo * ((dprob - delta) * (weight * scale))).astype(BF16)
            prob = (expo * weight).astype(BF16)
            key_sum[...] += jnp.dot(dscore, query_rows, preferred_element_type=F32)
            value_sum[...] += jnp.dot(prob, grad_rows, preferred_element_type=F32)
            query_grad = lax.dot_general(
                dscore, keys[...], CONTRACT_FIRST, preferred_element_type=F32
            )
            for i, cols in enumerate(heads):
                unit, inverse = unit_rows(raw_query_ref[:, cols])
                raw_grad, term = norm_rope_back(
                    query_grad[i * length : (i + 1) * length], unit, inverse, query_gain, cos, sin
                )
                query_out[:, cols] = raw_grad
                query_terms[...] += fold(term)
            query_copy(first).start()
            return 0

        lax.fori_loop(0, group // HEADS_AT_ONCE, some_heads, 0, unroll=UNROLL)
        raw_grad, term = norm_rope_back(
            key_sum[:prefix, :], pre_unit, pre_inverse, key_gain, pre_cos, pre_sin
        )
        blocks_out[:, own_cols] = raw_grad.astype(BF16)
        blocks_out[:, value_cols] = value_sum[:prefix, :].astype(BF16)
        key_terms[...] += fold(term)
        unit, inverse = unit_rows(raw_key_ref[:, own_cols])
        raw_grad, term = norm_rope_back(key_sum[prefix:, :], unit, inverse, key_gain, cos, sin)
        key_out[:, own_cols] = raw_grad
        value_out[:, own_cols] = value_sum[prefix:, :]
        key_terms[...] += fold(term)
        return 0

    lax.fori_loop(0, kv_heads, one_kv_head, 0, unroll=UNROLL_KV)
    last_copies = [
        pltpu.make_async_copy(key_out, key_hbm, sems.at[kv_heads * group // HEADS_AT_ONCE]),
        pltpu.make_async_copy(value_out, value_hbm, sems.at[kv_heads * group // HEADS_AT_ONCE + 1]),
    ]
    for copy in last_copies:
        copy.start()
    reward = jnp.full((1, width), reward_ref[0, 0], F32)
    rows = split_terms(jnp.sum(query_terms[...], axis=0, keepdims=True), 2)
    rows += split_terms(jnp.sum(key_terms[...], axis=0, keepdims=True), 2)
    rows += split_terms(reward, 3)
    rows = jnp.concatenate(rows + [jnp.zeros((own - len(rows), width), F32)], axis=0)
    pair = jnp.concatenate([rows, rows], axis=0).astype(BF16)
    for i in range(responses // 2):
        blocks_out[2 * own * i : 2 * own * (i + 1), 2 * kv_cols :] = pair
    for copy in [query_copy(h) for h in range(0, kv_heads * group, HEADS_AT_ONCE)] + last_copies:
        copy.wait()


def advantages(tail, responses):
    tail = tail.astype(F32).reshape(responses, -1, tail.shape[1])
    row = lax.broadcasted_iota(jnp.int32, tail.shape, 1)
    reward = jnp.sum(jnp.where((row >= 4) & (row < 7), tail, 0.0), axis=1, keepdims=True)
    mean = jnp.sum(reward, axis=0, keepdims=True) / responses
    return tail, jnp.broadcast_to(reward - mean, tail.shape), mean[0]


def weigh(blocks_ref, gains_out, *, responses):
    width = gains_out.shape[1]
    tail, weights, _ = advantages(blocks_ref[:, blocks_ref.shape[1] - width :], responses)
    terms = jnp.sum(tail * weights, axis=0)
    query, key = terms[0:1] + terms[1:2], terms[2:3] + terms[3:4]
    row = lax.broadcasted_iota(jnp.int32, gains_out.shape, 0)
    gains_out[...] = jnp.where(row % 2 == 0, query, key)


def finish(
    reward_ref, blocks_ref, query_ref, key_ref, value_ref,
    query_out, key_out, value_out, prefix_key_out, prefix_value_out, *, responses,
):
    own, kv_cols = prefix_key_out.shape
    width = blocks_ref.shape[1] - 2 * kv_cols
    _, weights, mean = advantages(blocks_ref[:, 2 * kv_cols :], responses)
    for out, first in ((prefix_key_out, 0), (prefix_value_out, kv_cols)):
        for cols in range(0, kv_cols, width):
            block = blocks_ref[:, first + cols : first + cols + width].astype(F32)
            out[:, cols : cols + width] = jnp.sum(block.reshape(weights.shape) * weights, axis=0)
    weight = (reward_ref[0, 0] - mean)[:, :1]
    for source, out in ((query_ref, query_out), (key_ref, key_out), (value_ref, value_out)):
        out[...] = (source[...] * weight).astype(BF16)


def local(
    query_raw, response_key_input, response_value_input, prompt_key_input, prompt_value_input,
    query_gain, key_gain, grad_out, rewards, resp_len, prompt_len,
):
    length = query_raw.shape[2]
    width = query_gain.shape[0]
    kv_cols = response_key_input.shape[3]
    kv_heads = kv_cols // width
    query_heads = query_raw.shape[3] // width
    responses = lax.axis_size("resp")
    own = prompt_key_input.shape[1]
    prefix = own * responses
    slot_cols = 2 * kv_cols + width
    table = jnp.asarray(rope_tables(prefix + length, width))
    gains = (query_gain.reshape(1, width), key_gain.reshape(1, width))
    query, key, value, grad = (
        a[0, 0] for a in (query_raw, response_key_input, response_value_input, grad_out)
    )
    shape = jax.ShapeDtypeStruct

    slots = pl.pallas_call(
        send_prompt,
        out_shape=pltpu.VMEM((prefix, 2 * kv_cols), BF16),
        in_specs=[VMEM] * 2,
        out_specs=VMEM,
        name="send_prompt",
    )(prompt_key_input[0], prompt_value_input[0])
    arrived = lax.all_to_all(slots.reshape(responses, own, 2 * kv_cols), "resp", 0, 0)
    prepared = pl.pallas_call(
        prepare,
        out_shape=(
            pltpu.VMEM((query_heads * length, width), BF16),
            pltpu.VMEM((kv_heads * length, width), BF16),
            pltpu.VMEM((table.shape[0] + 8, width), F32),
        ),
        in_specs=[SMEM] + [VMEM] * 5,
        out_specs=(VMEM,) * 3,
        cost_estimate=pl.CostEstimate(
            flops=100_000_000, bytes_accessed=4_000_000, transcendentals=0
        ),
        name="prepare",
    )(prompt_len, query, key, *gains, table)
    *grads, blocks = pl.pallas_call(
        functools.partial(attend, responses=responses),
        out_shape=(
            pltpu.HBM(query.shape, F32),
            pltpu.HBM(key.shape, F32),
            pltpu.HBM(key.shape, F32),
            pltpu.VMEM((prefix, slot_cols), BF16),
        ),
        in_specs=[SMEM] * 3 + [VMEM] * 8,
        out_specs=(pl.BlockSpec(memory_space=pltpu.HBM),) * 3 + (VMEM,),
        scratch_shapes=[
            pltpu.VMEM((prefix + length, width), BF16),
            pltpu.VMEM((prefix + length, width), BF16),
            pltpu.VMEM((prefix + length, width), F32),
            pltpu.VMEM((prefix + length, width), F32),
            pltpu.VMEM((8, width), F32),
            pltpu.VMEM((8, width), F32),
            pltpu.VMEM(query.shape, F32),
            pltpu.VMEM(key.shape, F32),
            pltpu.VMEM(key.shape, F32),
            pltpu.SemaphoreType.DMA((query_heads // HEADS_AT_ONCE + 2,)),
        ],
        compiler_params=pltpu.CompilerParams(vmem_limit_bytes=16 * 2**20),
        name="attend",
    )(
        rewards, resp_len, prompt_len, arrived.reshape(prefix, 2 * kv_cols), *prepared,
        query, key, value, grad,
    )
    received = lax.all_to_all(blocks.reshape(responses, own, slot_cols), "resp", 0, 0)
    received = pltpu.with_memory_space_constraint(
        received.reshape(prefix, slot_cols), pltpu.VMEM
    )
    others = lax.axis_size("dp") * lax.axis_size("tensor")
    gain_slots = pl.pallas_call(
        functools.partial(weigh, responses=responses),
        out_shape=pltpu.VMEM((others * 2, width), F32),
        in_specs=[VMEM],
        out_specs=VMEM,
        name="weigh",
    )(received)
    gain_slots = lax.all_to_all(gain_slots.reshape(others, 2, width), ("dp", "tensor"), 0, 0)
    grad_query, grad_key, grad_value, prefix_key, prefix_value = pl.pallas_call(
        functools.partial(finish, responses=responses),
        out_shape=(
            shape(query.shape, BF16),
            shape(key.shape, BF16),
            shape(key.shape, BF16),
            shape((own, kv_cols), F32),
            shape((own, kv_cols), F32),
        ),
        in_specs=[SMEM] + [VMEM] * 4,
        out_specs=(VMEM,) * 5,
        cost_estimate=pl.CostEstimate(
            flops=10_000_000, bytes_accessed=4_000_000, transcendentals=0
        ),
        name="finish",
    )(rewards, received, *grads)
    totals = jnp.sum(gain_slots, axis=0) / (lax.axis_size("dp") * responses)
    return (
        grad_query[None, None],
        grad_key[None, None],
        grad_value[None, None],
        prefix_key[None],
        prefix_value[None],
        totals[0],
        totals[1],
    )


def solution(mesh):
    token_spec = P("dp", "resp", None, "tensor")
    prompt_spec = P("dp", "resp", "tensor")
    return jax.shard_map(
        local,
        mesh=mesh,
        in_specs=(token_spec,) * 3 + (prompt_spec,) * 2 + (P(), P(), token_spec)
        + (P("dp", "resp"), P("dp", "resp"), P("dp")),
        out_specs=(token_spec,) * 3 + (prompt_spec,) * 2 + (P(), P()),
        check_vma=False,
    )
```

time: 79.8 us -> 71.7 us (0.90)
  blocking collectives: 33.4 us -> 19.7 us
  starting transfers between devices: 16.6 us -> 23.9 us
  waiting for transfers between devices: 8.06 us -> 11.1 us
  local copies, waits for them, and re-layouts: 3.06 us -> 0.54 us
  Pallas kernels: 15.4 us -> 13.4 us
    all_to_all x1 -> x0, blocking collectives: 12.7 us -> none  [local(): lax.all_to_all(gain_slots.reshape(others, 2, width), ('dp', 'tensor'), 0, 0)]
    all_to_all x1 -> x2, starting transfers between devices: 16.6 us -> 23.9 us  [the longest x1 16.6 us: local(): lax.all_to_all(slots.reshape(responses, own, 2 * kv_cols), 'resp', 0, 0)]
    all_to_all x1 -> x2, waiting for transfers between devices: 8.06 us -> 11.1 us  [the longest x1 7.61 us: local(): lax.all_to_all(slots.reshape(responses, own, 2 * kv_cols), 'resp', 0, 0)]
    unnamed x20 -> x8, local copies, waits for them, and re-layouts: 2.54 us -> 0.02 us
    pallas_call x1, Pallas kernels: 8.47 us -> 6.11 us  [local(): pl.pallas_call(functools.partial(attend, responses=responses), out_shape=...]
    all_to_all x1, blocking collectives: 20.7 us -> 19.7 us  [local(): lax.all_to_all(blocks.reshape(responses, own, slot_cols), 'resp', 0, 0)]
    pallas_call x3 -> x4, Pallas kernels: 6.9 us -> 7.33 us  [the longest x1 2.89 us: local(): pl.pallas_call(prepare, out_shape=(pltpu.VMEM((query_heads * length, widt...]
  transfers between devices with their start and end apart: 1 -> 2, of which waited for: 1 -> 2; matrix products, arithmetic and copies ran while one was open for 0% -> 0% of each run, Pallas kernels for 5% -> 7%
where the time goes in v3:
time: 71.7 us; the launch traced here: 71.3 us
  starting transfers between devices  23.9 us (33%)
  blocking collectives  19.7 us (27%)
  Pallas kernels  13.4 us (19%)
  waiting for transfers between devices  11.1 us (15%)
  between operations  2.63 us (4%)
    all_to_all x1, blocking collectives, local(): lax.all_to_all(blocks.reshape(responses, own, slot_cols), 'resp', 0, 0)  19.7 us
    all_to_all x1, starting transfers between devices, local(): lax.all_to_all(slots.reshape(responses, own, 2 * kv_cols), 'resp', 0, 0)  16.6 us
    all_to_all x1, waiting for transfers between devices, local(): lax.all_to_all(slots.reshape(responses, own, 2 * kv_cols), 'resp', 0, 0)  7.61 us
    all_to_all x1, starting transfers between devices, local(): lax.all_to_all(gain_slots.reshape(others, 2, width), ('dp', 'tensor'), 0, 0)  7.29 us
    pallas_call x1, Pallas kernels, local(): pl.pallas_call(functools.partial(attend, responses=responses), out_shape=...  6.11 us
    all_to_all x1, waiting for transfers between devices, local(): lax.all_to_all(gain_slots.reshape(others, 2, width), ('dp', 'tensor'), 0, 0)  3.45 us
    pallas_call x1, Pallas kernels, local(): pl.pallas_call(prepare, out_shape=(pltpu.VMEM((query_heads * length, widt...  2.89 us
    pallas_call x1, Pallas kernels, local(): pl.pallas_call(functools.partial(finish, responses=responses), out_shape=...  2.34 us
  transfers between devices with their start and end apart: 2, of which 2 were waited for; matrix products, arithmetic and copies ran while one was open for 0% of the time, Pallas kernels for 7%

profile of v3, /device:TPU:1, one launch (start us, length us, event | category | flops | bytes accessed | tf_op | source)
XLA Modules:
  0.0 71.3 jit_solution(2875216087644209313)
XLA Ops:
  0.6 1.4 %send_prompt.1 = bf16[256,512]{1,0:T(8,128)(2,1)} custom-call(bf16[8,256]{1,0:T(8,128)(2,1)} %bitcast.32, bf16[8,256]{1,0:T(8,128)(2,1)} %bitcast.33), custom_call_target="tpu_custom_call" | custom-call | tf_op jit(solution)/shard_map/send_prompt/pallas_call | solution.py:304
  2.1 0.0 copy-start
  2.1 0.0 copy-start.1
  2.1 16.6 %all-to-all-start = ((bf16[32,8,512]{2,1,0:T(8,128)(2,1)}), bf16[32,8,512]{2,1,0:T(8,128)(2,1)S(1)}, u32[]{:S(2)}, u32[]{:S(2)}) async-start(bf16[32,8,512]{2,1,0:T(8,128)(2,1)} %bitcast.2), calls=%async_computation | async-start | bytes 524288 | tf_op jit(solution)/shard_map/all_to_all | solution.py:311
  20.7 0.0 copy-start.2
  20.7 0.0 copy-start.3
  20.7 2.9 %prepare.1 = (bf16[2048,128]{1,0:T(8,128)(2,1)S(1)}, bf16[256,128]{1,0:T(8,128)(2,1)S(1)}, f32[88,128]{1,0:T(8,128)S(1)}) custom-call(s32[1]{0:T(128)S(6)} %copy.21.prompt_len_ref, bf16[128,2048]{1,0:T(8,128)(2,1)} %bitcast.24, bf16[128,256]{1,0:T(8,128)(2,1)} %bitcast.29, f32[1,128]{1,0:T(1,128)} %bitcast.34, f32[1,128]{1,0:T(1,128)} %bitcast.35, ...), custom_call_target="tpu_custom_call" | custom-call | flops 100000000 | bytes 4000000 | tf_op jit(solution)/shard_map/prepare/pallas_call | solution.py:312
  23.6 7.6 %all-to-all-done = bf16[32,8,512]{2,1,0:T(8,128)(2,1)S(1)} async-done(((bf16[32,8,512]{2,1,0:T(8,128)(2,1)}), bf16[32,8,512]{2,1,0:T(8,128)(2,1)S(1)}, u32[]{:S(2)}, u32[]{:S(2)}) %all-to-all-start) | async-done | bytes 262176 | tf_op jit(solution)/shard_map/all_to_all | solution.py:311
  31.2 0.0 copy-done
  31.2 0.0 copy-done.1
  31.2 0.0 copy-done.2
  31.2 0.0 copy-done.3
  31.2 6.1 %attend.1 = (f32[128,2048]{1,0:T(8,128)}, f32[128,256]{1,0:T(8,128)}, f32[128,256]{1,0:T(8,128)}, bf16[256,640]{1,0:T(8,128)(2,1)S(1)}) custom-call(f32[1,1]{1,0:T(1,128)S(6)} %copy.19.reward_ref, s32[1,1]{1,0:T(1,128)S(6)} %copy.20.resp_len_ref, s32[1]{0:T(128)S(6)} %copy.21.prompt_len_ref, bf16[256,512]{1,0:T(8,128)(2,1)S(1)} %bitcast.26, ...), custom_call_target="tpu_custom_call" | custom-call | tf_op jit(solution)/shard_map/attend/pallas_call | solution.py:326
  37.3 19.7 %all_to_all.15 = bf16[32,8,640]{2,1,0:T(8,128)(2,1)S(1)} all-to-all(bf16[32,8,640]{2,1,0:T(8,128)(2,1)S(1)} %bitcast.28), channel_id=1, replica_groups=mesh['dp'=8,'resp'=32,'tensor'=2] {'resp'}, dimensions={0} | all-to-all | bytes 655360 | tf_op jit(solution)/shard_map/all_to_all | solution.py:354
  57.0 0.7 weigh.1
  57.7 7.3 %all-to-all-start.2 = ((f32[16,2,128]{2,1,0:T(2,128)}), f32[16,2,128]{2,1,0:T(2,128)S(1)}, u32[]{:S(2)}, u32[]{:S(2)}) async-start(f32[16,2,128]{2,1,0:T(2,128)} %bitcast.17), calls=%async_computation.2 | async-start | bytes 32768 | tf_op jit(solution)/shard_map/all_to_all | solution.py:366
  65.0 2.3 %finish.1 = (bf16[128,2048]{1,0:T(8,128)(2,1)}, bf16[128,256]{1,0:T(8,128)(2,1)}, bf16[128,256]{1,0:T(8,128)(2,1)}, f32[8,256]{1,0:T(8,128)}, f32[8,256]{1,0:T(8,128)}) custom-call(f32[1,1]{1,0:T(1,128)S(6)} %copy.19.reward_ref, bf16[256,640]{1,0:T(8,128)(2,1)S(1)} %bitcast.23, f32[128,2048]{1,0:T(8,128)} %get-tuple-element.23.query_ref, ...), custom_call_target="tpu_custom_call" | custom-call | flops 10000000 | bytes 4000000 | tf_op jit(solution)/shard_map/finish/pallas_call | solution.py:367
  67.3 3.4 %all-to-all-done.2 = f32[16,2,128]{2,1,0:T(2,128)S(1)} async-done(((f32[16,2,128]{2,1,0:T(2,128)}), f32[16,2,128]{2,1,0:T(2,128)S(1)}, u32[]{:S(2)}, u32[]{:S(2)}) %all-to-all-start.2) | async-done | bytes 16416 | tf_op jit(solution)/shard_map/all_to_all | solution.py:366
  70.8 0.5 slice_bitcast_fusion
  (2 shorter events, 0.0 us)
Async XLA Ops:
  2.1 29.1 %copy-start = (bf16[1,1,128,2048]{3,2,1,0:T(8,128)(2,1)S(1)}, bf16[1,1,128,2048]{3,2,1,0:T(8,128)(2,1)}, u32[]{:S(2)}) copy-start(bf16[1,1,128,2048]{3,2,1,0:T(8,128)(2,1)} %param.12) | copy-start | bytes 1572868
  2.1 29.1 %copy-start.1 = (bf16[1,1,128,2048]{3,2,1,0:T(8,128)(2,1)S(1)}, bf16[1,1,128,2048]{3,2,1,0:T(8,128)(2,1)}, u32[]{:S(2)}) copy-start(bf16[1,1,128,2048]{3,2,1,0:T(8,128)(2,1)} %param.19) | copy-start | bytes 1572868
  2.1 29.1 %all-to-all-start = ((bf16[32,8,512]{2,1,0:T(8,128)(2,1)}), bf16[32,8,512]{2,1,0:T(8,128)(2,1)S(1)}, u32[]{:S(2)}, u32[]{:S(2)}) async-start(bf16[32,8,512]{2,1,0:T(8,128)(2,1)} %bitcast.2), calls=%async_computation | async-start | bytes 524288 | tf_op jit(solution)/shard_map/all_to_all | solution.py:311
  20.7 10.5 %copy-start.2 = (bf16[1,1,128,256]{3,2,1,0:T(8,128)(2,1)S(1)}, bf16[1,1,128,256]{3,2,1,0:T(8,128)(2,1)}, u32[]{:S(2)}) copy-start(bf16[1,1,128,256]{3,2,1,0:T(8,128)(2,1)} %param.13) | copy-start | bytes 196612
  20.7 10.5 %copy-start.3 = (bf16[1,1,128,256]{3,2,1,0:T(8,128)(2,1)S(1)}, bf16[1,1,128,256]{3,2,1,0:T(8,128)(2,1)}, u32[]{:S(2)}) copy-start(bf16[1,1,128,256]{3,2,1,0:T(8,128)(2,1)} %param.14) | copy-start | bytes 196612
  57.7 13.1 %all-to-all-start.2 = ((f32[16,2,128]{2,1,0:T(2,128)}), f32[16,2,128]{2,1,0:T(2,128)S(1)}, u32[]{:S(2)}, u32[]{:S(2)}) async-start(f32[16,2,128]{2,1,0:T(2,128)} %bitcast.17), calls=%async_computation.2 | async-start | bytes 32768 | tf_op jit(solution)/shard_map/all_to_all | solution.py:366

commit v4 on v3

--- a/solution.py
+++ b/solution.py
@@ -17,10 +17,9 @@
 VMEM = pl.BlockSpec(memory_space=pltpu.VMEM)
 CONTRACT_LAST = (((1,), (1,)), ((), ()))
 CONTRACT_FIRST = (((0,), (0,)), ((), ()))
-HEADS_AT_ONCE = 4
+HEADS_AT_ONCE = 2
 STEP = 16
-UNROLL = 1
-UNROLL_KV = 1
+UNROLL = 2
 
 
 def rope_tables(positions, width):
@@ -147,7 +146,7 @@
     start = prompt_len_ref[0]
     table_ref = shared_ref.at[: shared_ref.shape[0] - 8]
     query_gain, key_gain = (shared_ref[pl.ds(shared_ref.shape[0] - 8 + i, 1), :] for i in range(2))
-    cos, sin = rope_at(table_ref, start, length)
+    back_cos, back_sin = (t * scale for t in rope_at(table_ref, start, length))
     pre_cos, pre_sin = rope_at(table_ref, 0, prefix)
 
     valid = lax.broadcasted_iota(jnp.int32, (1, count), 1) % length < resp_len_ref[0, 0]
@@ -164,78 +163,86 @@
             query_out.at[:, cols], query_hbm.at[:, cols], sems.at[first // HEADS_AT_ONCE]
         )
 
-    def one_kv_head(c, _):
-        own_cols = pl.ds(pl.multiple_of(c * width, width), width)
-        value_cols = pl.ds(pl.multiple_of(kv_cols + c * width, width), width)
-        pre_unit, pre_inverse = unit_rows(arrived_ref[:, own_cols])
-        keys[:prefix, :] = rotated(pre_unit, key_gain, pre_cos, pre_sin)
-        keys[prefix:, :] = key_ref[pl.ds(pl.multiple_of(c * length, length), length), :]
-        values[:prefix, :] = arrived_ref[:, value_cols]
-        values[prefix:, :] = value_ref[:, own_cols]
-        key_sum[...] = jnp.zeros_like(key_sum)
-        value_sum[...] = jnp.zeros_like(value_sum)
-
-        def some_heads(p, _):
-            first = c * group + p * HEADS_AT_ONCE
-            span = pl.ds(pl.multiple_of(first * length, count), count)
-            query_rows = query_ref[span, :]
-            heads = head_slices(first, width)
-            grad_rows = jnp.concatenate([grad_ref[:, cols] for cols in heads], axis=0)
-            score = lax.dot_general(
-                keys[...], query_rows, CONTRACT_LAST, preferred_element_type=F32
+    units = []
+    for c in range(kv_heads):
+        unit = unit_rows(arrived_ref[:, c * width : (c + 1) * width])
+        units.append(unit)
+        keys[c, :prefix, :] = rotated(unit[0], key_gain, pre_cos, pre_sin)
+        keys[c, prefix:, :] = key_ref[c * length : (c + 1) * length, :]
+        values[c, :prefix, :] = arrived_ref[:, kv_cols + c * width : kv_cols + (c + 1) * width]
+        values[c, prefix:, :] = value_ref[:, c * width : (c + 1) * width]
+    key_sum[...] = jnp.zeros_like(key_sum)
+    value_sum[...] = jnp.zeros_like(value_sum)
+
+    def products(c, first):
+        span = pl.ds(pl.multiple_of(first * length, length), count)
+        query_rows = query_ref[span, :]
+        grad_rows = jnp.concatenate(
+            [grad_ref[:, cols] for cols in head_slices(first, width)], axis=0
+        )
+        score = lax.dot_general(keys[c], query_rows, CONTRACT_LAST, preferred_element_type=F32)
+        dprob = lax.dot_general(values[c], grad_rows, CONTRACT_LAST, preferred_element_type=F32)
+        return query_rows, grad_rows, score, dprob
+
+    def softmax(score, dprob):
+        expo = jnp.exp2(score * (scale * LOG2_E))
+        expo = jnp.concatenate(
+            [jnp.where(visible, expo[:prefix], 0.0), jnp.where(causal, expo[prefix:], 0.0)], axis=0
+        )
+        inverse_sum = 1.0 / jnp.sum(expo, axis=0, keepdims=True)
+        delta = jnp.sum(expo * dprob, axis=0, keepdims=True) * inverse_sum
+        prob = expo * jnp.where(valid, inverse_sum, 0.0)
+        return prob.astype(BF16), (prob * (dprob - delta)).astype(BF16)
+
+    def some_heads(p, _):
+        firsts = [c * group + p * HEADS_AT_ONCE for c in range(kv_heads)]
+        blocks = [products(c, first) for c, first in enumerate(firsts)]
+        probs = [softmax(*block[2:]) for block in blocks]
+        query_grads = []
+        for c, (prob, dscore) in enumerate(probs):
+            query_rows, grad_rows = blocks[c][:2]
+            key_sum[c] += jnp.dot(dscore, query_rows, preferred_element_type=F32)
+            value_sum[c] += jnp.dot(prob, grad_rows, preferred_element_type=F32)
+            query_grads.append(
+                lax.dot_general(dscore, keys[c], CONTRACT_FIRST, preferred_element_type=F32)
             )
-            expo = jnp.exp2(score * (scale * LOG2_E))
-            expo = jnp.concatenate(
-                [
-                    jnp.where(visible, expo[:prefix], 0.0),
-                    jnp.where(causal, expo[prefix:], 0.0),
-                ],
-                axis=0,
-            )
-            dprob = lax.dot_general(
-                values[...], grad_rows, CONTRACT_LAST, preferred_element_type=F32
-            )
-            inverse_sum = 1.0 / jnp.sum(expo, axis=0, keepdims=True)
-            delta = jnp.sum(expo * dprob, axis=0, keepdims=True) * inverse_sum
-            weight = jnp.where(valid, inverse_sum, 0.0)
-            dscore = (expo * ((dprob - delta) * (weight * scale))).astype(BF16)
-            prob = (expo * weight).astype(BF16)
-            key_sum[...] += jnp.dot(dscore, query_rows, preferred_element_type=F32)
-            value_sum[...] += jnp.dot(prob, grad_rows, preferred_element_type=F32)
-            query_grad = lax.dot_general(
-                dscore, keys[...], CONTRACT_FIRST, preferred_element_type=F32
-            )
-            for i, cols in enumerate(heads):
+        for first, query_grad in zip(firsts, query_grads):
+            for i, cols in enumerate(head_slices(first, width)):
                 unit, inverse = unit_rows(raw_query_ref[:, cols])
                 raw_grad, term = norm_rope_back(
-                    query_grad[i * length : (i + 1) * length], unit, inverse, query_gain, cos, sin
+                    query_grad[i * length : (i + 1) * length], unit, inverse, query_gain,
+                    back_cos, back_sin,
                 )
                 query_out[:, cols] = raw_grad
                 query_terms[...] += fold(term)
             query_copy(first).start()
-            return 0
-
-        lax.fori_loop(0, group // HEADS_AT_ONCE, some_heads, 0, unroll=UNROLL)
+        return 0
+
+    lax.fori_loop(0, group // HEADS_AT_ONCE, some_heads, 0, unroll=UNROLL)
+    for c in range(kv_heads):
+        own_cols = slice(c * width, (c + 1) * width)
+        unit, inverse = unit_rows(raw_key_ref[:, own_cols])
         raw_grad, term = norm_rope_back(
-            key_sum[:prefix, :], pre_unit, pre_inverse, key_gain, pre_cos, pre_sin
+            key_sum[c, prefix:, :], unit, inverse, key_gain, back_cos, back_sin
         )
-        blocks_out[:, own_cols] = raw_grad.astype(BF16)
-        blocks_out[:, value_cols] = value_sum[:prefix, :].astype(BF16)
+        key_out[:, own_cols] = raw_grad
+        value_out[:, own_cols] = value_sum[c, prefix:, :]
         key_terms[...] += fold(term)
-        unit, inverse = unit_rows(raw_key_ref[:, own_cols])
-        raw_grad, term = norm_rope_back(key_sum[prefix:, :], unit, inverse, key_gain, cos, sin)
-        key_out[:, own_cols] = raw_grad
-        value_out[:, own_cols] = value_sum[prefix:, :]
-        key_terms[...] += fold(term)
-        return 0
-
-    lax.fori_loop(0, kv_heads, one_kv_head, 0, unroll=UNROLL_KV)
     last_copies = [
         pltpu.make_async_copy(key_out, key_hbm, sems.at[kv_heads * group // HEADS_AT_ONCE]),
         pltpu.make_async_copy(value_out, value_hbm, sems.at[kv_heads * group // HEADS_AT_ONCE + 1]),
     ]
     for copy in last_copies:
         copy.start()
+    for c in range(kv_heads):
+        raw_grad, term = norm_rope_back(
+            key_sum[c, :prefix, :], *units[c], key_gain, pre_cos * scale, pre_sin * scale
+        )
+        blocks_out[:, c * width : (c + 1) * width] = raw_grad.astype(BF16)
+        blocks_out[:, kv_cols + c * width : kv_cols + (c + 1) * width] = value_sum[
+            c, :prefix, :
+        ].astype(BF16)
+        key_terms[...] += fold(term)
     reward = jnp.full((1, width), reward_ref[0, 0], F32)
     rows = split_terms(jnp.sum(query_terms[...], axis=0, keepdims=True), 2)
     rows += split_terms(jnp.sum(key_terms[...], axis=0, keepdims=True), 2)
@@ -334,10 +341,10 @@
         in_specs=[SMEM] * 3 + [VMEM] * 8,
         out_specs=(pl.BlockSpec(memory_space=pltpu.HBM),) * 3 + (VMEM,),
         scratch_shapes=[
-            pltpu.VMEM((prefix + length, width), BF16),
-            pltpu.VMEM((prefix + length, width), BF16),
-            pltpu.VMEM((prefix + length, width), F32),
-            pltpu.VMEM((prefix + length, width), F32),
+            pltpu.VMEM((kv_heads, prefix + length, width), BF16),
+            pltpu.VMEM((kv_heads, prefix + length, width), BF16),
+            pltpu.VMEM((kv_heads, prefix + length, width), F32),
+            pltpu.VMEM((kv_heads, prefix + length, width), F32),
             pltpu.VMEM((8, width), F32),
             pltpu.VMEM((8, width), F32),
             pltpu.VMEM(query.shape, F32),

time: 71.7 us -> 70.5 us (0.983)
  Pallas kernels: 13.4 us -> 12.2 us
    pallas_call x1, Pallas kernels: 6.11 us -> 4.89 us  [local(): pl.pallas_call(functools.partial(attend, responses=responses), out_shape=...]
where the time goes in v4:
time: 70.5 us; the launch traced here: 70.1 us
  starting transfers between devices  23.9 us (34%)
  blocking collectives  19.7 us (28%)
  Pallas kernels  12.2 us (17%)
  waiting for transfers between devices  11.1 us (16%)
  between operations  2.63 us (4%)
    all_to_all x1, blocking collectives, local(): lax.all_to_all(blocks.reshape(responses, own, slot_cols), 'resp', 0, 0)  19.7 us
    all_to_all x1, starting transfers between devices, local(): lax.all_to_all(slots.reshape(responses, own, 2 * kv_cols), 'resp', 0, 0)  16.6 us
    all_to_all x1, waiting for transfers between devices, local(): lax.all_to_all(slots.reshape(responses, own, 2 * kv_cols), 'resp', 0, 0)  7.61 us
    all_to_all x1, starting transfers between devices, local(): lax.all_to_all(gain_slots.reshape(others, 2, width), ('dp', 'tensor'), 0, 0)  7.26 us
    pallas_call x1, Pallas kernels, local(): pl.pallas_call(functools.partial(attend, responses=responses), out_shape=...  4.89 us
    all_to_all x1, waiting for transfers between devices, local(): lax.all_to_all(gain_slots.reshape(others, 2, width), ('dp', 'tensor'), 0, 0)  3.45 us
    pallas_call x1, Pallas kernels, local(): pl.pallas_call(prepare, out_shape=(pltpu.VMEM((query_heads * length, widt...  2.89 us
    pallas_call x1, Pallas kernels, local(): pl.pallas_call(functools.partial(finish, responses=responses), out_shape=...  2.34 us
  transfers between devices with their start and end apart: 2, of which 2 were waited for; matrix products, arithmetic and copies ran while one was open for 0% of the time, Pallas kernels for 7%

profile of v4, /device:TPU:1, one launch (start us, length us, event | category | flops | bytes accessed | tf_op | source)
XLA Modules:
  0.0 70.1 jit_solution(17140602131338884898)
XLA Ops:
  0.6 1.4 %send_prompt.1 = bf16[256,512]{1,0:T(8,128)(2,1)} custom-call(bf16[8,256]{1,0:T(8,128)(2,1)} %bitcast.32, bf16[8,256]{1,0:T(8,128)(2,1)} %bitcast.33), custom_call_target="tpu_custom_call" | custom-call | tf_op jit(solution)/shard_map/send_prompt/pallas_call | solution.py:311
  2.1 0.0 copy-start
  2.1 0.0 copy-start.1
  2.1 16.6 %all-to-all-start = ((bf16[32,8,512]{2,1,0:T(8,128)(2,1)}), bf16[32,8,512]{2,1,0:T(8,128)(2,1)S(1)}, u32[]{:S(2)}, u32[]{:S(2)}) async-start(bf16[32,8,512]{2,1,0:T(8,128)(2,1)} %bitcast.2), calls=%async_computation | async-start | bytes 524288 | tf_op jit(solution)/shard_map/all_to_all | solution.py:318
  20.7 0.0 copy-start.2
  20.7 0.0 copy-start.3
  20.7 2.9 %prepare.1 = (bf16[2048,128]{1,0:T(8,128)(2,1)S(1)}, bf16[256,128]{1,0:T(8,128)(2,1)S(1)}, f32[88,128]{1,0:T(8,128)S(1)}) custom-call(s32[1]{0:T(128)S(6)} %copy.21.prompt_len_ref, bf16[128,2048]{1,0:T(8,128)(2,1)} %bitcast.24, bf16[128,256]{1,0:T(8,128)(2,1)} %bitcast.29, f32[1,128]{1,0:T(1,128)} %bitcast.34, f32[1,128]{1,0:T(1,128)} %bitcast.35, ...), custom_call_target="tpu_custom_call" | custom-call | flops 100000000 | bytes 4000000 | tf_op jit(solution)/shard_map/prepare/pallas_call | solution.py:319
  23.6 7.6 %all-to-all-done = bf16[32,8,512]{2,1,0:T(8,128)(2,1)S(1)} async-done(((bf16[32,8,512]{2,1,0:T(8,128)(2,1)}), bf16[32,8,512]{2,1,0:T(8,128)(2,1)S(1)}, u32[]{:S(2)}, u32[]{:S(2)}) %all-to-all-start) | async-done | bytes 262176 | tf_op jit(solution)/shard_map/all_to_all | solution.py:318
  31.2 0.0 copy-done
  31.2 0.0 copy-done.1
  31.2 0.0 copy-done.2
  31.2 0.0 copy-done.3
  31.2 4.9 %attend.1 = (f32[128,2048]{1,0:T(8,128)}, f32[128,256]{1,0:T(8,128)}, f32[128,256]{1,0:T(8,128)}, bf16[256,640]{1,0:T(8,128)(2,1)S(1)}) custom-call(f32[1,1]{1,0:T(1,128)S(6)} %copy.19.reward_ref, s32[1,1]{1,0:T(1,128)S(6)} %copy.20.resp_len_ref, s32[1]{0:T(128)S(6)} %copy.21.prompt_len_ref, bf16[256,512]{1,0:T(8,128)(2,1)S(1)} %bitcast.26, ...), custom_call_target="tpu_custom_call" | custom-call | tf_op jit(solution)/shard_map/attend/pallas_call | solution.py:333
  36.1 19.7 %all_to_all.15 = bf16[32,8,640]{2,1,0:T(8,128)(2,1)S(1)} all-to-all(bf16[32,8,640]{2,1,0:T(8,128)(2,1)S(1)} %bitcast.28), channel_id=1, replica_groups=mesh['dp'=8,'resp'=32,'tensor'=2] {'resp'}, dimensions={0} | all-to-all | bytes 655360 | tf_op jit(solution)/shard_map/all_to_all | solution.py:361
  55.8 0.7 weigh.1
  56.5 7.3 %all-to-all-start.2 = ((f32[16,2,128]{2,1,0:T(2,128)}), f32[16,2,128]{2,1,0:T(2,128)S(1)}, u32[]{:S(2)}, u32[]{:S(2)}) async-start(f32[16,2,128]{2,1,0:T(2,128)} %bitcast.17), calls=%async_computation.2 | async-start | bytes 32768 | tf_op jit(solution)/shard_map/all_to_all | solution.py:373
  63.8 2.3 %finish.1 = (bf16[128,2048]{1,0:T(8,128)(2,1)}, bf16[128,256]{1,0:T(8,128)(2,1)}, bf16[128,256]{1,0:T(8,128)(2,1)}, f32[8,256]{1,0:T(8,128)}, f32[8,256]{1,0:T(8,128)}) custom-call(f32[1,1]{1,0:T(1,128)S(6)} %copy.19.reward_ref, bf16[256,640]{1,0:T(8,128)(2,1)S(1)} %bitcast.23, f32[128,2048]{1,0:T(8,128)} %get-tuple-element.23.query_ref, ...), custom_call_target="tpu_custom_call" | custom-call | flops 10000000 | bytes 4000000 | tf_op jit(solution)/shard_map/finish/pallas_call | solution.py:374
  66.1 3.4 %all-to-all-done.2 = f32[16,2,128]{2,1,0:T(2,128)S(1)} async-done(((f32[16,2,128]{2,1,0:T(2,128)}), f32[16,2,128]{2,1,0:T(2,128)S(1)}, u32[]{:S(2)}, u32[]{:S(2)}) %all-to-all-start.2) | async-done | bytes 16416 | tf_op jit(solution)/shard_map/all_to_all | solution.py:373
  69.6 0.5 slice_bitcast_fusion
  (2 shorter events, 0.0 us)
Async XLA Ops:
  2.1 29.1 %copy-start = (bf16[1,1,128,2048]{3,2,1,0:T(8,128)(2,1)S(1)}, bf16[1,1,128,2048]{3,2,1,0:T(8,128)(2,1)}, u32[]{:S(2)}) copy-start(bf16[1,1,128,2048]{3,2,1,0:T(8,128)(2,1)} %param.12) | copy-start | bytes 1572868
  2.1 29.1 %copy-start.1 = (bf16[1,1,128,2048]{3,2,1,0:T(8,128)(2,1)S(1)}, bf16[1,1,128,2048]{3,2,1,0:T(8,128)(2,1)}, u32[]{:S(2)}) copy-start(bf16[1,1,128,2048]{3,2,1,0:T(8,128)(2,1)} %param.19) | copy-start | bytes 1572868
  2.1 29.1 %all-to-all-start = ((bf16[32,8,512]{2,1,0:T(8,128)(2,1)}), bf16[32,8,512]{2,1,0:T(8,128)(2,1)S(1)}, u32[]{:S(2)}, u32[]{:S(2)}) async-start(bf16[32,8,512]{2,1,0:T(8,128)(2,1)} %bitcast.2), calls=%async_computation | async-start | bytes 524288 | tf_op jit(solution)/shard_map/all_to_all | solution.py:318
  20.7 10.5 %copy-start.2 = (bf16[1,1,128,256]{3,2,1,0:T(8,128)(2,1)S(1)}, bf16[1,1,128,256]{3,2,1,0:T(8,128)(2,1)}, u32[]{:S(2)}) copy-start(bf16[1,1,128,256]{3,2,1,0:T(8,128)(2,1)} %param.13) | copy-start | bytes 196612
  20.7 10.5 %copy-start.3 = (bf16[1,1,128,256]{3,2,1,0:T(8,128)(2,1)S(1)}, bf16[1,1,128,256]{3,2,1,0:T(8,128)(2,1)}, u32[]{:S(2)}) copy-start(bf16[1,1,128,256]{3,2,1,0:T(8,128)(2,1)} %param.14) | copy-start | bytes 196612
  56.5 13.0 %all-to-all-start.2 = ((f32[16,2,128]{2,1,0:T(2,128)}), f32[16,2,128]{2,1,0:T(2,128)S(1)}, u32[]{:S(2)}, u32[]{:S(2)}) async-start(f32[16,2,128]{2,1,0:T(2,128)} %bitcast.17), calls=%async_computation.2 | async-start | bytes 32768 | tf_op jit(solution)/shard_map/all_to_all | solution.py:373

commit v5 on v4

--- a/solution.py
+++ b/solution.py
@@ -131,9 +131,8 @@
 def attend(
     reward_ref, resp_len_ref, prompt_len_ref,
     arrived_ref, query_ref, key_ref, shared_ref, raw_query_ref, raw_key_ref, value_ref, grad_ref,
-    query_hbm, key_hbm, value_hbm, blocks_out,
-    keys, values, key_sum, value_sum, query_terms, key_terms, query_out, key_out, value_out, sems,
-    *, responses,
+    query_hbm, last_out, key_out, value_out, blocks_out,
+    keys, values, key_sum, value_sum, query_terms, key_terms, query_out, sems, *, responses,
 ):
     length, width = grad_ref.shape[0], shared_ref.shape[1]
     prefix = arrived_ref.shape[0]
@@ -157,10 +156,14 @@
     query_terms[...] = jnp.zeros_like(query_terms)
     key_terms[...] = jnp.zeros_like(key_terms)
 
-    def query_copy(first):
-        cols = pl.ds(pl.multiple_of(first * width, width), HEADS_AT_ONCE * width)
+    steps = group // HEADS_AT_ONCE
+    step_cols = HEADS_AT_ONCE * width
+
+    def query_copy(c, p):
+        source = pl.ds(pl.multiple_of((c * steps + p) * step_cols, step_cols), step_cols)
+        target = pl.ds(pl.multiple_of((c * (steps - 1) + p) * step_cols, step_cols), step_cols)
         return pltpu.make_async_copy(
-            query_out.at[:, cols], query_hbm.at[:, cols], sems.at[first // HEADS_AT_ONCE]
+            query_out.at[:, source], query_hbm.at[:, target], sems.at[c * (steps - 1) + p]
         )
 
     units = []
@@ -206,7 +209,7 @@
             query_grads.append(
                 lax.dot_general(dscore, keys[c], CONTRACT_FIRST, preferred_element_type=F32)
             )
-        for first, query_grad in zip(firsts, query_grads):
+        for c, (first, query_grad) in enumerate(zip(firsts, query_grads)):
             for i, cols in enumerate(head_slices(first, width)):
                 unit, inverse = unit_rows(raw_query_ref[:, cols])
                 raw_grad, term = norm_rope_back(
@@ -215,10 +218,14 @@
                 )
                 query_out[:, cols] = raw_grad
                 query_terms[...] += fold(term)
-            query_copy(first).start()
+
+            @pl.when(p < steps - 1)
+            def _(c=c):
+                query_copy(c, p).start()
+
         return 0
 
-    lax.fori_loop(0, group // HEADS_AT_ONCE, some_heads, 0, unroll=UNROLL)
+    lax.fori_loop(0, steps, some_heads, 0, unroll=UNROLL)
     for c in range(kv_heads):
         own_cols = slice(c * width, (c + 1) * width)
         unit, inverse = unit_rows(raw_key_ref[:, own_cols])
@@ -228,12 +235,9 @@
         key_out[:, own_cols] = raw_grad
         value_out[:, own_cols] = value_sum[c, prefix:, :]
         key_terms[...] += fold(term)
-    last_copies = [
-        pltpu.make_async_copy(key_out, key_hbm, sems.at[kv_heads * group // HEADS_AT_ONCE]),
-        pltpu.make_async_copy(value_out, value_hbm, sems.at[kv_heads * group // HEADS_AT_ONCE + 1]),
-    ]
-    for copy in last_copies:
-        copy.start()
+    for c in range(kv_heads):
+        cols = slice(((c + 1) * steps - 1) * step_cols, (c + 1) * steps * step_cols)
+        last_out[:, c * step_cols : (c + 1) * step_cols] = query_out[:, cols]
     for c in range(kv_heads):
         raw_grad, term = norm_rope_back(
             key_sum[c, :prefix, :], *units[c], key_gain, pre_cos * scale, pre_sin * scale
@@ -251,8 +255,9 @@
     pair = jnp.concatenate([rows, rows], axis=0).astype(BF16)
     for i in range(responses // 2):
         blocks_out[2 * own * i : 2 * own * (i + 1), 2 * kv_cols :] = pair
-    for copy in [query_copy(h) for h in range(0, kv_heads * group, HEADS_AT_ONCE)] + last_copies:
-        copy.wait()
+    for c in range(kv_heads):
+        for p in range(steps - 1):
+            query_copy(c, p).wait()
 
 
 def advantages(tail, responses):
@@ -273,7 +278,7 @@
 
 
 def finish(
-    reward_ref, blocks_ref, query_ref, key_ref, value_ref,
+    reward_ref, blocks_ref, query_ref, last_ref, key_ref, value_ref,
     query_out, key_out, value_out, prefix_key_out, prefix_value_out, *, responses,
 ):
     own, kv_cols = prefix_key_out.shape
@@ -284,8 +289,15 @@
             block = blocks_ref[:, first + cols : first + cols + width].astype(F32)
             out[:, cols : cols + width] = jnp.sum(block.reshape(weights.shape) * weights, axis=0)
     weight = (reward_ref[0, 0] - mean)[:, :1]
-    for source, out in ((query_ref, query_out), (key_ref, key_out), (value_ref, value_out)):
+    for source, out in ((key_ref, key_out), (value_ref, value_out)):
         out[...] = (source[...] * weight).astype(BF16)
+    kv_heads = kv_cols // width
+    early, late = query_ref.shape[1] // kv_heads, last_ref.shape[1] // kv_heads
+    for c in range(kv_heads):
+        first = c * (early + late)
+        for source, begin, cols in ((query_ref, first, early), (last_ref, first + early, late)):
+            grad = source[:, c * cols : (c + 1) * cols]
+            query_out[:, begin : begin + cols] = (grad * weight).astype(BF16)
 
 
 def local(
@@ -330,16 +342,18 @@
         ),
         name="prepare",
     )(prompt_len, query, key, *gains, table)
+    last_cols = kv_heads * HEADS_AT_ONCE * width
     *grads, blocks = pl.pallas_call(
         functools.partial(attend, responses=responses),
         out_shape=(
-            pltpu.HBM(query.shape, F32),
-            pltpu.HBM(key.shape, F32),
-            pltpu.HBM(key.shape, F32),
+            pltpu.HBM((length, query.shape[1] - last_cols), F32),
+            pltpu.VMEM((length, last_cols), F32),
+            pltpu.VMEM(key.shape, F32),
+            pltpu.VMEM(key.shape, F32),
             pltpu.VMEM((prefix, slot_cols), BF16),
         ),
         in_specs=[SMEM] * 3 + [VMEM] * 8,
-        out_specs=(pl.BlockSpec(memory_space=pltpu.HBM),) * 3 + (VMEM,),
+        out_specs=(pl.BlockSpec(memory_space=pltpu.HBM),) + (VMEM,) * 4,
         scratch_shapes=[
             pltpu.VMEM((kv_heads, prefix + length, width), BF16),
             pltpu.VMEM((kv_heads, prefix + length, width), BF16),
@@ -348,9 +362,7 @@
             pltpu.VMEM((8, width), F32),
             pltpu.VMEM((8, width), F32),
             pltpu.VMEM(query.shape, F32),
-            pltpu.VMEM(key.shape, F32),
-            pltpu.VMEM(key.shape, F32),
-            pltpu.SemaphoreType.DMA((query_heads // HEADS_AT_ONCE + 2,)),
+            pltpu.SemaphoreType.DMA((query_heads // HEADS_AT_ONCE - kv_heads,)),
         ],
         compiler_params=pltpu.CompilerParams(vmem_limit_bytes=16 * 2**20),
         name="attend",
@@ -380,7 +392,7 @@
             shape((own, kv_cols), F32),
             shape((own, kv_cols), F32),
         ),
-        in_specs=[SMEM] + [VMEM] * 4,
+        in_specs=[SMEM] + [VMEM] * 5,
         out_specs=(VMEM,) * 5,
         cost_estimate=pl.CostEstimate(
             flops=10_000_000, bytes_accessed=4_000_000, transcendentals=0

time: 70.5 us -> 70 us (level)
  no operation moved by 1% of the time
where the time goes in v5:
time: 70 us; the launch traced here: 69.6 us
  starting transfers between devices  23.9 us (34%)
  blocking collectives  19.7 us (28%)
  Pallas kernels  11.6 us (17%)
  waiting for transfers between devices  11.1 us (16%)
  between operations  2.66 us (4%)
    all_to_all x1, blocking collectives, local(): lax.all_to_all(blocks.reshape(responses, own, slot_cols), 'resp', 0, 0)  19.7 us
    all_to_all x1, starting transfers between devices, local(): lax.all_to_all(slots.reshape(responses, own, 2 * kv_cols), 'resp', 0, 0)  16.6 us
    all_to_all x1, waiting for transfers between devices, local(): lax.all_to_all(slots.reshape(responses, own, 2 * kv_cols), 'resp', 0, 0)  7.61 us
    all_to_all x1, starting transfers between devices, local(): lax.all_to_all(gain_slots.reshape(others, 2, width), ('dp', 'tensor'), 0, 0)  7.26 us
    pallas_call x1, Pallas kernels, local(): pl.pallas_call(functools.partial(attend, responses=responses), out_shape=...  4.34 us
    all_to_all x1, waiting for transfers between devices, local(): lax.all_to_all(gain_slots.reshape(others, 2, width), ('dp', 'tensor'), 0, 0)  3.52 us
    pallas_call x1, Pallas kernels, local(): pl.pallas_call(prepare, out_shape=(pltpu.VMEM((query_heads * length, widt...  2.89 us
    pallas_call x1, Pallas kernels, local(): pl.pallas_call(functools.partial(finish, responses=responses), out_shape=...  2.26 us
  transfers between devices with their start and end apart: 2, of which 2 were waited for; matrix products, arithmetic and copies ran while one was open for 0% of the time, Pallas kernels for 7%

profile of v5, /device:TPU:1, one launch (start us, length us, event | category | flops | bytes accessed | tf_op | source)
XLA Modules:
  0.0 69.6 jit_solution(14876930306622218149)
XLA Ops:
  0.6 1.4 %send_prompt.1 = bf16[256,512]{1,0:T(8,128)(2,1)} custom-call(bf16[8,256]{1,0:T(8,128)(2,1)} %bitcast.32, bf16[8,256]{1,0:T(8,128)(2,1)} %bitcast.33), custom_call_target="tpu_custom_call" | custom-call | tf_op jit(solution)/shard_map/send_prompt/pallas_call | solution.py:323
  2.1 0.0 copy-start
  2.1 0.0 copy-start.1
  2.1 16.6 %all-to-all-start = ((bf16[32,8,512]{2,1,0:T(8,128)(2,1)}), bf16[32,8,512]{2,1,0:T(8,128)(2,1)S(1)}, u32[]{:S(2)}, u32[]{:S(2)}) async-start(bf16[32,8,512]{2,1,0:T(8,128)(2,1)} %bitcast.2), calls=%async_computation | async-start | bytes 524288 | tf_op jit(solution)/shard_map/all_to_all | solution.py:330
  20.7 0.0 copy-start.3
  20.7 0.0 copy-start.6
  20.7 2.9 %prepare.1 = (bf16[2048,128]{1,0:T(8,128)(2,1)S(1)}, bf16[256,128]{1,0:T(8,128)(2,1)S(1)}, f32[88,128]{1,0:T(8,128)S(1)}) custom-call(s32[1]{0:T(128)S(6)} %copy.21.prompt_len_ref, bf16[128,2048]{1,0:T(8,128)(2,1)} %bitcast.24, bf16[128,256]{1,0:T(8,128)(2,1)} %bitcast.29, f32[1,128]{1,0:T(1,128)} %bitcast.34, f32[1,128]{1,0:T(1,128)} %bitcast.35, ...), custom_call_target="tpu_custom_call" | custom-call | flops 100000000 | bytes 4000000 | tf_op jit(solution)/shard_map/prepare/pallas_call | solution.py:331
  23.6 7.6 %all-to-all-done = bf16[32,8,512]{2,1,0:T(8,128)(2,1)S(1)} async-done(((bf16[32,8,512]{2,1,0:T(8,128)(2,1)}), bf16[32,8,512]{2,1,0:T(8,128)(2,1)S(1)}, u32[]{:S(2)}, u32[]{:S(2)}) %all-to-all-start) | async-done | bytes 262176 | tf_op jit(solution)/shard_map/all_to_all | solution.py:330
  31.2 0.0 copy-done
  31.2 0.0 copy-done.1
  31.2 0.0 copy-done.3
  31.2 0.0 copy-done.6
  31.2 4.3 %attend.1 = (f32[128,1536]{1,0:T(8,128)}, f32[128,512]{1,0:T(8,128)S(1)}, f32[128,256]{1,0:T(8,128)S(1)}, f32[128,256]{1,0:T(8,128)S(1)}, bf16[256,640]{1,0:T(8,128)(2,1)S(1)}) custom-call(f32[1,1]{1,0:T(1,128)S(6)} %copy.19.reward_ref, s32[1,1]{1,0:T(1,128)S(6)} %copy.20.resp_len_ref, s32[1]{0:T(128)S(6)} %copy.21.prompt_len_ref, ...), custom_call_target="tpu_custom_call" | custom-call | tf_op jit(solution)/shard_map/attend/pallas_call | solution.py:346
  35.6 0.0 copy-start.2
  35.6 0.0 copy-start.4
  35.6 0.0 copy-start.5
  35.6 19.7 %all_to_all.15 = bf16[32,8,640]{2,1,0:T(8,128)(2,1)S(1)} all-to-all(bf16[32,8,640]{2,1,0:T(8,128)(2,1)S(1)} %bitcast.28), channel_id=1, replica_groups=mesh['dp'=8,'resp'=32,'tensor'=2] {'resp'}, dimensions={0} | all-to-all | bytes 655360 | tf_op jit(solution)/shard_map/all_to_all | solution.py:373
  55.3 0.0 copy-done.2
  55.3 0.0 copy-done.4
  55.3 0.0 copy-done.5
  55.3 0.7 weigh.1
  56.0 7.3 %all-to-all-start.2 = ((f32[16,2,128]{2,1,0:T(2,128)}), f32[16,2,128]{2,1,0:T(2,128)S(1)}, u32[]{:S(2)}, u32[]{:S(2)}) async-start(f32[16,2,128]{2,1,0:T(2,128)} %bitcast.17), calls=%async_computation.2 | async-start | bytes 32768 | tf_op jit(solution)/shard_map/all_to_all | solution.py:385
  63.3 2.3 %finish.1 = (bf16[128,2048]{1,0:T(8,128)(2,1)}, bf16[128,256]{1,0:T(8,128)(2,1)}, bf16[128,256]{1,0:T(8,128)(2,1)}, f32[8,256]{1,0:T(8,128)}, f32[8,256]{1,0:T(8,128)}) custom-call(f32[1,1]{1,0:T(1,128)S(6)} %copy.19.reward_ref, bf16[256,640]{1,0:T(8,128)(2,1)S(1)} %bitcast.23, f32[128,1536]{1,0:T(8,128)} %get-tuple-element.24.query_ref, ...), custom_call_target="tpu_custom_call" | custom-call | flops 10000000 | bytes 4000000 | tf_op jit(solution)/shard_map/finish/pallas_call | solution.py:386
  65.5 3.5 %all-to-all-done.2 = f32[16,2,128]{2,1,0:T(2,128)S(1)} async-done(((f32[16,2,128]{2,1,0:T(2,128)}), f32[16,2,128]{2,1,0:T(2,128)S(1)}, u32[]{:S(2)}, u32[]{:S(2)}) %all-to-all-start.2) | async-done | bytes 16416 | tf_op jit(solution)/shard_map/all_to_all | solution.py:385
  69.1 0.5 slice_bitcast_fusion
  (2 shorter events, 0.0 us)
Async XLA Ops:
  2.1 29.1 %copy-start = (bf16[1,1,128,2048]{3,2,1,0:T(8,128)(2,1)S(1)}, bf16[1,1,128,2048]{3,2,1,0:T(8,128)(2,1)}, u32[]{:S(2)}) copy-start(bf16[1,1,128,2048]{3,2,1,0:T(8,128)(2,1)} %param.12) | copy-start | bytes 1572868
  2.1 29.1 %copy-start.1 = (bf16[1,1,128,2048]{3,2,1,0:T(8,128)(2,1)S(1)}, bf16[1,1,128,2048]{3,2,1,0:T(8,128)(2,1)}, u32[]{:S(2)}) copy-start(bf16[1,1,128,2048]{3,2,1,0:T(8,128)(2,1)} %param.19) | copy-start | bytes 1572868
  2.1 29.1 %all-to-all-start = ((bf16[32,8,512]{2,1,0:T(8,128)(2,1)}), bf16[32,8,512]{2,1,0:T(8,128)(2,1)S(1)}, u32[]{:S(2)}, u32[]{:S(2)}) async-start(bf16[32,8,512]{2,1,0:T(8,128)(2,1)} %bitcast.2), calls=%async_computation | async-start | bytes 524288 | tf_op jit(solution)/shard_map/all_to_all | solution.py:330
  20.7 10.5 %copy-start.3 = (bf16[1,1,128,256]{3,2,1,0:T(8,128)(2,1)S(1)}, bf16[1,1,128,256]{3,2,1,0:T(8,128)(2,1)}, u32[]{:S(2)}) copy-start(bf16[1,1,128,256]{3,2,1,0:T(8,128)(2,1)} %param.13) | copy-start | bytes 196612
  20.7 10.5 %copy-start.6 = (bf16[1,1,128,256]{3,2,1,0:T(8,128)(2,1)S(1)}, bf16[1,1,128,256]{3,2,1,0:T(8,128)(2,1)}, u32[]{:S(2)}) copy-start(bf16[1,1,128,256]{3,2,1,0:T(8,128)(2,1)} %param.14) | copy-start | bytes 196612
  35.6 19.7 %copy-start.2 = (f32[128,512]{1,0:T(8,128)}, f32[128,512]{1,0:T(8,128)S(1)}, u32[]{:S(2)}) copy-start(f32[128,512]{1,0:T(8,128)S(1)} %get-tuple-element.25.last_ref) | copy-start | bytes 786436
  35.6 19.7 %copy-start.4 = (f32[128,256]{1,0:T(8,128)}, f32[128,256]{1,0:T(8,128)S(1)}, u32[]{:S(2)}) copy-start(f32[128,256]{1,0:T(8,128)S(1)} %get-tuple-element.26.key_ref) | copy-start | bytes 393220
  35.6 19.7 %copy-start.5 = (f32[128,256]{1,0:T(8,128)}, f32[128,256]{1,0:T(8,128)S(1)}, u32[]{:S(2)}) copy-start(f32[128,256]{1,0:T(8,128)S(1)} %get-tuple-element.27.value_ref) | copy-start | bytes 393220
  56.0 13.0 %all-to-all-start.2 = ((f32[16,2,128]{2,1,0:T(2,128)}), f32[16,2,128]{2,1,0:T(2,128)S(1)}, u32[]{:S(2)}, u32[]{:S(2)}) async-start(f32[16,2,128]{2,1,0:T(2,128)} %bitcast.17), calls=%async_computation.2 | async-start | bytes 32768 | tf_op jit(solution)/shard_map/all_to_all | solution.py:385

commit v6 on v5

--- a/solution.py
+++ b/solution.py
@@ -70,11 +70,19 @@
     return (normed * cos + half_turn(normed) * sin).astype(BF16)
 
 
+def rope_back(grad, cos, sin):
+    return grad * cos - half_turn(grad) * sin
+
+
+def norm_back(normed_grad, term, unit, inverse, gain):
+    mean = jnp.mean(term * gain, axis=1, keepdims=True)
+    return inverse * (normed_grad * gain - unit * mean)
+
+
 def norm_rope_back(grad, unit, inverse, gain, cos, sin):
-    normed_grad = grad * cos - half_turn(grad) * sin
+    normed_grad = rope_back(grad, cos, sin)
     term = normed_grad * unit
-    mean = jnp.mean(term * gain, axis=1, keepdims=True)
-    return inverse * (normed_grad * gain - unit * mean), term
+    return norm_back(normed_grad, term, unit, inverse, gain), term
 
 
 def fold(rows):
@@ -105,7 +113,7 @@
 
 def prepare(
     prompt_len_ref, query_ref, key_ref, query_gain_ref, key_gain_ref, table_ref,
-    query_out, key_out, shared_out,
+    query_out, key_out, unit_out, shared_out,
 ):
     length, width = query_ref.shape[0], query_gain_ref.shape[1]
     cos, sin = rope_at(table_ref, prompt_len_ref[0], length)
@@ -120,8 +128,11 @@
         gain = gain_ref[...]
 
         def one(h, _, source=source, gain=gain, out=out):
-            raw = source[:, pl.ds(pl.multiple_of(h * width, width), width)]
-            rows = rotated(unit_rows(raw)[0], gain, cos, sin)
+            cols = pl.ds(pl.multiple_of(h * width, width), width)
+            unit = unit_rows(source[:, cols])[0]
+            if out is query_out:
+                unit_out[:, cols] = unit.astype(BF16)
+            rows = rotated(unit, gain, cos, sin)
             out[pl.ds(pl.multiple_of(h * length, length), length), :] = rows
             return 0
 
@@ -130,7 +141,7 @@
 
 def attend(
     reward_ref, resp_len_ref, prompt_len_ref,
-    arrived_ref, query_ref, key_ref, shared_ref, raw_query_ref, raw_key_ref, value_ref, grad_ref,
+    arrived_ref, query_ref, key_ref, unit_ref, shared_ref, raw_key_ref, value_ref, grad_ref,
     query_hbm, last_out, key_out, value_out, blocks_out,
     keys, values, key_sum, value_sum, query_terms, key_terms, query_out, sems, *, responses,
 ):
@@ -144,7 +155,7 @@
     scale = width**-0.5
     start = prompt_len_ref[0]
     table_ref = shared_ref.at[: shared_ref.shape[0] - 8]
-    query_gain, key_gain = (shared_ref[pl.ds(shared_ref.shape[0] - 8 + i, 1), :] for i in range(2))
+    key_gain = shared_ref[pl.ds(shared_ref.shape[0] - 7, 1), :]
     back_cos, back_sin = (t * scale for t in rope_at(table_ref, start, length))
     pre_cos, pre_sin = rope_at(table_ref, 0, prefix)
 
@@ -211,13 +222,11 @@
             )
         for c, (first, query_grad) in enumerate(zip(firsts, query_grads)):
             for i, cols in enumerate(head_slices(first, width)):
-                unit, inverse = unit_rows(raw_query_ref[:, cols])
-                raw_grad, term = norm_rope_back(
-                    query_grad[i * length : (i + 1) * length], unit, inverse, query_gain,
-                    back_cos, back_sin,
+                normed_grad = rope_back(
+                    query_grad[i * length : (i + 1) * length], back_cos, back_sin
                 )
-                query_out[:, cols] = raw_grad
-                query_terms[...] += fold(term)
+                query_out[:, cols] = normed_grad
+                query_terms[...] += fold(normed_grad * unit_ref[:, cols].astype(F32))
 
             @pl.when(p < steps - 1)
             def _(c=c):
@@ -278,7 +287,7 @@
 
 
 def finish(
-    reward_ref, blocks_ref, query_ref, last_ref, key_ref, value_ref,
+    reward_ref, blocks_ref, raw_query_ref, query_gain_ref, query_ref, last_ref, key_ref, value_ref,
     query_out, key_out, value_out, prefix_key_out, prefix_value_out, *, responses,
 ):
     own, kv_cols = prefix_key_out.shape
@@ -296,8 +305,18 @@
     for c in range(kv_heads):
         first = c * (early + late)
         for source, begin, cols in ((query_ref, first, early), (last_ref, first + early, late)):
-            grad = source[:, c * cols : (c + 1) * cols]
-            query_out[:, begin : begin + cols] = (grad * weight).astype(BF16)
+
+            def one(h, _, source=source, begin=begin, skip=c * cols):
+                at = [pl.ds(pl.multiple_of(x + h * width, width), width) for x in (begin, skip)]
+                normed_grad = source[:, at[1]]
+                unit, inverse = unit_rows(raw_query_ref[:, at[0]])
+                grad = norm_back(
+                    normed_grad, normed_grad * unit, unit, inverse, query_gain_ref[...]
+                )
+                query_out[:, at[0]] = (grad * weight).astype(BF16)
+                return 0
+
+            lax.fori_loop(0, cols // width, one, 0, unroll=2)
 
 
 def local(
@@ -333,10 +352,11 @@
         out_shape=(
             pltpu.VMEM((query_heads * length, width), BF16),
             pltpu.VMEM((kv_heads * length, width), BF16),
+            pltpu.VMEM(query.shape, BF16),
             pltpu.VMEM((table.shape[0] + 8, width), F32),
         ),
         in_specs=[SMEM] + [VMEM] * 5,
-        out_specs=(VMEM,) * 3,
+        out_specs=(VMEM,) * 4,
         cost_estimate=pl.CostEstimate(
             flops=100_000_000, bytes_accessed=4_000_000, transcendentals=0
         ),
@@ -368,7 +388,7 @@
         name="attend",
     )(
         rewards, resp_len, prompt_len, arrived.reshape(prefix, 2 * kv_cols), *prepared,
-        query, key, value, grad,
+        key, value, grad,
     )
     received = lax.all_to_all(blocks.reshape(responses, own, slot_cols), "resp", 0, 0)
     received = pltpu.with_memory_space_constraint(
@@ -392,13 +412,13 @@
             shape((own, kv_cols), F32),
             shape((own, kv_cols), F32),
         ),
-        in_specs=[SMEM] + [VMEM] * 5,
+        in_specs=[SMEM] + [VMEM] * 7,
         out_specs=(VMEM,) * 5,
         cost_estimate=pl.CostEstimate(
             flops=10_000_000, bytes_accessed=4_000_000, transcendentals=0
         ),
         name="finish",
-    )(rewards, received, *grads)
+    )(rewards, received, query, gains[0], *grads)
     totals = jnp.sum(gain_slots, axis=0) / (lax.axis_size("dp") * responses)
     return (
         grad_query[None, None],

time: 70 us -> 69.7 us (level)
  waiting for transfers between devices: 11.1 us -> 9.42 us
  Pallas kernels: 11.6 us -> 13 us
    pallas_call x1, Pallas kernels: 2.26 us -> 3.98 us  [local(): pl.pallas_call(functools.partial(finish, responses=responses), out_shape=...]
    all_to_all x1, waiting for transfers between devices: 3.52 us -> 1.81 us  [local(): lax.all_to_all(gain_slots.reshape(others, 2, width), ('dp', 'tensor'), 0, 0)]
  transfers between devices with their start and end apart: 2 -> 2, of which waited for: 2 -> 2; matrix products, arithmetic and copies ran while one was open for 0% -> 0% of each run, Pallas kernels for 7% -> 10%
where the time goes in v6:
time: 69.7 us; the launch traced here: 69.3 us
  starting transfers between devices  23.9 us (34%)
  blocking collectives  19.7 us (28%)
  Pallas kernels  13 us (19%)
  waiting for transfers between devices  9.42 us (14%)
  between operations  2.65 us (4%)
    all_to_all x1, blocking collectives, local(): lax.all_to_all(blocks.reshape(responses, own, slot_cols), 'resp', 0, 0)  19.7 us
    all_to_all x1, starting transfers between devices, local(): lax.all_to_all(slots.reshape(responses, own, 2 * kv_cols), 'resp', 0, 0)  16.6 us
    all_to_all x1, waiting for transfers between devices, local(): lax.all_to_all(slots.reshape(responses, own, 2 * kv_cols), 'resp', 0, 0)  7.62 us
    all_to_all x1, starting transfers between devices, local(): lax.all_to_all(gain_slots.reshape(others, 2, width), ('dp', 'tensor'), 0, 0)  7.27 us
    pallas_call x1, Pallas kernels, local(): pl.pallas_call(functools.partial(attend, responses=responses), out_shape=...  4.06 us
    pallas_call x1, Pallas kernels, local(): pl.pallas_call(functools.partial(finish, responses=responses), out_shape=...  3.98 us
    pallas_call x1, Pallas kernels, local(): pl.pallas_call(prepare, out_shape=(pltpu.VMEM((query_heads * length, widt...  2.89 us
    all_to_all x1, waiting for transfers between devices, local(): lax.all_to_all(gain_slots.reshape(others, 2, width), ('dp', 'tensor'), 0, 0)  1.81 us
  transfers between devices with their start and end apart: 2, of which 2 were waited for; matrix products, arithmetic and copies ran while one was open for 0% of the time, Pallas kernels for 10%

profile of v6, /device:TPU:1, one launch (start us, length us, event | category | flops | bytes accessed | tf_op | source)
XLA Modules:
  0.0 69.3 jit_solution(17635404038196680732)
XLA Ops:
  0.6 1.4 %send_prompt.1 = bf16[256,512]{1,0:T(8,128)(2,1)} custom-call(bf16[8,256]{1,0:T(8,128)(2,1)} %bitcast.32, bf16[8,256]{1,0:T(8,128)(2,1)} %bitcast.33), custom_call_target="tpu_custom_call" | custom-call | tf_op jit(solution)/shard_map/send_prompt/pallas_call | solution.py:342
  2.1 0.0 copy-start
  2.1 16.6 %all-to-all-start = ((bf16[32,8,512]{2,1,0:T(8,128)(2,1)}), bf16[32,8,512]{2,1,0:T(8,128)(2,1)S(1)}, u32[]{:S(2)}, u32[]{:S(2)}) async-start(bf16[32,8,512]{2,1,0:T(8,128)(2,1)} %bitcast.2), calls=%async_computation | async-start | bytes 524288 | tf_op jit(solution)/shard_map/all_to_all | solution.py:349
  20.7 0.0 copy-start.1
  20.7 0.0 copy-start.5
  20.7 2.9 %prepare.1 = (bf16[2048,128]{1,0:T(8,128)(2,1)S(1)}, bf16[256,128]{1,0:T(8,128)(2,1)S(1)}, bf16[128,2048]{1,0:T(8,128)(2,1)S(1)}, f32[88,128]{1,0:T(8,128)S(1)}) custom-call(s32[1]{0:T(128)S(6)} %copy.21.prompt_len_ref, bf16[128,2048]{1,0:T(8,128)(2,1)} %bitcast.30, bf16[128,256]{1,0:T(8,128)(2,1)} %bitcast.27, f32[1,128]{1,0:T(1,128)} %bitcast.34, ...), custom_call_target="tpu_custom_call" | custom-call | flops 100000000 | bytes 4000000 | tf_op jit(solution)/shard_map/prepare/pallas_call | solution.py:350
  23.6 7.6 %all-to-all-done = bf16[32,8,512]{2,1,0:T(8,128)(2,1)S(1)} async-done(((bf16[32,8,512]{2,1,0:T(8,128)(2,1)}), bf16[32,8,512]{2,1,0:T(8,128)(2,1)S(1)}, u32[]{:S(2)}, u32[]{:S(2)}) %all-to-all-start) | async-done | bytes 262176 | tf_op jit(solution)/shard_map/all_to_all | solution.py:349
  31.2 0.0 copy-done
  31.2 0.0 copy-done.1
  31.2 0.0 copy-done.5
  31.2 4.1 %attend.1 = (f32[128,1536]{1,0:T(8,128)}, f32[128,512]{1,0:T(8,128)S(1)}, f32[128,256]{1,0:T(8,128)S(1)}, f32[128,256]{1,0:T(8,128)S(1)}, bf16[256,640]{1,0:T(8,128)(2,1)S(1)}) custom-call(f32[1,1]{1,0:T(1,128)S(6)} %copy.19.reward_ref, s32[1,1]{1,0:T(1,128)S(6)} %copy.20.resp_len_ref, s32[1]{0:T(128)S(6)} %copy.21.prompt_len_ref, ...), custom_call_target="tpu_custom_call" | custom-call | tf_op jit(solution)/shard_map/attend/pallas_call | solution.py:366
  35.3 0.0 copy-start.2
  35.3 0.0 copy-start.3
  35.3 0.0 copy-start.4
  35.3 19.7 %all_to_all.15 = bf16[32,8,640]{2,1,0:T(8,128)(2,1)S(1)} all-to-all(bf16[32,8,640]{2,1,0:T(8,128)(2,1)S(1)} %bitcast.26), channel_id=1, replica_groups=mesh['dp'=8,'resp'=32,'tensor'=2] {'resp'}, dimensions={0} | all-to-all | bytes 655360 | tf_op jit(solution)/shard_map/all_to_all | solution.py:393
  55.0 0.0 copy-done.2
  55.0 0.0 copy-done.3
  55.0 0.0 copy-done.4
  55.0 0.7 weigh.1
  55.7 7.3 %all-to-all-start.2 = ((f32[16,2,128]{2,1,0:T(2,128)}), f32[16,2,128]{2,1,0:T(2,128)S(1)}, u32[]{:S(2)}, u32[]{:S(2)}) async-start(f32[16,2,128]{2,1,0:T(2,128)} %bitcast.17), calls=%async_computation.2 | async-start | bytes 32768 | tf_op jit(solution)/shard_map/all_to_all | solution.py:405
  63.0 4.0 %finish.1 = (bf16[128,2048]{1,0:T(8,128)(2,1)}, bf16[128,256]{1,0:T(8,128)(2,1)}, bf16[128,256]{1,0:T(8,128)(2,1)}, f32[8,256]{1,0:T(8,128)}, f32[8,256]{1,0:T(8,128)}) custom-call(f32[1,1]{1,0:T(1,128)S(6)} %copy.19.reward_ref, bf16[256,640]{1,0:T(8,128)(2,1)S(1)} %bitcast.23, bf16[128,2048]{1,0:T(8,128)(2,1)} %bitcast.31, f32[1,128]{1,0:T(1,128)} %bitcast.35, ...), custom_call_target="tpu_custom_call" | custom-call | flops 10000000 | bytes 4000000 | tf_op jit(solution)/shard_map/finish/pallas_call | solution.py:406
  66.9 1.8 %all-to-all-done.2 = f32[16,2,128]{2,1,0:T(2,128)S(1)} async-done(((f32[16,2,128]{2,1,0:T(2,128)}), f32[16,2,128]{2,1,0:T(2,128)S(1)}, u32[]{:S(2)}, u32[]{:S(2)}) %all-to-all-start.2) | async-done | bytes 16416 | tf_op jit(solution)/shard_map/all_to_all | solution.py:405
  68.8 0.5 slice_bitcast_fusion
  (2 shorter events, 0.0 us)
Async XLA Ops:
  2.1 29.1 %copy-start = (bf16[1,1,128,2048]{3,2,1,0:T(8,128)(2,1)S(1)}, bf16[1,1,128,2048]{3,2,1,0:T(8,128)(2,1)}, u32[]{:S(2)}) copy-start(bf16[1,1,128,2048]{3,2,1,0:T(8,128)(2,1)} %param.19) | copy-start | bytes 1572868
  2.1 29.1 %all-to-all-start = ((bf16[32,8,512]{2,1,0:T(8,128)(2,1)}), bf16[32,8,512]{2,1,0:T(8,128)(2,1)S(1)}, u32[]{:S(2)}, u32[]{:S(2)}) async-start(bf16[32,8,512]{2,1,0:T(8,128)(2,1)} %bitcast.2), calls=%async_computation | async-start | bytes 524288 | tf_op jit(solution)/shard_map/all_to_all | solution.py:349
  20.7 10.5 %copy-start.1 = (bf16[1,1,128,256]{3,2,1,0:T(8,128)(2,1)S(1)}, bf16[1,1,128,256]{3,2,1,0:T(8,128)(2,1)}, u32[]{:S(2)}) copy-start(bf16[1,1,128,256]{3,2,1,0:T(8,128)(2,1)} %param.13) | copy-start | bytes 196612
  20.7 10.5 %copy-start.5 = (bf16[1,1,128,256]{3,2,1,0:T(8,128)(2,1)S(1)}, bf16[1,1,128,256]{3,2,1,0:T(8,128)(2,1)}, u32[]{:S(2)}) copy-start(bf16[1,1,128,256]{3,2,1,0:T(8,128)(2,1)} %param.14) | copy-start | bytes 196612
  35.3 19.7 %copy-start.2 = (f32[128,512]{1,0:T(8,128)}, f32[128,512]{1,0:T(8,128)S(1)}, u32[]{:S(2)}) copy-start(f32[128,512]{1,0:T(8,128)S(1)} %get-tuple-element.27.last_ref) | copy-start | bytes 786436
  35.3 19.7 %copy-start.3 = (f32[128,256]{1,0:T(8,128)}, f32[128,256]{1,0:T(8,128)S(1)}, u32[]{:S(2)}) copy-start(f32[128,256]{1,0:T(8,128)S(1)} %get-tuple-element.28.key_ref) | copy-start | bytes 393220
  35.3 19.7 %copy-start.4 = (f32[128,256]{1,0:T(8,128)}, f32[128,256]{1,0:T(8,128)S(1)}, u32[]{:S(2)}) copy-start(f32[128,256]{1,0:T(8,128)S(1)} %get-tuple-element.29.value_ref) | copy-start | bytes 393220
  55.7 13.1 %all-to-all-start.2 = ((f32[16,2,128]{2,1,0:T(2,128)}), f32[16,2,128]{2,1,0:T(2,128)S(1)}, u32[]{:S(2)}, u32[]{:S(2)}) async-start(f32[16,2,128]{2,1,0:T(2,128)} %bitcast.17), calls=%async_computation.2 | async-start | bytes 32768 | tf_op jit(solution)/shard_map/all_to_all | solution.py:405

commit v7 on v6

--- a/solution.py
+++ b/solution.py
@@ -160,7 +160,7 @@
     pre_cos, pre_sin = rope_at(table_ref, 0, prefix)
 
     valid = lax.broadcasted_iota(jnp.int32, (1, count), 1) % length < resp_len_ref[0, 0]
-    visible = lax.broadcasted_iota(jnp.int32, (prefix, count), 0) < start
+    visible = (lax.broadcasted_iota(jnp.int32, (prefix, 1), 0) < start).astype(F32)
     causal = lax.broadcasted_iota(jnp.int32, (length, count), 0) <= (
         lax.broadcasted_iota(jnp.int32, (length, count), 1) % length
     )
@@ -201,7 +201,7 @@
     def softmax(score, dprob):
         expo = jnp.exp2(score * (scale * LOG2_E))
         expo = jnp.concatenate(
-            [jnp.where(visible, expo[:prefix], 0.0), jnp.where(causal, expo[prefix:], 0.0)], axis=0
+            [expo[:prefix] * visible, jnp.where(causal, expo[prefix:], 0.0)], axis=0
         )
         inverse_sum = 1.0 / jnp.sum(expo, axis=0, keepdims=True)
         delta = jnp.sum(expo * dprob, axis=0, keepdims=True) * inverse_sum
@@ -237,13 +237,10 @@
     lax.fori_loop(0, steps, some_heads, 0, unroll=UNROLL)
     for c in range(kv_heads):
         own_cols = slice(c * width, (c + 1) * width)
-        unit, inverse = unit_rows(raw_key_ref[:, own_cols])
-        raw_grad, term = norm_rope_back(
-            key_sum[c, prefix:, :], unit, inverse, key_gain, back_cos, back_sin
-        )
-        key_out[:, own_cols] = raw_grad
+        normed_grad = rope_back(key_sum[c, prefix:, :], back_cos, back_sin)
+        key_out[:, own_cols] = normed_grad
         value_out[:, own_cols] = value_sum[c, prefix:, :]
-        key_terms[...] += fold(term)
+        key_terms[...] += fold(normed_grad * unit_rows(raw_key_ref[:, own_cols])[0])
     for c in range(kv_heads):
         cols = slice(((c + 1) * steps - 1) * step_cols, (c + 1) * steps * step_cols)
         last_out[:, c * step_cols : (c + 1) * step_cols] = query_out[:, cols]
@@ -287,7 +284,8 @@
 
 
 def finish(
-    reward_ref, blocks_ref, raw_query_ref, query_gain_ref, query_ref, last_ref, key_ref, value_ref,
+    reward_ref, blocks_ref, raw_query_ref, raw_key_ref, query_gain_ref, key_gain_ref,
+    query_ref, last_ref, key_ref, value_ref,
     query_out, key_out, value_out, prefix_key_out, prefix_value_out, *, responses,
 ):
     own, kv_cols = prefix_key_out.shape
@@ -298,8 +296,12 @@
             block = blocks_ref[:, first + cols : first + cols + width].astype(F32)
             out[:, cols : cols + width] = jnp.sum(block.reshape(weights.shape) * weights, axis=0)
     weight = (reward_ref[0, 0] - mean)[:, :1]
-    for source, out in ((key_ref, key_out), (value_ref, value_out)):
-        out[...] = (source[...] * weight).astype(BF16)
+    value_out[...] = (value_ref[...] * weight).astype(BF16)
+    for cols in range(0, kv_cols, width):
+        normed_grad = key_ref[:, cols : cols + width]
+        unit, inverse = unit_rows(raw_key_ref[:, cols : cols + width])
+        grad = norm_back(normed_grad, normed_grad * unit, unit, inverse, key_gain_ref[...])
+        key_out[:, cols : cols + width] = (grad * weight).astype(BF16)
     kv_heads = kv_cols // width
     early, late = query_ref.shape[1] // kv_heads, last_ref.shape[1] // kv_heads
     for c in range(kv_heads):
@@ -412,13 +414,13 @@
             shape((own, kv_cols), F32),
             shape((own, kv_cols), F32),
         ),
-        in_specs=[SMEM] + [VMEM] * 7,
+        in_specs=[SMEM] + [VMEM] * 9,
         out_specs=(VMEM,) * 5,
         cost_estimate=pl.CostEstimate(
             flops=10_000_000, bytes_accessed=4_000_000, transcendentals=0
         ),
         name="finish",
-    )(rewards, received, query, gains[0], *grads)
+    )(rewards, received, query, key, *gains, *grads)
     totals = jnp.sum(gain_slots, axis=0) / (lax.axis_size("dp") * responses)
     return (
         grad_query[None, None],

time: 69.7 us -> 69.6 us (level)
  no operation moved by 1% of the time
where the time goes in v7:
time: 69.6 us; the launch traced here: 69.3 us
  starting transfers between devices  23.9 us (34%)
  blocking collectives  19.7 us (28%)
  Pallas kernels  13.1 us (19%)
  waiting for transfers between devices  9.25 us (13%)
  between operations  2.65 us (4%)
    all_to_all x1, blocking collectives, local(): lax.all_to_all(blocks.reshape(responses, own, slot_cols), 'resp', 0, 0)  19.7 us
    all_to_all x1, starting transfers between devices, local(): lax.all_to_all(slots.reshape(responses, own, 2 * kv_cols), 'resp', 0, 0)  16.6 us
    all_to_all x1, waiting for transfers between devices, local(): lax.all_to_all(slots.reshape(responses, own, 2 * kv_cols), 'resp', 0, 0)  7.62 us
    all_to_all x1, starting transfers between devices, local(): lax.all_to_all(gain_slots.reshape(others, 2, width), ('dp', 'tensor'), 0, 0)  7.27 us
    pallas_call x1, Pallas kernels, local(): pl.pallas_call(functools.partial(finish, responses=responses), out_shape=...  4.15 us
    pallas_call x1, Pallas kernels, local(): pl.pallas_call(functools.partial(attend, responses=responses), out_shape=...  3.99 us
    pallas_call x1, Pallas kernels, local(): pl.pallas_call(prepare, out_shape=(pltpu.VMEM((query_heads * length, widt...  2.89 us
    all_to_all x1, waiting for transfers between devices, local(): lax.all_to_all(gain_slots.reshape(others, 2, width), ('dp', 'tensor'), 0, 0)  1.63 us
  transfers between devices with their start and end apart: 2, of which 2 were waited for; matrix products, arithmetic and copies ran while one was open for 0% of the time, Pallas kernels for 10%

profile of v7, /device:TPU:1, one launch (start us, length us, event | category | flops | bytes accessed | tf_op | source)
XLA Modules:
  0.0 69.3 jit_solution(16986873860793727186)
XLA Ops:
  0.6 1.4 %send_prompt.1 = bf16[256,512]{1,0:T(8,128)(2,1)} custom-call(bf16[8,256]{1,0:T(8,128)(2,1)} %bitcast.33, bf16[8,256]{1,0:T(8,128)(2,1)} %bitcast.34), custom_call_target="tpu_custom_call" | custom-call | tf_op jit(solution)/shard_map/send_prompt/pallas_call | solution.py:344
  2.1 0.0 copy-start.1
  2.1 16.6 %all-to-all-start = ((bf16[32,8,512]{2,1,0:T(8,128)(2,1)}), bf16[32,8,512]{2,1,0:T(8,128)(2,1)S(1)}, u32[]{:S(2)}, u32[]{:S(2)}) async-start(bf16[32,8,512]{2,1,0:T(8,128)(2,1)} %bitcast.2), calls=%async_computation | async-start | bytes 524288 | tf_op jit(solution)/shard_map/all_to_all | solution.py:351
  20.7 0.0 copy-start
  20.7 0.0 copy-start.5
  20.7 2.9 %prepare.1 = (bf16[2048,128]{1,0:T(8,128)(2,1)S(1)}, bf16[256,128]{1,0:T(8,128)(2,1)S(1)}, bf16[128,2048]{1,0:T(8,128)(2,1)S(1)}, f32[88,128]{1,0:T(8,128)S(1)}) custom-call(s32[1]{0:T(128)S(6)} %copy.21.prompt_len_ref, bf16[128,2048]{1,0:T(8,128)(2,1)} %bitcast.31, bf16[128,256]{1,0:T(8,128)(2,1)} %bitcast.25, f32[1,128]{1,0:T(1,128)} %bitcast.35, ...), custom_call_target="tpu_custom_call" | custom-call | flops 100000000 | bytes 4000000 | tf_op jit(solution)/shard_map/prepare/pallas_call | solution.py:352
  23.6 7.6 %all-to-all-done = bf16[32,8,512]{2,1,0:T(8,128)(2,1)S(1)} async-done(((bf16[32,8,512]{2,1,0:T(8,128)(2,1)}), bf16[32,8,512]{2,1,0:T(8,128)(2,1)S(1)}, u32[]{:S(2)}, u32[]{:S(2)}) %all-to-all-start) | async-done | bytes 262176 | tf_op jit(solution)/shard_map/all_to_all | solution.py:351
  31.2 0.0 copy-done.1
  31.2 0.0 copy-done
  31.2 0.0 copy-done.5
  31.2 4.0 %attend.1 = (f32[128,1536]{1,0:T(8,128)}, f32[128,512]{1,0:T(8,128)S(1)}, f32[128,256]{1,0:T(8,128)S(1)}, f32[128,256]{1,0:T(8,128)S(1)}, bf16[256,640]{1,0:T(8,128)(2,1)S(1)}) custom-call(f32[1,1]{1,0:T(1,128)S(6)} %copy.19.reward_ref, s32[1,1]{1,0:T(1,128)S(6)} %copy.20.resp_len_ref, s32[1]{0:T(128)S(6)} %copy.21.prompt_len_ref, ...), custom_call_target="tpu_custom_call" | custom-call | tf_op jit(solution)/shard_map/attend/pallas_call | solution.py:368
  35.2 0.0 copy-start.2
  35.2 0.0 copy-start.3
  35.2 0.0 copy-start.4
  35.2 19.7 %all_to_all.15 = bf16[32,8,640]{2,1,0:T(8,128)(2,1)S(1)} all-to-all(bf16[32,8,640]{2,1,0:T(8,128)(2,1)S(1)} %bitcast.29), channel_id=1, replica_groups=mesh['dp'=8,'resp'=32,'tensor'=2] {'resp'}, dimensions={0} | all-to-all | bytes 655360 | tf_op jit(solution)/shard_map/all_to_all | solution.py:395
  54.9 0.0 copy-done.2
  54.9 0.0 copy-done.3
  54.9 0.0 copy-done.4
  55.0 0.7 weigh.1
  55.6 7.3 %all-to-all-start.2 = ((f32[16,2,128]{2,1,0:T(2,128)}), f32[16,2,128]{2,1,0:T(2,128)S(1)}, u32[]{:S(2)}, u32[]{:S(2)}) async-start(f32[16,2,128]{2,1,0:T(2,128)} %bitcast.17), calls=%async_computation.2 | async-start | bytes 32768 | tf_op jit(solution)/shard_map/all_to_all | solution.py:407
  62.9 4.2 %finish.1 = (bf16[128,2048]{1,0:T(8,128)(2,1)}, bf16[128,256]{1,0:T(8,128)(2,1)}, bf16[128,256]{1,0:T(8,128)(2,1)}, f32[8,256]{1,0:T(8,128)}, f32[8,256]{1,0:T(8,128)}) custom-call(f32[1,1]{1,0:T(1,128)S(6)} %copy.19.reward_ref, bf16[256,640]{1,0:T(8,128)(2,1)S(1)} %bitcast.23, bf16[128,2048]{1,0:T(8,128)(2,1)} %bitcast.32, bf16[128,256]{1,0:T(8,128)(2,1)} %bitcast.26, ...), custom_call_target="tpu_custom_call" | custom-call | flops 10000000 | bytes 4000000 | tf_op jit(solution)/shard_map/finish/pallas_call | solution.py:408
  67.1 1.6 %all-to-all-done.2 = f32[16,2,128]{2,1,0:T(2,128)S(1)} async-done(((f32[16,2,128]{2,1,0:T(2,128)}), f32[16,2,128]{2,1,0:T(2,128)S(1)}, u32[]{:S(2)}, u32[]{:S(2)}) %all-to-all-start.2) | async-done | bytes 16416 | tf_op jit(solution)/shard_map/all_to_all | solution.py:407
  68.7 0.5 slice_bitcast_fusion
  (2 shorter events, 0.0 us)
Async XLA Ops:
  2.1 29.1 %copy-start.1 = (bf16[1,1,128,2048]{3,2,1,0:T(8,128)(2,1)S(1)}, bf16[1,1,128,2048]{3,2,1,0:T(8,128)(2,1)}, u32[]{:S(2)}) copy-start(bf16[1,1,128,2048]{3,2,1,0:T(8,128)(2,1)} %param.19) | copy-start | bytes 1572868
  2.1 29.1 %all-to-all-start = ((bf16[32,8,512]{2,1,0:T(8,128)(2,1)}), bf16[32,8,512]{2,1,0:T(8,128)(2,1)S(1)}, u32[]{:S(2)}, u32[]{:S(2)}) async-start(bf16[32,8,512]{2,1,0:T(8,128)(2,1)} %bitcast.2), calls=%async_computation | async-start | bytes 524288 | tf_op jit(solution)/shard_map/all_to_all | solution.py:351
  20.7 10.5 %copy-start = (bf16[1,1,128,256]{3,2,1,0:T(8,128)(2,1)S(1)}, bf16[1,1,128,256]{3,2,1,0:T(8,128)(2,1)}, u32[]{:S(2)}) copy-start(bf16[1,1,128,256]{3,2,1,0:T(8,128)(2,1)} %param.13) | copy-start | bytes 196612
  20.7 10.5 %copy-start.5 = (bf16[1,1,128,256]{3,2,1,0:T(8,128)(2,1)S(1)}, bf16[1,1,128,256]{3,2,1,0:T(8,128)(2,1)}, u32[]{:S(2)}) copy-start(bf16[1,1,128,256]{3,2,1,0:T(8,128)(2,1)} %param.14) | copy-start | bytes 196612
  35.2 19.7 %copy-start.2 = (f32[128,512]{1,0:T(8,128)}, f32[128,512]{1,0:T(8,128)S(1)}, u32[]{:S(2)}) copy-start(f32[128,512]{1,0:T(8,128)S(1)} %get-tuple-element.27.last_ref) | copy-start | bytes 786436
  35.2 19.7 %copy-start.3 = (f32[128,256]{1,0:T(8,128)}, f32[128,256]{1,0:T(8,128)S(1)}, u32[]{:S(2)}) copy-start(f32[128,256]{1,0:T(8,128)S(1)} %get-tuple-element.28.key_ref) | copy-start | bytes 393220
  35.2 19.7 %copy-start.4 = (f32[128,256]{1,0:T(8,128)}, f32[128,256]{1,0:T(8,128)S(1)}, u32[]{:S(2)}) copy-start(f32[128,256]{1,0:T(8,128)S(1)} %get-tuple-element.29.value_ref) | copy-start | bytes 393220
  55.6 13.1 %all-to-all-start.2 = ((f32[16,2,128]{2,1,0:T(2,128)}), f32[16,2,128]{2,1,0:T(2,128)S(1)}, u32[]{:S(2)}, u32[]{:S(2)}) async-start(f32[16,2,128]{2,1,0:T(2,128)} %bitcast.17), calls=%async_computation.2 | async-start | bytes 32768 | tf_op jit(solution)/shard_map/all_to_all | solution.py:407

commit v8 on v7

--- a/solution.py
+++ b/solution.py
@@ -220,18 +220,20 @@
             query_grads.append(
                 lax.dot_general(dscore, keys[c], CONTRACT_FIRST, preferred_element_type=F32)
             )
+        terms = []
         for c, (first, query_grad) in enumerate(zip(firsts, query_grads)):
             for i, cols in enumerate(head_slices(first, width)):
                 normed_grad = rope_back(
                     query_grad[i * length : (i + 1) * length], back_cos, back_sin
                 )
                 query_out[:, cols] = normed_grad
-                query_terms[...] += fold(normed_grad * unit_ref[:, cols].astype(F32))
+                terms.append(fold(normed_grad * unit_ref[:, cols].astype(F32)))
 
             @pl.when(p < steps - 1)
             def _(c=c):
                 query_copy(c, p).start()
 
+        query_terms[...] += sum(terms)
         return 0
 
     lax.fori_loop(0, steps, some_heads, 0, unroll=UNROLL)

time: 69.6 us -> 69.6 us (level)
  no operation moved by 1% of the time
where the time goes in v8:
time: 69.6 us; the launch traced here: 69.3 us
  starting transfers between devices  23.9 us (34%)
  blocking collectives  19.7 us (28%)
  Pallas kernels  13.1 us (19%)
  waiting for transfers between devices  9.25 us (13%)
  between operations  2.65 us (4%)
    all_to_all x1, blocking collectives, local(): lax.all_to_all(blocks.reshape(responses, own, slot_cols), 'resp', 0, 0)  19.7 us
    all_to_all x1, starting transfers between devices, local(): lax.all_to_all(slots.reshape(responses, own, 2 * kv_cols), 'resp', 0, 0)  16.6 us
    all_to_all x1, waiting for transfers between devices, local(): lax.all_to_all(slots.reshape(responses, own, 2 * kv_cols), 'resp', 0, 0)  7.62 us
    all_to_all x1, starting transfers between devices, local(): lax.all_to_all(gain_slots.reshape(others, 2, width), ('dp', 'tensor'), 0, 0)  7.27 us
    pallas_call x1, Pallas kernels, local(): pl.pallas_call(functools.partial(finish, responses=responses), out_shape=...  4.15 us
    pallas_call x1, Pallas kernels, local(): pl.pallas_call(functools.partial(attend, responses=responses), out_shape=...  4 us
    pallas_call x1, Pallas kernels, local(): pl.pallas_call(prepare, out_shape=(pltpu.VMEM((query_heads * length, widt...  2.89 us
    all_to_all x1, waiting for transfers between devices, local(): lax.all_to_all(gain_slots.reshape(others, 2, width), ('dp', 'tensor'), 0, 0)  1.63 us
  transfers between devices with their start and end apart: 2, of which 2 were waited for; matrix products, arithmetic and copies ran while one was open for 0% of the time, Pallas kernels for 10%

profile of v8, /device:TPU:1, one launch (start us, length us, event | category | flops | bytes accessed | tf_op | source)
XLA Modules:
  0.0 69.3 jit_solution(10676278710496476456)
XLA Ops:
  0.6 1.4 %send_prompt.1 = bf16[256,512]{1,0:T(8,128)(2,1)} custom-call(bf16[8,256]{1,0:T(8,128)(2,1)} %bitcast.33, bf16[8,256]{1,0:T(8,128)(2,1)} %bitcast.34), custom_call_target="tpu_custom_call" | custom-call | tf_op jit(solution)/shard_map/send_prompt/pallas_call | solution.py:346
  2.1 0.0 copy-start.1
  2.1 16.6 %all-to-all-start = ((bf16[32,8,512]{2,1,0:T(8,128)(2,1)}), bf16[32,8,512]{2,1,0:T(8,128)(2,1)S(1)}, u32[]{:S(2)}, u32[]{:S(2)}) async-start(bf16[32,8,512]{2,1,0:T(8,128)(2,1)} %bitcast.2), calls=%async_computation | async-start | bytes 524288 | tf_op jit(solution)/shard_map/all_to_all | solution.py:353
  20.7 0.0 copy-start
  20.7 0.0 copy-start.5
  20.7 2.9 %prepare.1 = (bf16[2048,128]{1,0:T(8,128)(2,1)S(1)}, bf16[256,128]{1,0:T(8,128)(2,1)S(1)}, bf16[128,2048]{1,0:T(8,128)(2,1)S(1)}, f32[88,128]{1,0:T(8,128)S(1)}) custom-call(s32[1]{0:T(128)S(6)} %copy.21.prompt_len_ref, bf16[128,2048]{1,0:T(8,128)(2,1)} %bitcast.31, bf16[128,256]{1,0:T(8,128)(2,1)} %bitcast.25, f32[1,128]{1,0:T(1,128)} %bitcast.35, ...), custom_call_target="tpu_custom_call" | custom-call | flops 100000000 | bytes 4000000 | tf_op jit(solution)/shard_map/prepare/pallas_call | solution.py:354
  23.6 7.6 %all-to-all-done = bf16[32,8,512]{2,1,0:T(8,128)(2,1)S(1)} async-done(((bf16[32,8,512]{2,1,0:T(8,128)(2,1)}), bf16[32,8,512]{2,1,0:T(8,128)(2,1)S(1)}, u32[]{:S(2)}, u32[]{:S(2)}) %all-to-all-start) | async-done | bytes 262176 | tf_op jit(solution)/shard_map/all_to_all | solution.py:353
  31.2 0.0 copy-done.1
  31.2 0.0 copy-done
  31.2 0.0 copy-done.5
  31.2 4.0 %attend.1 = (f32[128,1536]{1,0:T(8,128)}, f32[128,512]{1,0:T(8,128)S(1)}, f32[128,256]{1,0:T(8,128)S(1)}, f32[128,256]{1,0:T(8,128)S(1)}, bf16[256,640]{1,0:T(8,128)(2,1)S(1)}) custom-call(f32[1,1]{1,0:T(1,128)S(6)} %copy.19.reward_ref, s32[1,1]{1,0:T(1,128)S(6)} %copy.20.resp_len_ref, s32[1]{0:T(128)S(6)} %copy.21.prompt_len_ref, ...), custom_call_target="tpu_custom_call" | custom-call | tf_op jit(solution)/shard_map/attend/pallas_call | solution.py:370
  35.2 0.0 copy-start.2
  35.2 0.0 copy-start.3
  35.2 0.0 copy-start.4
  35.2 19.7 %all_to_all.15 = bf16[32,8,640]{2,1,0:T(8,128)(2,1)S(1)} all-to-all(bf16[32,8,640]{2,1,0:T(8,128)(2,1)S(1)} %bitcast.29), channel_id=1, replica_groups=mesh['dp'=8,'resp'=32,'tensor'=2] {'resp'}, dimensions={0} | all-to-all | bytes 655360 | tf_op jit(solution)/shard_map/all_to_all | solution.py:397
  54.9 0.0 copy-done.2
  54.9 0.0 copy-done.3
  54.9 0.0 copy-done.4
  55.0 0.7 weigh.1
  55.6 7.3 %all-to-all-start.2 = ((f32[16,2,128]{2,1,0:T(2,128)}), f32[16,2,128]{2,1,0:T(2,128)S(1)}, u32[]{:S(2)}, u32[]{:S(2)}) async-start(f32[16,2,128]{2,1,0:T(2,128)} %bitcast.17), calls=%async_computation.2 | async-start | bytes 32768 | tf_op jit(solution)/shard_map/all_to_all | solution.py:409
  62.9 4.2 %finish.1 = (bf16[128,2048]{1,0:T(8,128)(2,1)}, bf16[128,256]{1,0:T(8,128)(2,1)}, bf16[128,256]{1,0:T(8,128)(2,1)}, f32[8,256]{1,0:T(8,128)}, f32[8,256]{1,0:T(8,128)}) custom-call(f32[1,1]{1,0:T(1,128)S(6)} %copy.19.reward_ref, bf16[256,640]{1,0:T(8,128)(2,1)S(1)} %bitcast.23, bf16[128,2048]{1,0:T(8,128)(2,1)} %bitcast.32, bf16[128,256]{1,0:T(8,128)(2,1)} %bitcast.26, ...), custom_call_target="tpu_custom_call" | custom-call | flops 10000000 | bytes 4000000 | tf_op jit(solution)/shard_map/finish/pallas_call | solution.py:410
  67.1 1.6 %all-to-all-done.2 = f32[16,2,128]{2,1,0:T(2,128)S(1)} async-done(((f32[16,2,128]{2,1,0:T(2,128)}), f32[16,2,128]{2,1,0:T(2,128)S(1)}, u32[]{:S(2)}, u32[]{:S(2)}) %all-to-all-start.2) | async-done | bytes 16416 | tf_op jit(solution)/shard_map/all_to_all | solution.py:409
  68.7 0.5 slice_bitcast_fusion
  (2 shorter events, 0.0 us)
Async XLA Ops:
  2.1 29.1 %copy-start.1 = (bf16[1,1,128,2048]{3,2,1,0:T(8,128)(2,1)S(1)}, bf16[1,1,128,2048]{3,2,1,0:T(8,128)(2,1)}, u32[]{:S(2)}) copy-start(bf16[1,1,128,2048]{3,2,1,0:T(8,128)(2,1)} %param.19) | copy-start | bytes 1572868
  2.1 29.1 %all-to-all-start = ((bf16[32,8,512]{2,1,0:T(8,128)(2,1)}), bf16[32,8,512]{2,1,0:T(8,128)(2,1)S(1)}, u32[]{:S(2)}, u32[]{:S(2)}) async-start(bf16[32,8,512]{2,1,0:T(8,128)(2,1)} %bitcast.2), calls=%async_computation | async-start | bytes 524288 | tf_op jit(solution)/shard_map/all_to_all | solution.py:353
  20.7 10.5 %copy-start = (bf16[1,1,128,256]{3,2,1,0:T(8,128)(2,1)S(1)}, bf16[1,1,128,256]{3,2,1,0:T(8,128)(2,1)}, u32[]{:S(2)}) copy-start(bf16[1,1,128,256]{3,2,1,0:T(8,128)(2,1)} %param.13) | copy-start | bytes 196612
  20.7 10.5 %copy-start.5 = (bf16[1,1,128,256]{3,2,1,0:T(8,128)(2,1)S(1)}, bf16[1,1,128,256]{3,2,1,0:T(8,128)(2,1)}, u32[]{:S(2)}) copy-start(bf16[1,1,128,256]{3,2,1,0:T(8,128)(2,1)} %param.14) | copy-start | bytes 196612
  35.2 19.7 %copy-start.2 = (f32[128,512]{1,0:T(8,128)}, f32[128,512]{1,0:T(8,128)S(1)}, u32[]{:S(2)}) copy-start(f32[128,512]{1,0:T(8,128)S(1)} %get-tuple-element.27.last_ref) | copy-start | bytes 786436
  35.2 19.7 %copy-start.3 = (f32[128,256]{1,0:T(8,128)}, f32[128,256]{1,0:T(8,128)S(1)}, u32[]{:S(2)}) copy-start(f32[128,256]{1,0:T(8,128)S(1)} %get-tuple-element.28.key_ref) | copy-start | bytes 393220
  35.2 19.7 %copy-start.4 = (f32[128,256]{1,0:T(8,128)}, f32[128,256]{1,0:T(8,128)S(1)}, u32[]{:S(2)}) copy-start(f32[128,256]{1,0:T(8,128)S(1)} %get-tuple-element.29.value_ref) | copy-start | bytes 393220
  55.6 13.1 %all-to-all-start.2 = ((f32[16,2,128]{2,1,0:T(2,128)}), f32[16,2,128]{2,1,0:T(2,128)S(1)}, u32[]{:S(2)}, u32[]{:S(2)}) async-start(f32[16,2,128]{2,1,0:T(2,128)} %bitcast.17), calls=%async_computation.2 | async-start | bytes 32768 | tf_op jit(solution)/shard_map/all_to_all | solution.py:409
